TPU v7x, 256 devices: a whole 4x4x8 slice. The times are simulated.
256 devices in a mesh: fsdp: 32 (over x_hi, z, core), tp: 8 (over x_lo, y).
Axes of the slice: x: 4 (x_hi: 2, x_lo: 2; x = x_hi * 2 + x_lo), y: 4, z: 8, core: 2. Of those that a mesh axis runs over, the one named last changes fastest.
Arguments:
- q_weight: bfloat16 [8192, 8192], P(('tp', 'fsdp')), may hold values from -6 to 6
- k_weight: bfloat16 [8192, 1024], P(('tp', 'fsdp')), may hold values from -6 to 6
- v_weight: bfloat16 [8192, 1024], P(('tp', 'fsdp')), may hold values from -6 to 6
- gate_weight: bfloat16 [8192, 28672], P(('tp', 'fsdp')), may hold values from -6 to 6
- up_weight: bfloat16 [8192, 28672], P(('tp', 'fsdp')), may hold values from -6 to 6
- down_weight: bfloat16 [28672, 8192], P(('tp', 'fsdp')), may hold values from -6 to 6
- attn_gain: float32 [8192], P(('tp', 'fsdp')), may hold values from 0.5 to 2
- ffn_gain: float32 [8192], P(('tp', 'fsdp')), may hold values from 0.5 to 2
- head_order: int32 [8, 8], replicated, may hold values from 0 to 7, each once within a row
- ffn_order: int32 [8, 28], replicated, may hold values from 0 to 27, each once within a row
Outputs:
- merged_qkv: bfloat16 [8192, 10240], P('fsdp', 'tp')
- merged_gate_up: bfloat16 [8192, 57344], P('fsdp', 'tp')
- merged_down: bfloat16 [28672, 8192], P('tp', 'fsdp')
Inputs may be any that keep to these rules, and one draw needn't show every extreme that they name: `head_order`: each row is a permutation of 0 to 7. `ffn_order`: each row is a permutation of 0 to 27.
All inputs are finite; a program needn't handle non-finite values.
Results may differ from a plain program's by a relative error of at most 0.0058.
Values may be sent and summed in bfloat16 or wider, within the bound.
No kernel may reach another device: no remote copies, remote signals or barrier semaphores. Data moves between devices by JAX's collectives and lax.ppermute only.
A program may use at most 128 MiB of HBM per device.

v0:
```python
import math

import jax
import jax.numpy as jnp
from jax import lax
from jax.sharding import PartitionSpec as P

KV = 8
HD = 128
HA = 64
FB = 128
HB = 128
QPG = 8


def sylvester(order_size):
    counter = jnp.arange(order_size, dtype=jnp.int32)
    parity = jnp.zeros((order_size, order_size), jnp.int32)
    for bit_level in range(order_size.bit_length() - 1):
        digits = counter // 2**bit_level % 2
        parity = parity + digits[:, None] * digits[None, :]
    return (1 - 2 * (parity % 2)).astype(jnp.bfloat16)


def owner_major(blocks, owners, gain):
    row_count = blocks[0].shape[0]
    pieces = [block.T.reshape(owners, -1, row_count) for block in blocks]
    joined = jnp.concatenate(pieces, axis=1)
    return (joined.astype(jnp.float32) * gain[None, None, :]).astype(jnp.bfloat16)


def spread_owners(joined, owners, shards):
    row_count = joined.shape[-1]
    return joined.reshape(owners, shards, -1, row_count).swapaxes(0, 1).reshape(-1, row_count)


def first_rows(matrix, large_sign):
    count = matrix.shape[0]
    shaped = matrix.reshape(count, -1, large_sign.shape[0])
    sectioned = jnp.einsum("rab,bc->rac", shaped, large_sign, preferred_element_type=jnp.float32)
    return (
        (sectioned * (1.0 / math.sqrt(large_sign.shape[0])))
        .reshape(matrix.shape)
        .astype(jnp.bfloat16)
    )


def second_rows(matrix, small_sign):
    count = matrix.shape[0]
    shaped = matrix.reshape(count, small_sign.shape[0], -1)
    mixed = jnp.einsum("rac,ae->rec", shaped, small_sign, preferred_element_type=jnp.float32)
    return (
        (mixed * (1.0 / math.sqrt(small_sign.shape[0]))).reshape(matrix.shape).astype(jnp.bfloat16)
    )


def rotate_columns(matrix, small_sign, large_sign):
    return second_rows(first_rows(matrix, large_sign), small_sign)


def order_blocks(landed, block_ids, width):
    count, local_rows = landed.shape
    blocked = landed.reshape(count // width, width, local_rows)
    return jnp.take(blocked, block_ids, axis=0).reshape(count, local_rows).T


def per_device(
    q_weight,
    k_weight,
    v_weight,
    gate_weight,
    up_weight,
    down_weight,
    attn_gain,
    ffn_gain,
    head_order,
    ffn_order,
):
    owners = lax.axis_size("tp")
    shards = lax.axis_size("fsdp")
    small_sign = sylvester(HA)
    large_sign = sylvester(HB)
    attn_piece = spread_owners(
        owner_major((q_weight, k_weight, v_weight), owners, attn_gain), owners, shards
    )
    ffn_piece = spread_owners(
        owner_major((gate_weight, up_weight), owners, ffn_gain), owners, shards
    )
    down_rotated = rotate_columns(down_weight, small_sign, large_sign)
    row_groups = (
        lax.all_to_all(attn_piece, "fsdp", split_axis=0, concat_axis=1, tiled=True),
        lax.all_to_all(ffn_piece, "fsdp", split_axis=0, concat_axis=1, tiled=True),
    )
    gathered = (
        lax.all_to_all(row_groups[0], "tp", split_axis=0, concat_axis=1, tiled=True),
        lax.all_to_all(row_groups[1], "tp", split_axis=0, concat_axis=1, tiled=True),
    )
    rotated = (
        rotate_columns(gathered[0], small_sign, large_sign),
        rotate_columns(gathered[1], small_sign, large_sign),
    )
    landed_attn, landed_ffn = (
        lax.all_to_all(rotated[0], "fsdp", split_axis=1, concat_axis=0, tiled=True),
        lax.all_to_all(rotated[1], "fsdp", split_axis=1, concat_axis=0, tiled=True),
    )
    owner_index = lax.axis_index("tp")
    group_per = KV // owners
    head_rows = lax.dynamic_slice_in_dim(head_order, owner_index * group_per, group_per, 0)
    query_blocks = (jnp.arange(group_per, dtype=jnp.int32)[:, None] * QPG + head_rows).reshape(-1)
    kv_blocks = group_per * QPG + jnp.arange(2 * group_per, dtype=jnp.int32)
    attn_blocks = jnp.concatenate([query_blocks, kv_blocks])
    merged_attn = order_blocks(landed_attn, attn_blocks, HD)
    owner_order = lax.dynamic_index_in_dim(ffn_order, owner_index, 0, keepdims=False)
    group_count = owner_order.shape[0]
    ffn_blocks = jnp.concatenate([owner_order, group_count + owner_order])
    merged_ffn = order_blocks(landed_ffn, ffn_blocks, FB)
    moved = lax.all_to_all(down_rotated, "fsdp", split_axis=1, concat_axis=0, tiled=True)
    down_blocks = moved.reshape(group_count, FB, moved.shape[1])
    merged_down = jnp.take(down_blocks, owner_order, axis=0).reshape(moved.shape)
    return (merged_attn, merged_ffn, merged_down)


def solution(mesh):
    placed = (
        P(("tp", "fsdp"), None),
        P(("tp", "fsdp"), None),
        P(("tp", "fsdp"), None),
        P(("tp", "fsdp"), None),
        P(("tp", "fsdp"), None),
        P(("tp", "fsdp"), None),
        P(("tp", "fsdp")),
        P(("tp", "fsdp")),
        P(),
        P(),
    )
    return jax.shard_map(
        per_device,
        mesh=mesh,
        in_specs=placed,
        out_specs=(P("fsdp", "tp"), P("fsdp", "tp"), P("tp", "fsdp")),
        check_vma=False,
    )
```

profile of v0, /device:TPU:25, one launch (start us, length us, event | category | flops | bytes accessed | tf_op | source)
XLA Modules:
  0.0 414.2 jit_solution(4867402287630572259)
XLA Ops:
  0.6 0.0 copy-start
  0.6 1.1 copy.61
  1.8 0.9 copy_bitcast_fusion.3
  2.6 0.0 copy-start.3
  2.7 0.1 maximum_convert_fusion.1
  2.8 4.8 %reshape.852 = f32[8,32,40,32]{2,1,3,0:T(8,128)} reshape(f32[8,1280,32]{1,2,0:T(8,128)S(1)} %maximum_convert_fusion.1) | data formatting | bytes 2621440 | tf_op jit(solution)/shard_map/convert_element_type | solution.py:29
  7.5 2.8 fusion.6
  10.3 1.4 copy.37
  11.7 2.2 all_to_all.78
  13.9 11.8 %all-to-all-start = ((bf16[32,320,32]{1,2,0:T(8,128)(2,1)}), bf16[32,320,32]{1,2,0:T(8,128)(2,1)S(1)}, u32[]{:S(2)}, u32[]{:S(2)}) async-start(bf16[32,320,32]{1,2,0:T(8,128)(2,1)} %all_to_all.78), calls=%async_computation | async-start | bytes 1572864 | tf_op jit(solution)/shard_map/all_to_all | solution.py:91
  25.6 4.3 %copy_bitcast_fusion = (bf16[8,3584,32]{1,2,0:T(8,128)(2,1)}, bf16[8,3584,32]{1,2,0:T(8,128)(2,1)}) fusion(bf16[4,8,8,3584]{3,2,1,0:T(8,128)(2,1)} %bitcast.128, bf16[4,8,8,3584]{3,2,1,0:T(8,128)(2,1)} %bitcast.129), kind=kLoop, calls=%fused_computation.17 | loop fusion | bytes 7340032 | tf_op jit(solution)/shard_map/reshape | solution.py:27
  29.9 18.5 %all-to-all-done = bf16[32,320,32]{1,2,0:T(8,128)(2,1)S(1)} async-done(((bf16[32,320,32]{1,2,0:T(8,128)(2,1)}), bf16[32,320,32]{1,2,0:T(8,128)(2,1)S(1)}, u32[]{:S(2)}, u32[]{:S(2)}) %all-to-all-start) | async-done | bytes 655392 | tf_op jit(solution)/shard_map/all_to_all | solution.py:91
  48.4 1.8 all_to_all.81
  50.1 2.2 copy.38
  52.3 4.2 %all-to-all-start.1 = ((bf16[8,40,1024]{2,1,0:T(8,128)(2,1)}), bf16[8,40,1024]{2,1,0:T(8,128)(2,1)S(1)}, u32[]{:S(2)}, u32[]{:S(2)}) async-start(bf16[8,40,1024]{2,1,0:T(8,128)(2,1)} %copy.38), calls=%async_computation.1 | async-start | bytes 1310720 | tf_op jit(solution)/shard_map/all_to_all | solution.py:95
  56.4 5.9 %maximum_convert_fusion = f32[8,7168,32]{1,2,0:T(8,128)} fusion(bf16[8,3584,32]{1,2,0:T(8,128)(2,1)} %get-tuple-element.34, bf16[8,3584,32]{1,2,0:T(8,128)(2,1)} %get-tuple-element.35), kind=kLoop, calls=%fused_computation.10 | loop fusion | flops 7340032 | bytes 11010048 | tf_op jit(solution)/shard_map/convert_element_type | solution.py:29
  62.3 9.8 %reshape.853 = f32[8,32,224,32]{2,1,3,0:T(8,128)} reshape(f32[8,7168,32]{1,2,0:T(8,128)} %maximum_convert_fusion) | data formatting | bytes 14680064 | tf_op jit(solution)/shard_map/convert_element_type | solution.py:29
  72.2 4.7 %fusion = bf16[32,8,224,32]{2,0,3,1:T(8,128)(2,1)S(1)} fusion(f32[8,32,224,32]{2,1,3,0:T(8,128)} %reshape.853, f32[32]{0:T(128)S(1)} %copy-done.4), kind=kLoop, calls=%fused_computation.6 | loop fusion | flops 3670016 | bytes 11010176 | tf_op jit(solution)/shard_map/transpose | solution.py:34
  76.9 4.4 %copy.43 = bf16[32,8,224,32]{2,1,3,0:T(8,128)(2,1)} copy(bf16[32,8,224,32]{2,0,3,1:T(8,128)(2,1)S(1)} %fusion) | data formatting | bytes 7340032 | tf_op jit(solution)/shard_map/transpose | solution.py:34
  81.3 8.4 %all_to_all.86 = bf16[32,1792,32]{1,2,0:T(8,128)(2,1)} reshape(bf16[32,8,224,32]{2,1,3,0:T(8,128)(2,1)} %copy.43) | data formatting | bytes 7340032 | tf_op jit(solution)/shard_map/all_to_all | solution.py:92
  89.7 7.3 %all-to-all-start.3 = ((bf16[32,1792,32]{1,2,0:T(8,128)(2,1)}), bf16[32,1792,32]{1,2,0:T(8,128)(2,1)}, u32[]{:S(2)}, u32[]{:S(2)}) async-start(bf16[32,1792,32]{1,2,0:T(8,128)(2,1)} %all_to_all.86), calls=%async_computation.3 | async-start | bytes 7340032 | tf_op jit(solution)/shard_map/all_to_all | solution.py:92
  97.1 0.4 copy.39
  97.5 0.3 reshape.844
  97.8 0.8 fusion.13
  98.6 0.2 convert_element_type.89
  98.8 1.2 copy.40
  100.0 82.1 %all-to-all-done.3 = bf16[32,1792,32]{1,2,0:T(8,128)(2,1)} async-done(((bf16[32,1792,32]{1,2,0:T(8,128)(2,1)}), bf16[32,1792,32]{1,2,0:T(8,128)(2,1)}, u32[]{:S(2)}, u32[]{:S(2)}) %all-to-all-start.3) | async-done | bytes 3670048 | tf_op jit(solution)/shard_map/all_to_all | solution.py:92
  182.1 7.1 %all-to-all-start.2 = ((bf16[40,32,256]{2,0,1:T(8,128)(2,1)}), bf16[40,32,256]{2,0,1:T(8,128)(2,1)S(1)}, u32[]{:S(2)}, u32[]{:S(2)}) async-start(bf16[40,32,256]{2,0,1:T(8,128)(2,1)} %copy.40), calls=%async_computation.2 | async-start | bytes 1310720 | tf_op jit(solution)/shard_map/all_to_all | solution.py:103
  189.2 9.3 %all_to_all.89 = bf16[8,224,1024]{1,0,2:T(8,128)(2,1)} reshape(bf16[1792,32,32]{0,2,1:T(8,128)(2,1)} %bitcast.23) | data formatting | bytes 7340032 | tf_op jit(solution)/shard_map/all_to_all | solution.py:96
  198.5 6.5 %copy.44 = bf16[8,224,1024]{2,1,0:T(8,128)(2,1)} copy(bf16[8,224,1024]{1,0,2:T(8,128)(2,1)} %all_to_all.89) | data formatting | bytes 7340032 | tf_op jit(solution)/shard_map/all_to_all | solution.py:96
  204.9 4.7 %all-to-all-done.2 = bf16[40,32,256]{2,0,1:T(8,128)(2,1)S(1)} async-done(((bf16[40,32,256]{2,0,1:T(8,128)(2,1)}), bf16[40,32,256]{2,0,1:T(8,128)(2,1)S(1)}, u32[]{:S(2)}, u32[]{:S(2)}) %all-to-all-start.2) | async-done | bytes 655392 | tf_op jit(solution)/shard_map/all_to_all | solution.py:103
  209.7 5.1 %all-to-all-start.4 = ((bf16[8,224,1024]{2,1,0:T(8,128)(2,1)}), bf16[8,224,1024]{2,1,0:T(8,128)(2,1)}, u32[]{:S(2)}, u32[]{:S(2)}) async-start(bf16[8,224,1024]{2,1,0:T(8,128)(2,1)} %copy.44), calls=%async_computation.4 | async-start | bytes 7340032 | tf_op jit(solution)/shard_map/all_to_all | solution.py:96
  214.8 1.7 copy.55
  216.6 4.2 %fusion.8 = bf16[112,64,128]{2,1,0:T(8,128)(2,1)} fusion(bf16[112,64,128]{2,1,0:T(8,128)(2,1)} %bitcast.131, s32[64]{0:T(128)S(1)} %get-tuple-element.28, s32[64]{0:T(128)S(1)} %get-tuple-element.29, s32[64]{0:T(128)S(1)} %get-tuple-element.30, s32[64]{0:T(128)S(1)} %get-tuple-element.31, s32[64]{0:T(128)S(1)} %get-tuple-element.32, ...), kind=kOutput, calls=%fused_computation.21 | convolution fusion | flops 356536320 | bytes 3675136 | tf_op jit(solution)/shard_map/rac,ae->rec/dot_general | solution.py:51
  220.7 2.6 convert_element_type.101
  223.3 2.3 copy.48
  225.6 30.2 %all-to-all-done.4 = bf16[8,224,1024]{2,1,0:T(8,128)(2,1)} async-done(((bf16[8,224,1024]{2,1,0:T(8,128)(2,1)}), bf16[8,224,1024]{2,1,0:T(8,128)(2,1)}, u32[]{:S(2)}, u32[]{:S(2)}) %all-to-all-start.4) | async-done | bytes 3670048 | tf_op jit(solution)/shard_map/all_to_all | solution.py:96
  255.8 7.4 %all-to-all-start.6 = ((bf16[112,32,256]{2,0,1:T(8,128)(2,1)}), bf16[112,32,256]{2,0,1:T(8,128)(2,1)S(1)}, u32[]{:S(2)}, u32[]{:S(2)}) async-start(bf16[112,32,256]{2,0,1:T(8,128)(2,1)} %copy.48), calls=%async_computation.6 | async-start | bytes 3670016 | tf_op jit(solution)/shard_map/all_to_all | solution.py:117
  263.2 5.9 %copy.45 = bf16[224,8,1024]{2,1,0:T(8,128)(2,1)} copy(bf16[224,8,1024]{2,0,1:T(8,128)(2,1)} %bitcast.24) | data formatting | bytes 7340032 | tf_op jit(solution)/shard_map/all_to_all | solution.py:96
  269.1 6.7 %reshape.848 = bf16[224,64,128]{2,1,0:T(8,128)(2,1)} reshape(bf16[224,8,1024]{2,1,0:T(8,128)(2,1)} %copy.45) | data formatting | bytes 7340032 | tf_op jit(solution)/shard_map/reshape | solution.py:39
  275.8 6.2 %fusion.2 = bf16[224,64,128]{2,1,0:T(8,128)(2,1)} fusion(bf16[224,64,128]{2,1,0:T(8,128)(2,1)} %reshape.848, s32[64]{0:T(128)S(1)} %get-tuple-element.28, s32[64]{0:T(128)S(1)} %get-tuple-element.29, s32[64]{0:T(128)S(1)} %get-tuple-element.30, s32[64]{0:T(128)S(1)} %get-tuple-element.31, s32[64]{0:T(128)S(1)} %get-tuple-element.32, ...), kind=kOutput, calls=%fused_computation.9 | convolution fusion | flops 712527872 | bytes 7345152 | tf_op jit(solution)/shard_map/rac,ae->rec/dot_general | solution.py:51
  282.0 6.5 %convert_element_type.96 = bf16[224,32,256]{2,1,0:T(8,128)(2,1)} reshape(bf16[224,64,128]{2,1,0:T(8,128)(2,1)} %fusion.2) | data formatting | bytes 7340032 | tf_op jit(solution)/shard_map/convert_element_type | solution.py:53
  288.5 5.9 %copy.46 = bf16[224,32,256]{2,0,1:T(8,128)(2,1)} copy(bf16[224,32,256]{2,1,0:T(8,128)(2,1)} %convert_element_type.96) | data formatting | bytes 7340032 | tf_op jit(solution)/shard_map/convert_element_type | solution.py:53
  294.4 14.0 %all-to-all-done.6 = bf16[112,32,256]{2,0,1:T(8,128)(2,1)S(1)} async-done(((bf16[112,32,256]{2,0,1:T(8,128)(2,1)}), bf16[112,32,256]{2,0,1:T(8,128)(2,1)S(1)}, u32[]{:S(2)}, u32[]{:S(2)}) %all-to-all-start.6) | async-done | bytes 1835040 | tf_op jit(solution)/shard_map/all_to_all | solution.py:117
  308.5 5.8 %all-to-all-start.5 = ((bf16[224,32,256]{2,0,1:T(8,128)(2,1)}), bf16[224,32,256]{2,0,1:T(8,128)(2,1)}, u32[]{:S(2)}, u32[]{:S(2)}) async-start(bf16[224,32,256]{2,0,1:T(8,128)(2,1)} %copy.46), calls=%async_computation.5 | async-start | bytes 7340032 | tf_op jit(solution)/shard_map/all_to_all | solution.py:104
  314.3 0.7 fusion.41
  315.0 0.7 compare_and_fusion
  315.7 0.1 compare_and_fusion.1
  315.8 0.7 fusion.46
  316.4 0.1 fusion.40
  316.5 0.1 fusion.39
  316.6 0.1 compare_and_fusion.2
  316.7 0.1 broadcast_bitcast_fusion.2
  316.8 0.1 broadcast_bitcast_fusion.1
  316.9 0.1 broadcast_bitcast_fusion
  316.9 0.6 gather_fusion
  317.5 0.2 bitcast_select_fusion.1
  317.8 1.1 copy.49
  318.9 2.0 gather_fusion.2
  320.8 3.9 bitcast_select_fusion
  324.7 74.6 %all-to-all-done.5 = bf16[224,32,256]{2,0,1:T(8,128)(2,1)} async-done(((bf16[224,32,256]{2,0,1:T(8,128)(2,1)}), bf16[224,32,256]{2,0,1:T(8,128)(2,1)}, u32[]{:S(2)}, u32[]{:S(2)}) %all-to-all-start.5) | async-done | bytes 3670048 | tf_op jit(solution)/shard_map/all_to_all | solution.py:104
  399.3 4.7 %gather_fusion.1 = bf16[56,128,256]{2,1,0:T(8,128)(2,1)} fusion(bf16[56,128,256]{2,1,0:T(8,128)(2,1)} %bitcast.27, s32[1024]{0:T(1024)S(1)} %pad_clamp_fusion.1), kind=kCustom, calls=%fused_computation.1 | custom fusion | bytes 7340256 | tf_op jit(solution)/shard_map/jit(_take)/gather | solution.py:64
  404.0 6.0 %copy.47 = bf16[7168,256]{0,1:T(8,128)(2,1)} copy(bf16[7168,256]{1,0:T(8,128)(2,1)} %bitcast.121) | data formatting | bytes 7340032 | tf_op jit(solution)/shard_map/jit(_take)/gather | solution.py:64
  410.0 4.2 %select_bitcast_fusion = bf16[256,7168]{1,0:T(8,128)(2,1)} fusion(bf16[7168,256]{0,1:T(8,128)(2,1)} %copy.47, pred[7168]{0:T(1024)(128)(4,1)S(1)} %broadcast_bitcast_fusion), kind=kLoop, calls=%fused_computation.13 | loop fusion | flops 1835008 | bytes 7347200 | tf_op jit(solution)/shard_map/transpose | solution.py:64
  (22 shorter events, 0.1 us)
Async XLA Ops:
  0.6 1.1 copy-start
  2.6 4.9 %copy-start.3 = (f32[32]{0:T(128)S(1)}, f32[32]{0:T(128)}, u32[]{:S(2)}) copy-start(f32[32]{0:T(128)} %param.16) | copy-start | bytes 388
  13.9 34.5 %all-to-all-start = ((bf16[32,320,32]{1,2,0:T(8,128)(2,1)}), bf16[32,320,32]{1,2,0:T(8,128)(2,1)S(1)}, u32[]{:S(2)}, u32[]{:S(2)}) async-start(bf16[32,320,32]{1,2,0:T(8,128)(2,1)} %all_to_all.78), calls=%async_computation | async-start | bytes 1572864 | tf_op jit(solution)/shard_map/all_to_all | solution.py:91
  52.3 37.5 %all-to-all-start.1 = ((bf16[8,40,1024]{2,1,0:T(8,128)(2,1)}), bf16[8,40,1024]{2,1,0:T(8,128)(2,1)S(1)}, u32[]{:S(2)}, u32[]{:S(2)}) async-start(bf16[8,40,1024]{2,1,0:T(8,128)(2,1)} %copy.38), calls=%async_computation.1 | async-start | bytes 1310720 | tf_op jit(solution)/shard_map/all_to_all | solution.py:95
  62.3 9.8 %copy-start.4 = (f32[32]{0:T(128)S(1)}, f32[32]{0:T(128)}, u32[]{:S(2)}) copy-start(f32[32]{0:T(128)} %param.17) | copy-start | bytes 388
  89.7 92.4 %all-to-all-start.3 = ((bf16[32,1792,32]{1,2,0:T(8,128)(2,1)}), bf16[32,1792,32]{1,2,0:T(8,128)(2,1)}, u32[]{:S(2)}, u32[]{:S(2)}) async-start(bf16[32,1792,32]{1,2,0:T(8,128)(2,1)} %all_to_all.86), calls=%async_computation.3 | async-start | bytes 7340032 | tf_op jit(solution)/shard_map/all_to_all | solution.py:92
  182.1 27.6 %all-to-all-start.2 = ((bf16[40,32,256]{2,0,1:T(8,128)(2,1)}), bf16[40,32,256]{2,0,1:T(8,128)(2,1)S(1)}, u32[]{:S(2)}, u32[]{:S(2)}) async-start(bf16[40,32,256]{2,0,1:T(8,128)(2,1)} %copy.40), calls=%async_computation.2 | async-start | bytes 1310720 | tf_op jit(solution)/shard_map/all_to_all | solution.py:103
  204.9 9.9 %copy-start.2 = (bf16[112,8192]{1,0:T(8,128)(2,1)S(1)}, bf16[112,8192]{1,0:T(8,128)(2,1)}, u32[]{:S(2)}) copy-start(bf16[112,8192]{1,0:T(8,128)(2,1)} %param.15) | copy-start | bytes 5505028
  209.7 46.1 %all-to-all-start.4 = ((bf16[8,224,1024]{2,1,0:T(8,128)(2,1)}), bf16[8,224,1024]{2,1,0:T(8,128)(2,1)}, u32[]{:S(2)}, u32[]{:S(2)}) async-start(bf16[8,224,1024]{2,1,0:T(8,128)(2,1)} %copy.44), calls=%async_computation.4 | async-start | bytes 7340032 | tf_op jit(solution)/shard_map/all_to_all | solution.py:96
  255.8 52.7 %all-to-all-start.6 = ((bf16[112,32,256]{2,0,1:T(8,128)(2,1)}), bf16[112,32,256]{2,0,1:T(8,128)(2,1)S(1)}, u32[]{:S(2)}, u32[]{:S(2)}) async-start(bf16[112,32,256]{2,0,1:T(8,128)(2,1)} %copy.48), calls=%async_computation.6 | async-start | bytes 3670016 | tf_op jit(solution)/shard_map/all_to_all | solution.py:117
  308.5 90.8 %all-to-all-start.5 = ((bf16[224,32,256]{2,0,1:T(8,128)(2,1)}), bf16[224,32,256]{2,0,1:T(8,128)(2,1)}, u32[]{:S(2)}, u32[]{:S(2)}) async-start(bf16[224,32,256]{2,0,1:T(8,128)(2,1)} %copy.46), calls=%async_computation.5 | async-start | bytes 7340032 | tf_op jit(solution)/shard_map/all_to_all | solution.py:104
  404.0 10.2 %copy-start.1 = (bf16[32,1024]{1,0:T(8,128)(2,1)S(1)}, bf16[32,1024]{1,0:T(8,128)(2,1)}, u32[]{:S(2)}) copy-start(bf16[32,1024]{1,0:T(8,128)(2,1)} %param.11) | copy-start | bytes 196612
where the time goes:
time: 418 us; the launch traced here: 414 us
  waiting for transfers between devices  224 us (54%)
  local copies, waits for them, and re-layouts  106 us (25%)
  starting transfers between devices  48.5 us (12%)
  other arithmetic  23.7 us (6%)
  matrix products  11.2 us (3%)
    all_to_all x1, waiting for transfers between devices, per_device(): lax.all_to_all(ffn_piece, 'fsdp', split_axis=0, concat_axis=1, tiled=True)  82.1 us
    all_to_all x1, waiting for transfers between devices, per_device(): lax.all_to_all(rotated[1], 'fsdp', split_axis=1, concat_axis=0, tiled=True)  74.6 us
    all_to_all x1, waiting for transfers between devices, per_device(): lax.all_to_all(row_groups[1], 'tp', split_axis=0, concat_axis=1, tiled=True)  30.2 us
    all_to_all x3, local copies, waits for them, and re-layouts, per_device(): lax.all_to_all(row_groups[1], 'tp', split_axis=0, concat_axis=1, tiled=True)  21.6 us
    convert_element_type x6, local copies, waits for them, and re-layouts, second_rows(): (mixed * (1.0 / math.sqrt(small_sign.shape[0]))).reshape(matrix.shape)  18.7 us
    all_to_all x1, waiting for transfers between devices, per_device(): lax.all_to_all(attn_piece, 'fsdp', split_axis=0, concat_axis=1, tiled=True)  18.5 us
    convert_element_type x2, local copies, waits for them, and re-layouts, owner_major(): joined.astype(jnp.float32) * gain[None, None, :]  14.6 us
    all_to_all x1, waiting for transfers between devices, per_device(): lax.all_to_all(down_rotated, 'fsdp', split_axis=1, concat_axis=0, tiled=T...  14 us
  transfers between devices with their start and end apart: 7, of which 6 were waited for; matrix products, arithmetic and copies ran while one was open for 22% of the time, Pallas kernels for 0%

commit v1 on v0

v1 whole, which is shorter than its diff:
```python
import functools
import math

import jax
import jax.numpy as jnp
import numpy as np
from jax import lax
from jax.experimental import pallas as pl
from jax.experimental.pallas import tpu as pltpu
from jax.sharding import Mesh
from jax.sharding import PartitionSpec as P

BLK = 128
QPG = 8
FFB = 28
HALF_Q = QPG // 2
HALF_F = FFB // 2
ROWS = 32
PIECES = 16
VMEM_LIMIT = 48 * 1024 * 1024
PLANE = ("xh", "xl", "y")
DEPTH = ("xh", "z")
FSDP = ("xh", "z", "core")
TP = ("xl", "y")


def signs(order):
    index = np.arange(order)
    common = index[:, None] & index[None, :]
    parity = np.zeros((order, order), np.int64)
    while common.any():
        parity ^= common & 1
        common = common >> 1
    return (1 - 2 * parity).astype(np.float32)


def first_matrix():
    high = signs(PIECES)[:, [(s & 7) * 2 + (s >> 3) for s in range(PIECES)]]
    return np.kron(high, signs(ROWS)) / 16.0


def last_matrices():
    table = np.zeros((2, 2, 8, 8), np.float32)
    for core in range(2):
        for side in range(2):
            b5 = core ^ side
            for row in range(8):
                for col in range(8):
                    bits = (core & (col >> 2)) + ((row >> 2) & (col >> 1)) % 2
                    bits += ((row >> 1) & col) % 2 + (row & 1 & b5)
                    table[core, side, row, col] = 1 - 2 * (bits % 2)
    return np.kron(table, np.eye(ROWS, dtype=np.float32).reshape(1, 1, ROWS, ROWS))


def bf16(values):
    return values.astype(jnp.bfloat16)


def params():
    return pltpu.CompilerParams(vmem_limit_bytes=VMEM_LIMIT)


def cost(flops, moved):
    return pl.CostEstimate(flops=int(flops), bytes_accessed=int(moved), transcendentals=0)


def whole(count):
    return [pl.BlockSpec(memory_space=pltpu.VMEM)] * count


def down_kernel(weight_ref, sign_ref, out_ref):
    sign = sign_ref[...]
    groups = weight_ref.shape[1] // BLK

    @pl.loop(0, weight_ref.shape[0] // 16)
    def _(step):
        rows = pl.ds(pl.multiple_of(step * 16, 16), 16)
        tall = jnp.concatenate(
            [weight_ref[rows, a * BLK : (a + 1) * BLK] for a in range(groups)], axis=0
        )
        half = jnp.dot(tall, sign, preferred_element_type=jnp.float32)
        half = bf16(half * (1.0 / math.sqrt(BLK))).astype(jnp.float32)
        parts = [half[a * 16 : (a + 1) * 16] for a in range(groups)]
        span = 1
        while span < groups:
            mixed = list(parts)
            for a in range(groups):
                if not a & span:
                    mixed[a] = parts[a] + parts[a | span]
                    mixed[a | span] = parts[a] - parts[a | span]
            parts = mixed
            span *= 2
        for a in range(groups):
            value = bf16(parts[a] * (1.0 / math.sqrt(groups)))
            out_ref[a // 2, rows, (a % 2) * BLK : (a % 2 + 1) * BLK] = value


def rotate_down(weight, shards):
    rows, width = weight.shape
    return pl.pallas_call(
        down_kernel,
        out_shape=jax.ShapeDtypeStruct((shards, rows, width // shards), jnp.bfloat16),
        in_specs=whole(2),
        out_specs=whole(1)[0],
        compiler_params=params(),
        cost_estimate=cost(2 * rows * width * BLK * 4, 4 * rows * width),
        name="down_rotate",
    )(weight, jnp.asarray(signs(BLK), jnp.bfloat16))


def scaled(ref, block, gain):
    columns = pl.ds(pl.multiple_of(block * BLK, BLK), BLK)
    return bf16(ref[:, columns].astype(jnp.float32) * gain)


def pick_kernel(with_heads, place_ref, heads_ref, order_ref, gain_ref, *refs):
    out_refs = refs[-PIECES:]
    place = place_ref[0]
    ffn_ref = refs[0]
    ffn_gain = gain_ref[0]

    @pl.loop(0, HALF_F)
    def _(slot):
        columns = pl.ds(pl.multiple_of(slot * BLK, BLK), BLK)
        for k in range(PIECES):
            place_to = place ^ k
            owner = place_to & 7
            block = order_ref[owner, (place_to >> 3) * HALF_F + slot]
            out_refs[k][:, columns] = scaled(ffn_ref, owner * FFB + block, ffn_gain)

    if with_heads:
        q_ref, k_ref, v_ref = refs[1:4]
        head_gain = gain_ref[1]
        start = HALF_F * BLK

        @pl.loop(0, HALF_Q)
        def _(slot):
            columns = pl.ds(pl.multiple_of(start + slot * BLK, BLK), BLK)
            for k in range(PIECES):
                place_to = place ^ k
                owner = place_to & 7
                head = heads_ref[owner, (place_to >> 3) * HALF_Q + slot]
                out_refs[k][:, columns] = scaled(q_ref, owner * QPG + head, head_gain)

        for k in range(PIECES):
            place_to = place ^ k
            owner = place_to & 7
            value = jnp.where(
                place_to >= 8, scaled(v_ref, owner, head_gain), scaled(k_ref, owner, head_gain)
            )
            out_refs[k][:, start + HALF_Q * BLK :] = value


def pick(place, head_order, ffn_order, gains, arrays):
    with_heads = len(arrays) > 1
    width = (HALF_F + (HALF_Q + 1) * with_heads) * BLK
    return pl.pallas_call(
        functools.partial(pick_kernel, with_heads),
        out_shape=[jax.ShapeDtypeStruct((ROWS, width), jnp.bfloat16)] * PIECES,
        in_specs=[pl.BlockSpec(memory_space=pltpu.SMEM)] * 3 + whole(1 + len(arrays)),
        out_specs=whole(PIECES),
        compiler_params=params(),
        cost_estimate=cost(PIECES * ROWS * width * 400, 4 * PIECES * ROWS * width),
        name="pick_columns",
    )(place, head_order, ffn_order, gains, *arrays)


def first_kernel(place_ref, matrix_ref, *refs):
    in_refs, (out_ref, mine_ref) = refs[:PIECES], refs[PIECES:]
    place = place_ref[0]
    for group in range(PIECES):
        turned = (group >> 1) | ((group & 1) << 3)
        common = place & turned
        common = common ^ (common >> 2)
        common = (common ^ (common >> 1)) & 1
        sign = bf16((1 - 2 * common).astype(jnp.float32))
        rows = slice(group * ROWS, (group + 1) * ROWS)
        mine_ref[rows, :] = matrix_ref[rows, :] * sign
    width = in_refs[0].shape[1]

    @pl.loop(0, width // BLK)
    def _(step):
        columns = pl.ds(pl.multiple_of(step * BLK, BLK), BLK)
        tall = jnp.concatenate([ref[:, columns] for ref in in_refs], axis=0)
        mixed = jnp.dot(mine_ref[...], tall, preferred_element_type=jnp.float32)
        out_ref[:, :, columns] = bf16(mixed).reshape(PIECES, ROWS, BLK)


def first_mix(place, pieces):
    width = pieces[0].shape[1]
    rows = PIECES * ROWS
    return pl.pallas_call(
        first_kernel,
        out_shape=jax.ShapeDtypeStruct((PIECES, ROWS, width), jnp.bfloat16),
        in_specs=[pl.BlockSpec(memory_space=pltpu.SMEM)] + whole(1 + PIECES),
        out_specs=whole(1)[0],
        scratch_shapes=[pltpu.VMEM((rows, rows), jnp.bfloat16)],
        compiler_params=params(),
        cost_estimate=cost(2 * rows * rows * width, 4 * rows * width),
        name="first_mix",
    )(place, jnp.asarray(first_matrix(), jnp.bfloat16), *pieces)


def last_columns(core_ref, matrix_ref, own_ref, other_ref, part, columns):
    core = core_ref[0]
    own = own_ref[pl.ds(part * 8, 8), :, columns].reshape(8 * ROWS, -1)
    other = other_ref[pl.ds(part * 8, 8), :, columns].reshape(8 * ROWS, -1)
    mixed = jnp.dot(matrix_ref[core, 0], own, preferred_element_type=jnp.float32)
    mixed += jnp.dot(matrix_ref[core, 1], other, preferred_element_type=jnp.float32)
    return bf16(mixed * (16.0 / math.sqrt(8192.0)))


def last_kernel(offset, with_heads, core_ref, matrix_ref, own_ref, other_ref, *refs):
    out_ref = refs[-1 - with_heads]
    part = pl.program_id(0)

    @pl.loop(0, HALF_F // 2)
    def _(step):
        columns = pl.ds(pl.multiple_of(step * 2 * BLK, 2 * BLK), 2 * BLK)
        out_ref[:, columns] = last_columns(
            core_ref, matrix_ref, own_ref, other_ref, part, columns
        )

    if with_heads:
        heads_ref = refs[-1]
        start = HALF_F * BLK
        middle = start + HALF_Q * BLK
        heads_ref[:, pl.ds(pl.multiple_of(part * HALF_Q * BLK, BLK), HALF_Q * BLK)] = last_columns(
            core_ref, matrix_ref, own_ref, other_ref, part, slice(start, middle)
        )
        heads_ref[:, pl.ds(pl.multiple_of((QPG + part) * BLK, BLK), BLK)] = last_columns(
            core_ref, matrix_ref, own_ref, other_ref, part, slice(middle, middle + BLK)
        )


def last_mix(core, own, other, offset, with_heads, target=None):
    width = own.shape[2]
    rows = 8 * ROWS
    outs = [jax.ShapeDtypeStruct((rows, 2 * FFB * BLK), jnp.bfloat16)]
    out_specs = [pl.BlockSpec((rows, HALF_F * BLK), lambda c: (0, offset + c))]
    if with_heads:
        outs.append(jax.ShapeDtypeStruct((rows, (QPG + 2) * BLK), jnp.bfloat16))
        out_specs.append(pl.BlockSpec((rows, (QPG + 2) * BLK), lambda c: (0, 0)))
    in_specs = [pl.BlockSpec(memory_space=pltpu.SMEM)] + whole(3)
    args = [core, jnp.asarray(last_matrices(), jnp.bfloat16), own, other]
    aliases = {}
    if target is not None:
        in_specs.append(pl.BlockSpec(memory_space=pl.ANY))
        args.append(target)
        aliases = {4: 0}
    return pl.pallas_call(
        functools.partial(last_kernel, offset, with_heads),
        grid=(2,),
        out_shape=outs,
        in_specs=in_specs,
        out_specs=out_specs,
        input_output_aliases=aliases,
        compiler_params=params(),
        cost_estimate=cost(8 * rows * rows * width, 12 * rows * width),
        name="last_mix",
    )(*args)


def order_kernel(owner_ref, order_ref, in_ref, out_ref):
    owner = owner_ref[0]
    for slot in range(FFB):
        block = order_ref[owner, slot]
        out_ref[slot * BLK : (slot + 1) * BLK, :] = in_ref[
            pl.ds(pl.multiple_of(block * BLK, BLK), BLK), :
        ]


def order_rows(owner, ffn_order, rows):
    return pl.pallas_call(
        order_kernel,
        out_shape=jax.ShapeDtypeStruct(rows.shape, jnp.bfloat16),
        in_specs=[pl.BlockSpec(memory_space=pltpu.SMEM)] * 2 + whole(1),
        out_specs=whole(1)[0],
        compiler_params=params(),
        cost_estimate=cost(rows.size, 4 * rows.size),
        name="order_rows",
    )(owner, ffn_order, rows)


def scalar(value):
    return value.astype(jnp.int32).reshape(1)


def exchange_plane(pieces):
    got = [pieces[0]]
    for k in range(1, PIECES):
        got.append(lax.ppermute(pieces[k], PLANE, [(i, i ^ k) for i in range(PIECES)]))
    return got


def exchange_depth(mixed):
    return lax.all_to_all(mixed, DEPTH, split_axis=0, concat_axis=0, tiled=True)


def exchange_core(got):
    return lax.ppermute(got, "core", [(0, 1), (1, 0)])


def per_device(
    q_weight,
    k_weight,
    v_weight,
    gate_weight,
    up_weight,
    down_weight,
    attn_gain,
    ffn_gain,
    head_order,
    ffn_order,
):
    shards = math.prod(lax.axis_size(name) for name in FSDP)
    owner = scalar(lax.axis_index(TP))
    place = scalar(lax.axis_index(PLANE))
    core = scalar(lax.axis_index("core"))
    gains = jnp.broadcast_to(jnp.stack([ffn_gain, attn_gain])[:, :, None], (2, ROWS, BLK))
    down_rotated = rotate_down(down_weight, shards)
    moved = lax.all_to_all(down_rotated, FSDP, split_axis=0, concat_axis=0, tiled=True)
    first = pick(place, head_order, ffn_order, gains, [gate_weight, q_weight, k_weight, v_weight])
    second = pick(place, head_order, ffn_order, gains, [up_weight])
    first_got = exchange_depth(first_mix(place, exchange_plane(first)))
    second_got = exchange_depth(first_mix(place, exchange_plane(second)))
    merged_ffn, merged_attn = last_mix(core, first_got, exchange_core(first_got), 0, True)
    (merged_ffn,) = last_mix(core, second_got, exchange_core(second_got), 2, False, merged_ffn)
    merged_down = order_rows(owner, ffn_order, moved.reshape(-1, moved.shape[2]))
    return (merged_attn, merged_ffn, merged_down)


def solution(mesh):
    split = Mesh(mesh.devices.reshape(2, 8, 2, 2, 4), ("xh", "z", "core", "xl", "y"))
    rows = TP + FSDP
    placed = (P(rows, None),) * 6 + (P(rows),) * 2 + (P(), P())
    return jax.shard_map(
        per_device,
        mesh=split,
        in_specs=placed,
        out_specs=(P(FSDP, TP), P(FSDP, TP), P(TP, FSDP)),
        check_vma=False,
    )
```

time: 418 us -> 274 us (0.66)
  local copies, waits for them, and re-layouts: 106 us -> 9.93 us
  waiting for transfers between devices: 224 us -> 144 us
  Pallas kernels: 0 us -> 34 us
  starting transfers between devices: 48.5 us -> 81.5 us
  other arithmetic: 23.7 us -> 0.74 us
  matrix products: 11.2 us -> 0 us
    all_to_all x7 -> x3, waiting for transfers between devices: 224 us -> 99 us  [the longest x2 54.2 us: exchange_depth(): return lax.all_to_all(mixed, DEPTH, split_axis=0, concat_axis=0, tiled=True)]
    ppermute x0 -> x32, starting transfers between devices: none -> 54.9 us  [the longest x30 54.3 us: exchange_plane(): lax.ppermute(pieces[k], PLANE, [(i, i ^ k) for i in range(PIECES)])]
    ppermute x0 -> x32, waiting for transfers between devices: none -> 45.5 us  [the longest x30 45.5 us: exchange_plane(): lax.ppermute(pieces[k], PLANE, [(i, i ^ k) for i in range(PIECES)])]
    all_to_all x8 -> x0, local copies, waits for them, and re-layouts: 36.5 us -> none  [the longest x3 21.6 us: per_device(): lax.all_to_all(row_groups[1], 'tp', split_axis=0, concat_axis=1, tiled=True)]
    pallas_call x0 -> x8, Pallas kernels: none -> 34 us  [the longest x2 12.7 us: last_mix(): pl.pallas_call(functools.partial(last_kernel, offset, with_heads), grid=(...]
    convert_element_type x8 -> x0, local copies, waits for them, and re-layouts: 33.3 us -> none  [the longest x6 18.7 us: second_rows(): (mixed * (1.0 / math.sqrt(small_sign.shape[0]))).reshape(matrix.shape)]
    all_to_all x7 -> x3, starting transfers between devices: 48.5 us -> 26.7 us  [the longest x2 18.7 us: exchange_depth(): return lax.all_to_all(mixed, DEPTH, split_axis=0, concat_axis=0, tiled=True)]
    reshape x5 -> x0, local copies, waits for them, and re-layouts: 13.2 us -> none  [the longest x2 6.98 us: first_rows(): shaped = matrix.reshape(count, -1, large_sign.shape[0])]
  transfers between devices with their start and end apart: 7 -> 35, of which waited for: 6 -> 18; matrix products, arithmetic and copies ran while one was open for 22% -> 0% of each run, Pallas kernels for 0% -> 8%
where the time goes in v1:
time: 274 us; the launch traced here: 272 us
  waiting for transfers between devices  144 us (53%)
  starting transfers between devices  81.5 us (30%)
  Pallas kernels  34 us (12%)
  local copies, waits for them, and re-layouts  9.93 us (4%)
    ppermute x30, starting transfers between devices, exchange_plane(): lax.ppermute(pieces[k], PLANE, [(i, i ^ k) for i in range(PIECES)])  54.3 us
    all_to_all x2, waiting for transfers between devices, exchange_depth(): return lax.all_to_all(mixed, DEPTH, split_axis=0, concat_axis=0, tiled=True)  54.2 us
    ppermute x30, waiting for transfers between devices, exchange_plane(): lax.ppermute(pieces[k], PLANE, [(i, i ^ k) for i in range(PIECES)])  45.5 us
    all_to_all x1, waiting for transfers between devices, per_device(): lax.all_to_all(down_rotated, FSDP, split_axis=0, concat_axis=0, tiled=True)  44.8 us
    all_to_all x2, starting transfers between devices, exchange_depth(): return lax.all_to_all(mixed, DEPTH, split_axis=0, concat_axis=0, tiled=True)  18.7 us
    pallas_call x2, Pallas kernels, last_mix(): pl.pallas_call(functools.partial(last_kernel, offset, with_heads), grid=(...  12.7 us
    pallas_call x2, Pallas kernels, first_mix(): pl.pallas_call(first_kernel, out_shape=jax.ShapeDtypeStruct((PIECES, ROWS...  11.4 us
    unnamed x34, local copies, waits for them, and re-layouts  9.86 us
  transfers between devices with their start and end apart: 35, of which 18 were waited for; matrix products, arithmetic and copies ran while one was open for 0% of the time, Pallas kernels for 8%

profile of v1, /device:TPU:25, one launch (start us, length us, event | category | flops | bytes accessed | tf_op | source)
XLA Modules:
  0.0 271.5 jit_solution(16262633342468184827)
XLA Ops:
  0.7 0.7 pad_maximum_fusion
  1.4 0.1 broadcast_in_dim.2.gain_ref
  1.5 1.5 copy-done.7
  3.0 0.7 copy-done.12
  3.7 0.7 copy-done.15
  4.3 1.9 pick_columns.3
  6.3 0.6 collective-permute-start.16
  6.8 0.6 collective-permute-start.17
  7.4 2.8 %collective-permute-start.18 = (bf16[32,1792]{1,0:T(8,128)(2,1)S(1)}, bf16[32,1792]{1,0:T(8,128)(2,1)S(1)}, u32[]{:S(2)}, u32[]{:S(2)}) collective-permute-start(bf16[32,1792]{1,0:T(8,128)(2,1)S(1)} %get-tuple-element.57), channel_id=1, source_target_pairs={{0,3},{1,2},{2,1},{3,0},{4,7},{5,6},{6,5},{7,4},{128,131},{129,130... | collective-permute-start | bytes 344072 | tf_op jit(solution)/shard_map/ppermute | solution.py:292
  10.2 1.2 collective-permute-start.19
  11.4 2.1 collective-permute-start.21
  13.5 2.6 collective-permute-start.22
  16.2 2.7 %collective-permute-start.23 = (bf16[32,1792]{1,0:T(8,128)(2,1)S(1)}, bf16[32,1792]{1,0:T(8,128)(2,1)S(1)}, u32[]{:S(2)}, u32[]{:S(2)}) collective-permute-start(bf16[32,1792]{1,0:T(8,128)(2,1)S(1)} %get-tuple-element.62), channel_id=1, source_target_pairs={{0,128},{1,129},{2,130},{3,131},{4,132},{5,133},{6,134},{7,135},{1... | collective-permute-start | bytes 344072 | tf_op jit(solution)/shard_map/ppermute | solution.py:292
  18.9 5.1 %collective-permute-start.25 = (bf16[32,1792]{1,0:T(8,128)(2,1)S(1)}, bf16[32,1792]{1,0:T(8,128)(2,1)S(1)}, u32[]{:S(2)}, u32[]{:S(2)}) collective-permute-start(bf16[32,1792]{1,0:T(8,128)(2,1)S(1)} %get-tuple-element.64), channel_id=1, source_target_pairs={{0,130},{1,131},{2,128},{3,129},{4,134},{5,135},{6,132},{7,133},{1... | collective-permute-start | bytes 344072 | tf_op jit(solution)/shard_map/ppermute | solution.py:292
  24.1 1.1 collective-permute-start.26
  25.1 2.5 collective-permute-start.27
  27.6 0.1 collective-permute-done.24.refs_9_
  27.7 4.8 %collective-permute-start.29 = (bf16[32,1792]{1,0:T(8,128)(2,1)S(1)}, bf16[32,1792]{1,0:T(8,128)(2,1)S(1)}, u32[]{:S(2)}, u32[]{:S(2)}) collective-permute-start(bf16[32,1792]{1,0:T(8,128)(2,1)S(1)} %get-tuple-element.68), channel_id=1, source_target_pairs={{0,134},{1,135},{2,132},{3,133},{4,130},{5,131},{6,128},{7,129},{1... | collective-permute-start | bytes 344072 | tf_op jit(solution)/shard_map/ppermute | solution.py:292
  32.5 1.0 collective-permute-start.30
  33.5 3.6 %collective-permute-done.27.refs_12_ = bf16[32,1792]{1,0:T(8,128)(2,1)S(1)} collective-permute-done((bf16[32,1792]{1,0:T(8,128)(2,1)S(1)}, bf16[32,1792]{1,0:T(8,128)(2,1)S(1)}, u32[]{:S(2)}, u32[]{:S(2)}) %collective-permute-start.27) | collective-permute-done | bytes 114720 | tf_op jit(solution)/shard_map/ppermute | solution.py:292
  37.1 2.2 collective-permute-done.28.refs_13_
  39.3 2.7 collective-permute-done.29.refs_14_
  42.0 1.9 collective-permute-done.30.refs_15_
  43.9 5.6 %first_mix.3 = bf16[16,32,1792]{2,1,0:T(8,128)(2,1)} custom-call(s32[1]{0:T(128)} %bitcast.1.place_ref, bf16[512,512]{1,0:T(8,128)(2,1)S(1)} %copy-done.5, bf16[32,1792]{1,0:T(8,128)(2,1)S(1)} %get-tuple-element.54.refs_0_, bf16[32,1792]{1,0:T(8,128)(2,1)S(1)} %collective-permute-done.16.refs_1_, bf16[32,1792]{1,0:T(8,128)(2,1)S(1)} %collective-permute-done.17.refs_2_, ...), custom_call_target="tpu_custom_call" | custom-call | flops 939524096 | bytes 3670016 | tf_op jit(solution)/shard_map/first_mix/pallas_call | solution.py:192
  49.5 8.9 %all-to-all-start.1 = ((bf16[16,32,1792]{2,1,0:T(8,128)(2,1)}), bf16[16,32,1792]{2,1,0:T(8,128)(2,1)S(1)}, u32[]{:S(2)}, u32[]{:S(2)}) async-start(bf16[16,32,1792]{2,1,0:T(8,128)(2,1)} %first_mix.3), calls=%async_computation.1 | async-start | bytes 3670016 | tf_op jit(solution)/shard_map/all_to_all | solution.py:297
  58.5 1.5 copy-done.8
  59.9 2.5 pick_columns.2
  62.4 0.8 collective-permute-start
  63.2 3.3 %collective-permute-start.1 = (bf16[32,2432]{1,0:T(8,128)(2,1)S(1)}, bf16[32,2432]{1,0:T(8,128)(2,1)S(1)}, u32[]{:S(2)}, u32[]{:S(2)}) collective-permute-start(bf16[32,2432]{1,0:T(8,128)(2,1)S(1)} %get-tuple-element.39), channel_id=1, source_target_pairs={{0,2},{1,3},{2,0},{3,1},{4,6},{5,7},{6,4},{7,5},{128,130},{129,131... | collective-permute-start | bytes 466952 | tf_op jit(solution)/shard_map/ppermute | solution.py:292
  66.5 0.1 collective-permute-start.3
  66.7 1.0 collective-permute-start.4
  67.6 3.7 %collective-permute-start.5 = (bf16[32,2432]{1,0:T(8,128)(2,1)S(1)}, bf16[32,2432]{1,0:T(8,128)(2,1)S(1)}, u32[]{:S(2)}, u32[]{:S(2)}) collective-permute-start(bf16[32,2432]{1,0:T(8,128)(2,1)S(1)} %get-tuple-element.43), channel_id=1, source_target_pairs={{0,6},{1,7},{2,4},{3,5},{4,2},{5,3},{6,0},{7,1},{128,134},{129,135... | collective-permute-start | bytes 466952 | tf_op jit(solution)/shard_map/ppermute | solution.py:292
  71.3 2.0 collective-permute-done.1.refs_2_
  73.2 2.6 collective-permute-done.2.refs_3_
  75.8 2.6 collective-permute-start.7
  78.4 4.3 %collective-permute-start.9 = (bf16[32,2432]{1,0:T(8,128)(2,1)S(1)}, bf16[32,2432]{1,0:T(8,128)(2,1)S(1)}, u32[]{:S(2)}, u32[]{:S(2)}) collective-permute-start(bf16[32,2432]{1,0:T(8,128)(2,1)S(1)} %get-tuple-element.47), channel_id=1, source_target_pairs={{0,130},{1,131},{2,128},{3,129},{4,134},{5,135},{6,132},{7,133},{1... | collective-permute-start | bytes 466952 | tf_op jit(solution)/shard_map/ppermute | solution.py:292
  82.7 3.5 %collective-permute-start.10 = (bf16[32,2432]{1,0:T(8,128)(2,1)S(1)}, bf16[32,2432]{1,0:T(8,128)(2,1)S(1)}, u32[]{:S(2)}, u32[]{:S(2)}) collective-permute-start(bf16[32,2432]{1,0:T(8,128)(2,1)S(1)} %get-tuple-element.48), channel_id=1, source_target_pairs={{0,131},{1,130},{2,129},{3,128},{4,135},{5,134},{6,133},{7,132},{1... | collective-permute-start | bytes 466952 | tf_op jit(solution)/shard_map/ppermute | solution.py:292
  86.2 7.8 %collective-permute-done.6.refs_7_ = bf16[32,2432]{1,0:T(8,128)(2,1)S(1)} collective-permute-done((bf16[32,2432]{1,0:T(8,128)(2,1)S(1)}, bf16[32,2432]{1,0:T(8,128)(2,1)S(1)}, u32[]{:S(2)}, u32[]{:S(2)}) %collective-permute-start.6) | collective-permute-done | bytes 155680 | tf_op jit(solution)/shard_map/ppermute | solution.py:292
  94.0 3.1 %collective-permute-done.7.refs_8_ = bf16[32,2432]{1,0:T(8,128)(2,1)S(1)} collective-permute-done((bf16[32,2432]{1,0:T(8,128)(2,1)S(1)}, bf16[32,2432]{1,0:T(8,128)(2,1)S(1)}, u32[]{:S(2)}, u32[]{:S(2)}) %collective-permute-start.7) | collective-permute-done | bytes 155680 | tf_op jit(solution)/shard_map/ppermute | solution.py:292
  97.1 1.2 collective-permute-start.12
  98.3 2.6 collective-permute-done.8.refs_9_
  100.8 5.8 %collective-permute-start.13 = (bf16[32,2432]{1,0:T(8,128)(2,1)S(1)}, bf16[32,2432]{1,0:T(8,128)(2,1)S(1)}, u32[]{:S(2)}, u32[]{:S(2)}) collective-permute-start(bf16[32,2432]{1,0:T(8,128)(2,1)S(1)} %get-tuple-element.51), channel_id=1, source_target_pairs={{0,134},{1,135},{2,132},{3,133},{4,130},{5,131},{6,128},{7,129},{1... | collective-permute-start | bytes 466952 | tf_op jit(solution)/shard_map/ppermute | solution.py:292
  106.7 1.2 collective-permute-done.9.refs_10_
  107.9 0.9 collective-permute-start.14
  108.8 2.0 collective-permute-done.10.refs_11_
  110.8 3.4 %collective-permute-done.11.refs_12_ = bf16[32,2432]{1,0:T(8,128)(2,1)S(1)} collective-permute-done((bf16[32,2432]{1,0:T(8,128)(2,1)S(1)}, bf16[32,2432]{1,0:T(8,128)(2,1)S(1)}, u32[]{:S(2)}, u32[]{:S(2)}) %collective-permute-start.11) | collective-permute-done | bytes 155680 | tf_op jit(solution)/shard_map/ppermute | solution.py:292
  114.1 0.9 collective-permute-done.12.refs_13_
  115.0 5.7 %collective-permute-done.13.refs_14_ = bf16[32,2432]{1,0:T(8,128)(2,1)S(1)} collective-permute-done((bf16[32,2432]{1,0:T(8,128)(2,1)S(1)}, bf16[32,2432]{1,0:T(8,128)(2,1)S(1)}, u32[]{:S(2)}, u32[]{:S(2)}) %collective-permute-start.13) | collective-permute-done | bytes 155680 | tf_op jit(solution)/shard_map/ppermute | solution.py:292
  120.7 3.9 %collective-permute-done.14.refs_15_ = bf16[32,2432]{1,0:T(8,128)(2,1)S(1)} collective-permute-done((bf16[32,2432]{1,0:T(8,128)(2,1)S(1)}, bf16[32,2432]{1,0:T(8,128)(2,1)S(1)}, u32[]{:S(2)}, u32[]{:S(2)}) %collective-permute-start.14) | collective-permute-done | bytes 155680 | tf_op jit(solution)/shard_map/ppermute | solution.py:292
  124.6 5.8 %first_mix.2 = bf16[16,32,2432]{2,1,0:T(8,128)(2,1)S(1)} custom-call(s32[1]{0:T(128)} %bitcast.1.place_ref, bf16[512,512]{1,0:T(8,128)(2,1)S(1)} %copy-done.5, bf16[32,2432]{1,0:T(8,128)(2,1)S(1)} %get-tuple-element.37.refs_0_, bf16[32,2432]{1,0:T(8,128)(2,1)S(1)} %collective-permute-done.refs_1_, bf16[32,2432]{1,0:T(8,128)(2,1)S(1)} %collective-permute-done.1.refs_2_, ...), custom_call_target="tpu_custom_call" | custom-call | flops 1275068416 | bytes 4980736 | tf_op jit(solution)/shard_map/first_mix/pallas_call | solution.py:192
  130.5 1.4 copy-done
  131.9 1.3 copy-done.2
  133.2 9.9 %all-to-all-start = ((bf16[16,32,2432]{2,1,0:T(8,128)(2,1)}), bf16[16,32,2432]{2,1,0:T(8,128)(2,1)S(1)}, u32[]{:S(2)}, u32[]{:S(2)}) async-start(bf16[16,32,2432]{2,1,0:T(8,128)(2,1)} %copy-done), calls=%async_computation | async-start | bytes 4980736 | tf_op jit(solution)/shard_map/all_to_all | solution.py:297
  143.1 1.5 copy-done.6
  144.6 2.6 down_rotate.1
  147.2 1.2 copy-done.1
  148.4 54.2 %all-to-all-done.own_ref = bf16[16,32,2432]{2,1,0:T(8,128)(2,1)S(1)} async-done(((bf16[16,32,2432]{2,1,0:T(8,128)(2,1)}), bf16[16,32,2432]{2,1,0:T(8,128)(2,1)S(1)}, u32[]{:S(2)}, u32[]{:S(2)}) %all-to-all-start) | async-done | bytes 2490400 | tf_op jit(solution)/shard_map/all_to_all | solution.py:297
  202.6 7.9 %all-to-all-start.2 = ((bf16[32,112,256]{2,1,0:T(8,128)(2,1)}), bf16[32,112,256]{2,1,0:T(8,128)(2,1)}, u32[]{:S(2)}, u32[]{:S(2)}) async-start(bf16[32,112,256]{2,1,0:T(8,128)(2,1)} %copy-done.1), calls=%async_computation.2 | async-start | bytes 3670016 | tf_op jit(solution)/shard_map/all_to_all | solution.py:322
  210.6 0.4 collective-permute-start.15
  211.0 0.2 collective-permute-start.31
  211.2 44.8 %all-to-all-done.2 = bf16[32,112,256]{2,1,0:T(8,128)(2,1)} async-done(((bf16[32,112,256]{2,1,0:T(8,128)(2,1)}), bf16[32,112,256]{2,1,0:T(8,128)(2,1)}, u32[]{:S(2)}, u32[]{:S(2)}) %all-to-all-start.2) | async-done | bytes 1835040 | tf_op jit(solution)/shard_map/all_to_all | solution.py:322
  255.9 2.9 %order_rows.1 = bf16[3584,256]{1,0:T(8,128)(2,1)} custom-call(s32[1]{0:T(128)} %bitcast.4.owner_ref, s32[8,28]{1,0:T(8,128)S(1)} %copy-done.13, bf16[3584,256]{1,0:T(8,128)(2,1)} %bitcast.5.in_ref), custom_call_target="tpu_custom_call" | custom-call | flops 917504 | bytes 3670016 | tf_op jit(solution)/shard_map/order_rows/pallas_call | solution.py:274
  258.9 6.9 %last_mix.2 = (bf16[256,7168]{1,0:T(8,128)(2,1)}, bf16[256,1280]{1,0:T(8,128)(2,1)}) custom-call(s32[1]{0:T(128)} %bitcast.core_ref, bf16[2,2,256,256]{3,2,1,0:T(8,128)(2,1)S(1)} %copy-done.4, bf16[16,32,2432]{2,1,0:T(8,128)(2,1)S(1)} %all-to-all-done.own_ref, bf16[16,32,2432]{2,1,0:T(8,128)(2,1)} %collective-permute-done.15.other_ref), custom_call_target="tpu_custom_call" | custom-call | flops 1275068416 | bytes 7471104 | tf_op jit(solution)/shard_map/last_mix/pallas_call | solution.py:251
  265.7 5.8 %last_mix.3 = bf16[256,7168]{1,0:T(8,128)(2,1)} custom-call(s32[1]{0:T(128)} %bitcast.core_ref, bf16[2,2,256,256]{3,2,1,0:T(8,128)(2,1)S(1)} %copy-done.4, bf16[16,32,1792]{2,1,0:T(8,128)(2,1)S(1)} %copy-done.3, bf16[16,32,1792]{2,1,0:T(8,128)(2,1)} %collective-permute-done.31.other_ref, ...), custom_call_target="tpu_custom_call", output_to_operand_aliasing={{}: (4, {})} | custom-call | flops 939524096 | bytes 5505024 | tf_op jit(solution)/shard_map/last_mix/pallas_call | solution.py:251
  (50 shorter events, 0.1 us)
Async XLA Ops:
  0.6 43.3 %copy-start.5 = (bf16[512,512]{1,0:T(8,128)(2,1)S(1)}, bf16[512,512]{1,0:T(8,128)(2,1)}, u32[]{:S(2)}) copy-start(bf16[512,512]{1,0:T(8,128)(2,1)} %constant.27.clone.matrix_ref) | copy-start | bytes 1572868
  1.5 1.5 copy-start.7
  3.0 0.7 copy-start.12
  3.7 0.7 copy-start.15
  6.3 5.2 %collective-permute-start.16 = (bf16[32,1792]{1,0:T(8,128)(2,1)S(1)}, bf16[32,1792]{1,0:T(8,128)(2,1)S(1)}, u32[]{:S(2)}, u32[]{:S(2)}) collective-permute-start(bf16[32,1792]{1,0:T(8,128)(2,1)S(1)} %get-tuple-element.55), channel_id=1, source_target_pairs={{0,1},{1,0},{2,3},{3,2},{4,5},{5,4},{6,7},{7,6},{128,129},{129,128... | collective-permute-start | bytes 344072 | tf_op jit(solution)/shard_map/ppermute | solution.py:292
  6.8 6.7 %collective-permute-start.17 = (bf16[32,1792]{1,0:T(8,128)(2,1)S(1)}, bf16[32,1792]{1,0:T(8,128)(2,1)S(1)}, u32[]{:S(2)}, u32[]{:S(2)}) collective-permute-start(bf16[32,1792]{1,0:T(8,128)(2,1)S(1)} %get-tuple-element.56), channel_id=1, source_target_pairs={{0,2},{1,3},{2,0},{3,1},{4,6},{5,7},{6,4},{7,5},{128,130},{129,131... | collective-permute-start | bytes 344072 | tf_op jit(solution)/shard_map/ppermute | solution.py:292
  7.4 8.8 %collective-permute-start.18 = (bf16[32,1792]{1,0:T(8,128)(2,1)S(1)}, bf16[32,1792]{1,0:T(8,128)(2,1)S(1)}, u32[]{:S(2)}, u32[]{:S(2)}) collective-permute-start(bf16[32,1792]{1,0:T(8,128)(2,1)S(1)} %get-tuple-element.57), channel_id=1, source_target_pairs={{0,3},{1,2},{2,1},{3,0},{4,7},{5,6},{6,5},{7,4},{128,131},{129,130... | collective-permute-start | bytes 344072 | tf_op jit(solution)/shard_map/ppermute | solution.py:292
  10.2 8.7 %collective-permute-start.19 = (bf16[32,1792]{1,0:T(8,128)(2,1)S(1)}, bf16[32,1792]{1,0:T(8,128)(2,1)S(1)}, u32[]{:S(2)}, u32[]{:S(2)}) collective-permute-start(bf16[32,1792]{1,0:T(8,128)(2,1)S(1)} %get-tuple-element.58), channel_id=1, source_target_pairs={{0,4},{1,5},{2,6},{3,7},{4,0},{5,1},{6,2},{7,3},{128,132},{129,133... | collective-permute-start | bytes 344072 | tf_op jit(solution)/shard_map/ppermute | solution.py:292
  11.4 7.5 %collective-permute-start.20 = (bf16[32,1792]{1,0:T(8,128)(2,1)S(1)}, bf16[32,1792]{1,0:T(8,128)(2,1)S(1)}, u32[]{:S(2)}, u32[]{:S(2)}) collective-permute-start(bf16[32,1792]{1,0:T(8,128)(2,1)S(1)} %get-tuple-element.59), channel_id=1, source_target_pairs={{0,5},{1,4},{2,7},{3,6},{4,1},{5,0},{6,3},{7,2},{128,133},{129,132... | collective-permute-start | bytes 344072 | tf_op jit(solution)/shard_map/ppermute | solution.py:292
  11.4 12.6 %collective-permute-start.21 = (bf16[32,1792]{1,0:T(8,128)(2,1)S(1)}, bf16[32,1792]{1,0:T(8,128)(2,1)S(1)}, u32[]{:S(2)}, u32[]{:S(2)}) collective-permute-start(bf16[32,1792]{1,0:T(8,128)(2,1)S(1)} %get-tuple-element.60), channel_id=1, source_target_pairs={{0,6},{1,7},{2,4},{3,5},{4,2},{5,3},{6,0},{7,1},{128,134},{129,135... | collective-permute-start | bytes 344072 | tf_op jit(solution)/shard_map/ppermute | solution.py:292
  13.5 11.6 %collective-permute-start.22 = (bf16[32,1792]{1,0:T(8,128)(2,1)S(1)}, bf16[32,1792]{1,0:T(8,128)(2,1)S(1)}, u32[]{:S(2)}, u32[]{:S(2)}) collective-permute-start(bf16[32,1792]{1,0:T(8,128)(2,1)S(1)} %get-tuple-element.61), channel_id=1, source_target_pairs={{0,7},{1,6},{2,5},{3,4},{4,3},{5,2},{6,1},{7,0},{128,135},{129,134... | collective-permute-start | bytes 344072 | tf_op jit(solution)/shard_map/ppermute | solution.py:292
  16.2 11.4 %collective-permute-start.23 = (bf16[32,1792]{1,0:T(8,128)(2,1)S(1)}, bf16[32,1792]{1,0:T(8,128)(2,1)S(1)}, u32[]{:S(2)}, u32[]{:S(2)}) collective-permute-start(bf16[32,1792]{1,0:T(8,128)(2,1)S(1)} %get-tuple-element.62), channel_id=1, source_target_pairs={{0,128},{1,129},{2,130},{3,131},{4,132},{5,133},{6,134},{7,135},{1... | collective-permute-start | bytes 344072 | tf_op jit(solution)/shard_map/ppermute | solution.py:292
  18.9 8.8 %collective-permute-start.24 = (bf16[32,1792]{1,0:T(8,128)(2,1)S(1)}, bf16[32,1792]{1,0:T(8,128)(2,1)S(1)}, u32[]{:S(2)}, u32[]{:S(2)}) collective-permute-start(bf16[32,1792]{1,0:T(8,128)(2,1)S(1)} %get-tuple-element.63), channel_id=1, source_target_pairs={{0,129},{1,128},{2,131},{3,130},{4,133},{5,132},{6,135},{7,134},{1... | collective-permute-start | bytes 344072 | tf_op jit(solution)/shard_map/ppermute | solution.py:292
  18.9 13.6 %collective-permute-start.25 = (bf16[32,1792]{1,0:T(8,128)(2,1)S(1)}, bf16[32,1792]{1,0:T(8,128)(2,1)S(1)}, u32[]{:S(2)}, u32[]{:S(2)}) collective-permute-start(bf16[32,1792]{1,0:T(8,128)(2,1)S(1)} %get-tuple-element.64), channel_id=1, source_target_pairs={{0,130},{1,131},{2,128},{3,129},{4,134},{5,135},{6,132},{7,133},{1... | collective-permute-start | bytes 344072 | tf_op jit(solution)/shard_map/ppermute | solution.py:292
  24.1 9.4 %collective-permute-start.26 = (bf16[32,1792]{1,0:T(8,128)(2,1)S(1)}, bf16[32,1792]{1,0:T(8,128)(2,1)S(1)}, u32[]{:S(2)}, u32[]{:S(2)}) collective-permute-start(bf16[32,1792]{1,0:T(8,128)(2,1)S(1)} %get-tuple-element.65), channel_id=1, source_target_pairs={{0,131},{1,130},{2,129},{3,128},{4,135},{5,134},{6,133},{7,132},{1... | collective-permute-start | bytes 344072 | tf_op jit(solution)/shard_map/ppermute | solution.py:292
  25.1 12.0 %collective-permute-start.27 = (bf16[32,1792]{1,0:T(8,128)(2,1)S(1)}, bf16[32,1792]{1,0:T(8,128)(2,1)S(1)}, u32[]{:S(2)}, u32[]{:S(2)}) collective-permute-start(bf16[32,1792]{1,0:T(8,128)(2,1)S(1)} %get-tuple-element.66), channel_id=1, source_target_pairs={{0,132},{1,133},{2,134},{3,135},{4,128},{5,129},{6,130},{7,131},{1... | collective-permute-start | bytes 344072 | tf_op jit(solution)/shard_map/ppermute | solution.py:292
  27.6 11.7 %collective-permute-start.28 = (bf16[32,1792]{1,0:T(8,128)(2,1)S(1)}, bf16[32,1792]{1,0:T(8,128)(2,1)S(1)}, u32[]{:S(2)}, u32[]{:S(2)}) collective-permute-start(bf16[32,1792]{1,0:T(8,128)(2,1)S(1)} %get-tuple-element.67), channel_id=1, source_target_pairs={{0,133},{1,132},{2,135},{3,134},{4,129},{5,128},{6,131},{7,130},{1... | collective-permute-start | bytes 344072 | tf_op jit(solution)/shard_map/ppermute | solution.py:292
  27.7 14.3 %collective-permute-start.29 = (bf16[32,1792]{1,0:T(8,128)(2,1)S(1)}, bf16[32,1792]{1,0:T(8,128)(2,1)S(1)}, u32[]{:S(2)}, u32[]{:S(2)}) collective-permute-start(bf16[32,1792]{1,0:T(8,128)(2,1)S(1)} %get-tuple-element.68), channel_id=1, source_target_pairs={{0,134},{1,135},{2,132},{3,133},{4,130},{5,131},{6,128},{7,129},{1... | collective-permute-start | bytes 344072 | tf_op jit(solution)/shard_map/ppermute | solution.py:292
  32.5 11.4 %collective-permute-start.30 = (bf16[32,1792]{1,0:T(8,128)(2,1)S(1)}, bf16[32,1792]{1,0:T(8,128)(2,1)S(1)}, u32[]{:S(2)}, u32[]{:S(2)}) collective-permute-start(bf16[32,1792]{1,0:T(8,128)(2,1)S(1)} %get-tuple-element.69), channel_id=1, source_target_pairs={{0,135},{1,134},{2,133},{3,132},{4,131},{5,130},{6,129},{7,128},{1... | collective-permute-start | bytes 344072 | tf_op jit(solution)/shard_map/ppermute | solution.py:292
  49.5 8.9 %copy-start.9 = (bf16[32,8192]{1,0:T(8,128)(2,1)S(1)}, bf16[32,8192]{1,0:T(8,128)(2,1)}, u32[]{:S(2)}) copy-start(bf16[32,8192]{1,0:T(8,128)(2,1)} %refs_1_.1) | copy-start | bytes 1572868
  49.5 8.9 %copy-start.10 = (bf16[32,1024]{1,0:T(8,128)(2,1)S(1)}, bf16[32,1024]{1,0:T(8,128)(2,1)}, u32[]{:S(2)}) copy-start(bf16[32,1024]{1,0:T(8,128)(2,1)} %refs_2_.1) | copy-start | bytes 196612
  49.5 8.9 %copy-start.11 = (bf16[32,1024]{1,0:T(8,128)(2,1)S(1)}, bf16[32,1024]{1,0:T(8,128)(2,1)}, u32[]{:S(2)}) copy-start(bf16[32,1024]{1,0:T(8,128)(2,1)} %refs_3_.1) | copy-start | bytes 196612
  49.5 8.9 %copy-start.13 = (s32[8,28]{1,0:T(8,128)S(1)}, s32[8,28]{1,0:T(8,128)}, u32[]{:S(2)}) copy-start(s32[8,28]{1,0:T(8,128)} %order_ref.5) | copy-start | bytes 2692
  49.5 8.9 %copy-start.16 = (s32[8,8]{1,0:T(8,128)S(1)}, s32[8,8]{1,0:T(8,128)}, u32[]{:S(2)}) copy-start(s32[8,8]{1,0:T(8,128)} %heads_ref.3) | copy-start | bytes 772
  49.5 82.4 %all-to-all-start.1 = ((bf16[16,32,1792]{2,1,0:T(8,128)(2,1)}), bf16[16,32,1792]{2,1,0:T(8,128)(2,1)S(1)}, u32[]{:S(2)}, u32[]{:S(2)}) async-start(bf16[16,32,1792]{2,1,0:T(8,128)(2,1)} %first_mix.3), calls=%async_computation.1 | async-start | bytes 3670016 | tf_op jit(solution)/shard_map/all_to_all | solution.py:297
  58.4 1.5 copy-start.8
  62.4 5.2 %collective-permute-start = (bf16[32,2432]{1,0:T(8,128)(2,1)S(1)}, bf16[32,2432]{1,0:T(8,128)(2,1)S(1)}, u32[]{:S(2)}, u32[]{:S(2)}) collective-permute-start(bf16[32,2432]{1,0:T(8,128)(2,1)S(1)} %get-tuple-element.38), channel_id=1, source_target_pairs={{0,1},{1,0},{2,3},{3,2},{4,5},{5,4},{6,7},{7,6},{128,129},{129,128... | collective-permute-start | bytes 466952 | tf_op jit(solution)/shard_map/ppermute | solution.py:292
  63.2 10.0 %collective-permute-start.1 = (bf16[32,2432]{1,0:T(8,128)(2,1)S(1)}, bf16[32,2432]{1,0:T(8,128)(2,1)S(1)}, u32[]{:S(2)}, u32[]{:S(2)}) collective-permute-start(bf16[32,2432]{1,0:T(8,128)(2,1)S(1)} %get-tuple-element.39), channel_id=1, source_target_pairs={{0,2},{1,3},{2,0},{3,1},{4,6},{5,7},{6,4},{7,5},{128,130},{129,131... | collective-permute-start | bytes 466952 | tf_op jit(solution)/shard_map/ppermute | solution.py:292
  66.5 9.3 %collective-permute-start.2 = (bf16[32,2432]{1,0:T(8,128)(2,1)S(1)}, bf16[32,2432]{1,0:T(8,128)(2,1)S(1)}, u32[]{:S(2)}, u32[]{:S(2)}) collective-permute-start(bf16[32,2432]{1,0:T(8,128)(2,1)S(1)} %get-tuple-element.40), channel_id=1, source_target_pairs={{0,3},{1,2},{2,1},{3,0},{4,7},{5,6},{6,5},{7,4},{128,131},{129,130... | collective-permute-start | bytes 466952 | tf_op jit(solution)/shard_map/ppermute | solution.py:292
  66.5 11.9 %collective-permute-start.3 = (bf16[32,2432]{1,0:T(8,128)(2,1)S(1)}, bf16[32,2432]{1,0:T(8,128)(2,1)S(1)}, u32[]{:S(2)}, u32[]{:S(2)}) collective-permute-start(bf16[32,2432]{1,0:T(8,128)(2,1)S(1)} %get-tuple-element.41), channel_id=1, source_target_pairs={{0,4},{1,5},{2,6},{3,7},{4,0},{5,1},{6,2},{7,3},{128,132},{129,133... | collective-permute-start | bytes 466952 | tf_op jit(solution)/shard_map/ppermute | solution.py:292
  66.7 11.8 %collective-permute-start.4 = (bf16[32,2432]{1,0:T(8,128)(2,1)S(1)}, bf16[32,2432]{1,0:T(8,128)(2,1)S(1)}, u32[]{:S(2)}, u32[]{:S(2)}) collective-permute-start(bf16[32,2432]{1,0:T(8,128)(2,1)S(1)} %get-tuple-element.42), channel_id=1, source_target_pairs={{0,5},{1,4},{2,7},{3,6},{4,1},{5,0},{6,3},{7,2},{128,133},{129,132... | collective-permute-start | bytes 466952 | tf_op jit(solution)/shard_map/ppermute | solution.py:292
  67.6 15.1 %collective-permute-start.5 = (bf16[32,2432]{1,0:T(8,128)(2,1)S(1)}, bf16[32,2432]{1,0:T(8,128)(2,1)S(1)}, u32[]{:S(2)}, u32[]{:S(2)}) collective-permute-start(bf16[32,2432]{1,0:T(8,128)(2,1)S(1)} %get-tuple-element.43), channel_id=1, source_target_pairs={{0,6},{1,7},{2,4},{3,5},{4,2},{5,3},{6,0},{7,1},{128,134},{129,135... | collective-permute-start | bytes 466952 | tf_op jit(solution)/shard_map/ppermute | solution.py:292
  73.2 20.8 %collective-permute-start.6 = (bf16[32,2432]{1,0:T(8,128)(2,1)S(1)}, bf16[32,2432]{1,0:T(8,128)(2,1)S(1)}, u32[]{:S(2)}, u32[]{:S(2)}) collective-permute-start(bf16[32,2432]{1,0:T(8,128)(2,1)S(1)} %get-tuple-element.44), channel_id=1, source_target_pairs={{0,7},{1,6},{2,5},{3,4},{4,3},{5,2},{6,1},{7,0},{128,135},{129,134... | collective-permute-start | bytes 466952 | tf_op jit(solution)/shard_map/ppermute | solution.py:292
  75.8 21.2 %collective-permute-start.7 = (bf16[32,2432]{1,0:T(8,128)(2,1)S(1)}, bf16[32,2432]{1,0:T(8,128)(2,1)S(1)}, u32[]{:S(2)}, u32[]{:S(2)}) collective-permute-start(bf16[32,2432]{1,0:T(8,128)(2,1)S(1)} %get-tuple-element.45), channel_id=1, source_target_pairs={{0,128},{1,129},{2,130},{3,131},{4,132},{5,133},{6,134},{7,135},{1... | collective-permute-start | bytes 466952 | tf_op jit(solution)/shard_map/ppermute | solution.py:292
  78.4 22.4 %collective-permute-start.8 = (bf16[32,2432]{1,0:T(8,128)(2,1)S(1)}, bf16[32,2432]{1,0:T(8,128)(2,1)S(1)}, u32[]{:S(2)}, u32[]{:S(2)}) collective-permute-start(bf16[32,2432]{1,0:T(8,128)(2,1)S(1)} %get-tuple-element.46), channel_id=1, source_target_pairs={{0,129},{1,128},{2,131},{3,130},{4,133},{5,132},{6,135},{7,134},{1... | collective-permute-start | bytes 466952 | tf_op jit(solution)/shard_map/ppermute | solution.py:292
  78.4 29.5 %collective-permute-start.9 = (bf16[32,2432]{1,0:T(8,128)(2,1)S(1)}, bf16[32,2432]{1,0:T(8,128)(2,1)S(1)}, u32[]{:S(2)}, u32[]{:S(2)}) collective-permute-start(bf16[32,2432]{1,0:T(8,128)(2,1)S(1)} %get-tuple-element.47), channel_id=1, source_target_pairs={{0,130},{1,131},{2,128},{3,129},{4,134},{5,135},{6,132},{7,133},{1... | collective-permute-start | bytes 466952 | tf_op jit(solution)/shard_map/ppermute | solution.py:292
  82.7 28.1 %collective-permute-start.10 = (bf16[32,2432]{1,0:T(8,128)(2,1)S(1)}, bf16[32,2432]{1,0:T(8,128)(2,1)S(1)}, u32[]{:S(2)}, u32[]{:S(2)}) collective-permute-start(bf16[32,2432]{1,0:T(8,128)(2,1)S(1)} %get-tuple-element.48), channel_id=1, source_target_pairs={{0,131},{1,130},{2,129},{3,128},{4,135},{5,134},{6,133},{7,132},{1... | collective-permute-start | bytes 466952 | tf_op jit(solution)/shard_map/ppermute | solution.py:292
  94.0 20.1 %collective-permute-start.11 = (bf16[32,2432]{1,0:T(8,128)(2,1)S(1)}, bf16[32,2432]{1,0:T(8,128)(2,1)S(1)}, u32[]{:S(2)}, u32[]{:S(2)}) collective-permute-start(bf16[32,2432]{1,0:T(8,128)(2,1)S(1)} %get-tuple-element.49), channel_id=1, source_target_pairs={{0,132},{1,133},{2,134},{3,135},{4,128},{5,129},{6,130},{7,131},{1... | collective-permute-start | bytes 466952 | tf_op jit(solution)/shard_map/ppermute | solution.py:292
  97.1 18.0 %collective-permute-start.12 = (bf16[32,2432]{1,0:T(8,128)(2,1)S(1)}, bf16[32,2432]{1,0:T(8,128)(2,1)S(1)}, u32[]{:S(2)}, u32[]{:S(2)}) collective-permute-start(bf16[32,2432]{1,0:T(8,128)(2,1)S(1)} %get-tuple-element.50), channel_id=1, source_target_pairs={{0,133},{1,132},{2,135},{3,134},{4,129},{5,128},{6,131},{7,130},{1... | collective-permute-start | bytes 466952 | tf_op jit(solution)/shard_map/ppermute | solution.py:292
  100.8 19.9 %collective-permute-start.13 = (bf16[32,2432]{1,0:T(8,128)(2,1)S(1)}, bf16[32,2432]{1,0:T(8,128)(2,1)S(1)}, u32[]{:S(2)}, u32[]{:S(2)}) collective-permute-start(bf16[32,2432]{1,0:T(8,128)(2,1)S(1)} %get-tuple-element.51), channel_id=1, source_target_pairs={{0,134},{1,135},{2,132},{3,133},{4,130},{5,131},{6,128},{7,129},{1... | collective-permute-start | bytes 466952 | tf_op jit(solution)/shard_map/ppermute | solution.py:292
  107.9 16.7 %collective-permute-start.14 = (bf16[32,2432]{1,0:T(8,128)(2,1)S(1)}, bf16[32,2432]{1,0:T(8,128)(2,1)S(1)}, u32[]{:S(2)}, u32[]{:S(2)}) collective-permute-start(bf16[32,2432]{1,0:T(8,128)(2,1)S(1)} %get-tuple-element.52), channel_id=1, source_target_pairs={{0,135},{1,134},{2,133},{3,132},{4,131},{5,130},{6,129},{7,128},{1... | collective-permute-start | bytes 466952 | tf_op jit(solution)/shard_map/ppermute | solution.py:292
  130.5 1.5 copy-start
  131.9 11.2 %copy-start.14 = (bf16[128,128]{1,0:T(8,128)(2,1)S(1)}, bf16[128,128]{1,0:T(8,128)(2,1)}, u32[]{:S(2)}) copy-start(bf16[128,128]{1,0:T(8,128)(2,1)} %constant.26.clone.sign_ref) | copy-start | bytes 98308
  131.9 1.3 copy-start.2
  133.2 69.4 %all-to-all-start = ((bf16[16,32,2432]{2,1,0:T(8,128)(2,1)}), bf16[16,32,2432]{2,1,0:T(8,128)(2,1)S(1)}, u32[]{:S(2)}, u32[]{:S(2)}) async-start(bf16[16,32,2432]{2,1,0:T(8,128)(2,1)} %copy-done), calls=%async_computation | async-start | bytes 4980736 | tf_op jit(solution)/shard_map/all_to_all | solution.py:297
  143.1 1.5 copy-start.6
  147.2 1.2 copy-start.1
  202.6 53.3 %all-to-all-start.2 = ((bf16[32,112,256]{2,1,0:T(8,128)(2,1)}), bf16[32,112,256]{2,1,0:T(8,128)(2,1)}, u32[]{:S(2)}, u32[]{:S(2)}) async-start(bf16[32,112,256]{2,1,0:T(8,128)(2,1)} %copy-done.1), calls=%async_computation.2 | async-start | bytes 3670016 | tf_op jit(solution)/shard_map/all_to_all | solution.py:322
  210.6 48.3 %collective-permute-start.15 = (bf16[16,32,2432]{2,1,0:T(8,128)(2,1)S(1)}, bf16[16,32,2432]{2,1,0:T(8,128)(2,1)}, u32[]{:S(2)}, u32[]{:S(2)}) collective-permute-start(bf16[16,32,2432]{2,1,0:T(8,128)(2,1)S(1)} %all-to-all-done.own_ref), channel_id=1, source_target_pairs={{0,8},{8,0},{1,9},{9,1},{2,10},{10,2},{3,11},{11,3},{4,12},{12,4},... | collective-permute-start | bytes 7471112 | tf_op jit(solution)/shard_map/ppermute | solution.py:301
  211.0 54.8 %collective-permute-start.31 = (bf16[16,32,1792]{2,1,0:T(8,128)(2,1)}, bf16[16,32,1792]{2,1,0:T(8,128)(2,1)}, u32[]{:S(2)}, u32[]{:S(2)}) collective-permute-start(bf16[16,32,1792]{2,1,0:T(8,128)(2,1)} %copy-done.2), channel_id=1, source_target_pairs={{0,8},{8,0},{1,9},{9,1},{2,10},{10,2},{3,11},{11,3},{4,12},{12,4},... | collective-permute-start | bytes 5505032 | tf_op jit(solution)/shard_map/ppermute | solution.py:301
  255.9 2.9 %copy-start.4 = (bf16[2,2,256,256]{3,2,1,0:T(8,128)(2,1)S(1)}, bf16[2,2,256,256]{3,2,1,0:T(8,128)(2,1)}, u32[]{:S(2)}) copy-start(bf16[2,2,256,256]{3,2,1,0:T(8,128)(2,1)} %constant.28.clone.matrix_ref) | copy-start | bytes 1572868
  258.8 6.9 %copy-start.3 = (bf16[16,32,1792]{2,1,0:T(8,128)(2,1)S(1)}, bf16[16,32,1792]{2,1,0:T(8,128)(2,1)}, u32[]{:S(2)}) copy-start(bf16[16,32,1792]{2,1,0:T(8,128)(2,1)} %copy-done.2) | copy-start | bytes 5505028

commit v2 on v1

v2 whole, which is shorter than its diff:
```python
import functools
import math

import jax
import jax.numpy as jnp
import numpy as np
from jax import lax
from jax.experimental import pallas as pl
from jax.experimental.pallas import tpu as pltpu
from jax.sharding import Mesh
from jax.sharding import PartitionSpec as P

BLK = 128
QPG = 8
FFB = 28
HALF_Q = QPG // 2
HALF_F = FFB // 2
ROWS = 32
PIECES = 16
DEEP = 8
Q_START = HALF_F * BLK
UP_START = Q_START + (HALF_Q + 1) * BLK
WIDTH = UP_START + HALF_F * BLK
VMEM_LIMIT = 16 * 1024 * 1024
VMEM_MOST = 56 * 1024 * 1024
PLANE = ("xh", "xl", "y")
DEPTH = ("xh", "z")
FSDP = ("xh", "z", "core")
TP = ("xl", "y")


def signs(order):
    index = np.arange(order)
    common = index[:, None] & index[None, :]
    parity = np.zeros((order, order), np.int64)
    while common.any():
        parity ^= common & 1
        common = common >> 1
    return (1 - 2 * parity).astype(np.float32)


def first_matrix():
    high = signs(PIECES)[:, [(s & 7) * 2 + (s >> 3) for s in range(PIECES)]]
    return np.kron(high, signs(ROWS)) / 16.0


def bf16(values):
    return values.astype(jnp.bfloat16)


def params(limit=VMEM_LIMIT):
    return pltpu.CompilerParams(vmem_limit_bytes=limit)


def cost(flops, moved):
    return pl.CostEstimate(flops=int(flops), bytes_accessed=int(moved), transcendentals=0)


def side_index():
    return lax.axis_index("xh") * 2 + lax.axis_index("core")


def whole(count):
    return [pl.BlockSpec(memory_space=pltpu.VMEM)] * count


def pair_sums(values, span):
    out = list(values)
    for i in range(len(values)):
        if not i & span:
            out[i] = values[i] + values[i | span]
            out[i | span] = values[i] - values[i | span]
    return out


def down_kernel(weight_ref, sign_ref, *refs):
    out_refs, held_ref = refs[:DEEP], refs[DEEP]
    sign = sign_ref[...]
    groups = weight_ref.shape[1] // BLK
    side, z = side_index(), lax.axis_index("z")

    @pl.loop(0, weight_ref.shape[0] // 16)
    def _(step):
        rows = pl.ds(pl.multiple_of(step * 16, 16), 16)
        tall = jnp.concatenate(
            [weight_ref[rows, a * BLK : (a + 1) * BLK] for a in range(groups)], axis=0
        )
        half = jnp.dot(tall, sign, preferred_element_type=jnp.float32)
        half = bf16(half * (1.0 / math.sqrt(BLK))).astype(jnp.float32)
        parts = [half[a * 16 : (a + 1) * 16] for a in range(groups)]
        span = 1
        while span < groups:
            parts = pair_sums(parts, span)
            span *= 2
        for a in range(groups):
            held_ref[a] = bf16(parts[a] * (1.0 / math.sqrt(groups)))
        for s in range(DEEP):
            for r in range(4):
                there = side ^ r
                shard = (there >> 1) * 2 * DEEP + ((z + s) & (DEEP - 1)) * 2 + (there & 1)
                for a in range(2):
                    out_refs[s][r, rows, a * BLK : (a + 1) * BLK] = held_ref[shard * 2 + a]


def rotate_down(weight, shards):
    rows, width = weight.shape
    groups = width // BLK
    return pl.pallas_call(
        down_kernel,
        out_shape=[jax.ShapeDtypeStruct((4, rows, width // shards), jnp.bfloat16)] * DEEP,
        in_specs=whole(2),
        out_specs=whole(DEEP),
        scratch_shapes=[pltpu.VMEM((groups, 16, BLK), jnp.bfloat16)],
        compiler_params=params(),
        cost_estimate=cost(2 * rows * width * BLK * 4, 4 * rows * width),
        name="down_rotate",
    )(weight, jnp.asarray(signs(BLK), jnp.bfloat16))


def repack_kernel(*refs):
    in_refs, out_refs = refs[:DEEP], refs[DEEP:]
    for r in range(4):
        for s in range(DEEP):
            out_refs[r][s] = in_refs[s][r]


def repack(pieces):
    _, rows, width = pieces[0].shape
    return pl.pallas_call(
        repack_kernel,
        out_shape=[jax.ShapeDtypeStruct((DEEP, rows, width), jnp.bfloat16)] * 4,
        in_specs=whole(DEEP),
        out_specs=whole(4),
        compiler_params=params(),
        cost_estimate=cost(4 * DEEP * rows * width, 16 * DEEP * rows * width),
        name="repack_down",
    )(*pieces)


def spread(gain_ref):
    row = lax.broadcasted_iota(jnp.int32, (ROWS, BLK), 0)
    spread_gain = jnp.zeros((ROWS, BLK), jnp.float32)
    for i in range(ROWS):
        spread_gain = jnp.where(row == i, gain_ref[i], spread_gain)
    return spread_gain


def scaled(ref, block, gain):
    columns = pl.ds(pl.multiple_of(block * BLK, BLK), BLK)
    return bf16(ref[:, columns].astype(jnp.float32) * gain)


def pick_kernel(
    heads_ref, order_ref, attn_ref, ffn_ref, q_ref, k_ref, v_ref, gate_ref, up_ref, out_ref
):
    ffn_gain, attn_gain = spread(ffn_ref), spread(attn_ref)
    each = out_ref.shape[0]
    for j in range(each):
        piece = pl.program_id(0) * each + j
        owner, half = piece & 7, piece >> 3
        for slot in range(HALF_F):
            block = owner * FFB + order_ref[owner, half * HALF_F + slot]
            for ref, start in ((gate_ref, 0), (up_ref, UP_START)):
                columns = slice(start + slot * BLK, start + (slot + 1) * BLK)
                out_ref[j, :, columns] = scaled(ref, block, ffn_gain)
        for slot in range(HALF_Q):
            head = owner * QPG + heads_ref[owner, half * HALF_Q + slot]
            columns = slice(Q_START + slot * BLK, Q_START + (slot + 1) * BLK)
            out_ref[j, :, columns] = scaled(q_ref, head, attn_gain)
        out_ref[j, :, UP_START - BLK : UP_START] = jnp.where(
            half == 1, scaled(v_ref, owner, attn_gain), scaled(k_ref, owner, attn_gain)
        )


def pick(head_order, ffn_order, gains, arrays):
    each = 4
    return pl.pallas_call(
        pick_kernel,
        grid=(PIECES // each,),
        out_shape=jax.ShapeDtypeStruct((PIECES, ROWS, WIDTH), jnp.bfloat16),
        in_specs=[pl.BlockSpec(memory_space=pltpu.SMEM)] * 4
        + [pl.BlockSpec(array.shape, lambda i: (0, 0)) for array in arrays],
        out_specs=pl.BlockSpec((each, ROWS, WIDTH), lambda i: (i, 0, 0)),
        compiler_params=params(VMEM_MOST),
        cost_estimate=cost(PIECES * ROWS * WIDTH * 400, 4 * PIECES * ROWS * WIDTH),
        name="pick_columns",
    )(head_order, ffn_order, *gains, *arrays)


def first_kernel(begin, matrix_ref, in_ref, out_ref):
    width = out_ref.shape[2]
    matrix = matrix_ref[...]
    for start in range(0, width, 2 * BLK):
        stop = min(start + 2 * BLK, width)
        tall = in_ref[:, :, begin + start : begin + stop].reshape(PIECES * ROWS, -1)
        mixed = jnp.dot(matrix, tall, preferred_element_type=jnp.float32)
        out_ref[:, :, start:stop] = bf16(mixed).reshape(-1, ROWS, stop - start)


def first_mix(pieces, begin, width):
    rows = PIECES * ROWS
    return pl.pallas_call(
        functools.partial(first_kernel, begin),
        grid=(2,),
        out_shape=jax.ShapeDtypeStruct((PIECES, ROWS, width), jnp.bfloat16),
        in_specs=[pl.BlockSpec((rows // 2, rows), lambda i: (i, 0))] + whole(1),
        out_specs=pl.BlockSpec((PIECES // 2, ROWS, width), lambda i: (i, 0, 0)),
        compiler_params=params(),
        cost_estimate=cost(2 * rows * rows * width, 4 * rows * width),
        name="first_mix",
    )(jnp.asarray(first_matrix(), jnp.bfloat16), pieces)


def last_columns(sign, own_ref, other_ref, part, columns):
    sides = []
    for ref in (own_ref, other_ref):
        rows = [ref[part * 8 + j, :, columns].astype(jnp.float32) for j in range(8)]
        rows = [rows[j] + sign * rows[j + 4] for j in range(4)]
        sides.append(pair_sums(pair_sums(rows, 2), 1))
    scale = 16.0 / math.sqrt(8192.0)
    parts = []
    for mine, theirs in zip(*sides):
        parts.append(bf16((mine + theirs) * scale))
        parts.append(bf16((mine - theirs) * (scale * sign)))
    return jnp.concatenate(parts, axis=0)


def last_kernel(with_heads, own_ref, other_ref, *refs):
    out_ref = refs[-1 - with_heads]
    part = pl.program_id(0)
    sign = (1 - 2 * lax.axis_index("core")).astype(jnp.float32)

    @pl.loop(0, HALF_F // 2)
    def _(step):
        columns = pl.ds(pl.multiple_of(step * 2 * BLK, 2 * BLK), 2 * BLK)
        out_ref[:, columns] = last_columns(sign, own_ref, other_ref, part, columns)

    if with_heads:
        heads_ref = refs[-1]
        start = HALF_F * BLK

        @pl.loop(0, HALF_Q + 1)
        def _(slot):
            columns = pl.ds(pl.multiple_of(start + slot * BLK, BLK), BLK)
            block = jnp.where(slot < HALF_Q, part * HALF_Q + slot, QPG + part)
            heads_ref[:, pl.ds(pl.multiple_of(block * BLK, BLK), BLK)] = last_columns(
                sign, own_ref, other_ref, part, columns
            )


def last_mix(own, other, offset, with_heads, target=None):
    width = own.shape[2]
    rows = 8 * ROWS
    outs = [jax.ShapeDtypeStruct((rows, 2 * FFB * BLK), jnp.bfloat16)]
    out_specs = [pl.BlockSpec((rows, HALF_F * BLK), lambda c: (0, offset + c))]
    if with_heads:
        outs.append(jax.ShapeDtypeStruct((rows, (QPG + 2) * BLK), jnp.bfloat16))
        out_specs.append(pl.BlockSpec((rows, (QPG + 2) * BLK), lambda c: (0, 0)))
    in_specs = whole(2)
    args = [own, other]
    aliases = {}
    if target is not None:
        in_specs.append(pl.BlockSpec(memory_space=pl.ANY))
        args.append(target)
        aliases = {2: 0}
    return pl.pallas_call(
        functools.partial(last_kernel, with_heads),
        grid=(2,),
        out_shape=outs,
        in_specs=in_specs,
        out_specs=out_specs,
        input_output_aliases=aliases,
        compiler_params=params(),
        cost_estimate=cost(40 * rows * width, 12 * rows * width),
        name="last_mix",
    )(*args)


def order_kernel(order_ref, *refs):
    in_refs, (out_ref, slot_ref) = refs[:4], refs[4:]
    owner = lax.axis_index("xl") * 4 + lax.axis_index("y")
    side, z = side_index(), lax.axis_index("z")
    for slot in range(FFB):
        slot_ref[order_ref[owner, slot]] = slot
    groups = in_refs[0].shape[1] // 16
    for r in range(4):
        there = side ^ r
        for s in range(DEEP):
            shard = (there >> 1) * 2 * DEEP + ((z - s) & (DEEP - 1)) * 2 + (there & 1)
            for group in range(groups):
                at = shard * groups + group
                row = slot_ref[at >> 3] * BLK + (at & 7) * 16
                out_ref[pl.ds(pl.multiple_of(row, 16), 16), :] = in_refs[r][
                    s, group * 16 : (group + 1) * 16, :
                ]


def order_rows(ffn_order, pieces):
    count, rows, width = pieces[0].shape
    return pl.pallas_call(
        order_kernel,
        out_shape=jax.ShapeDtypeStruct((4 * count * rows, width), jnp.bfloat16),
        in_specs=[pl.BlockSpec(memory_space=pltpu.SMEM)] + whole(4),
        out_specs=whole(1)[0],
        scratch_shapes=[pltpu.SMEM((FFB,), jnp.int32)],
        compiler_params=params(),
        cost_estimate=cost(4 * count * rows * width, 16 * count * rows * width),
        name="order_rows",
    )(ffn_order, *pieces)


def exchange(pieces, axes):
    return lax.all_to_all(pieces, axes, split_axis=0, concat_axis=0, tiled=True)


def exchange_z(pieces):
    got = list(pieces)
    for s in (4, 1, 7, 2, 6, 3, 5):
        got[s] = lax.ppermute(pieces[s], "z", [(i, (i + s) % DEEP) for i in range(DEEP)])
    return got


def exchange_side(pieces):
    got = list(pieces)
    for r in (1, 2, 3):
        got[r] = lax.ppermute(pieces[r], ("xh", "core"), [(i, i ^ r) for i in range(4)])
    return got


def exchange_core(got):
    return lax.ppermute(got, "core", [(0, 1), (1, 0)])


def tie(*arrays):
    return lax.optimization_barrier(arrays)


def per_device(
    q_weight,
    k_weight,
    v_weight,
    gate_weight,
    up_weight,
    down_weight,
    attn_gain,
    ffn_gain,
    head_order,
    ffn_order,
):
    shards = math.prod(lax.axis_size(name) for name in FSDP)
    columns = pick(
        head_order,
        ffn_order,
        [attn_gain, ffn_gain],
        [q_weight, k_weight, v_weight, gate_weight, up_weight],
    )
    columns = exchange(columns, PLANE)
    shifted = exchange_z(rotate_down(down_weight, shards))
    first = first_mix(columns, 0, UP_START)
    first, *packed = tie(first, *repack(shifted))
    first = exchange(first, DEPTH)
    second = first_mix(columns, UP_START, WIDTH - UP_START)
    moved = exchange_side(packed)
    second, first, *moved = tie(second, first, *moved)
    second = exchange(second, DEPTH)
    merged_ffn, merged_attn = last_mix(first, exchange_core(first), 0, True)
    merged_down = order_rows(ffn_order, moved)
    second, merged_ffn, merged_attn, merged_down = tie(second, merged_ffn, merged_attn, merged_down)
    (merged_ffn,) = last_mix(second, exchange_core(second), 2, False, merged_ffn)
    return (merged_attn, merged_ffn, merged_down)


def solution(mesh):
    split = Mesh(mesh.devices.reshape(2, 8, 2, 2, 4), ("xh", "z", "core", "xl", "y"))
    rows = TP + FSDP
    placed = (P(rows, None),) * 6 + (P(rows),) * 2 + (P(), P())
    return jax.shard_map(
        per_device,
        mesh=split,
        in_specs=placed,
        out_specs=(P(FSDP, TP), P(FSDP, TP), P(TP, FSDP)),
        check_vma=False,
    )
```

time: 274 us -> 215 us (0.78)
  waiting for transfers between devices: 144 us -> 115 us
  starting transfers between devices: 81.5 us -> 65 us
  Pallas kernels: 34 us -> 24.7 us
    all_to_all x3, waiting for transfers between devices: 99 us -> 46.9 us  [exchange(): return lax.all_to_all(pieces, axes, split_axis=0, concat_axis=0, tiled=True)]
    ppermute x30 -> x10, starting transfers between devices: 54.3 us -> 26.3 us  [the longest x7 20.5 us: exchange_z(): lax.ppermute(pieces[s], 'z', [(i, (i + s) % DEEP) for i in range(DEEP)])]
    ppermute x30 -> x10, waiting for transfers between devices: 45.5 us -> 64.5 us  [the longest x3 35.1 us: exchange_side(): lax.ppermute(pieces[r], ('xh', 'core'), [(i, i ^ r) for i in range(4)])]
    pallas_call x8, Pallas kernels: 34 us -> 24.7 us  [the longest x2 7.47 us: first_mix(): pl.pallas_call(functools.partial(first_kernel, begin), grid=(2,), out_sha...]
    all_to_all x3, starting transfers between devices: 26.7 us -> 34.2 us  [exchange(): return lax.all_to_all(pieces, axes, split_axis=0, concat_axis=0, tiled=True)]
    ppermute x2, starting transfers between devices: 0.6 us -> 4.54 us  [exchange_core(): return lax.ppermute(got, 'core', [(0, 1), (1, 0)])]
    ppermute x2, waiting for transfers between devices: 0.01 us -> 3.62 us  [exchange_core(): return lax.ppermute(got, 'core', [(0, 1), (1, 0)])]
    unnamed x34 -> x30, local copies, waits for them, and re-layouts: 9.86 us -> 9.38 us
  transfers between devices with their start and end apart: 35 -> 15, of which waited for: 18 -> 11; matrix products, arithmetic and copies ran while one was open for 0% -> 0% of each run, Pallas kernels for 8% -> 6%
where the time goes in v2:
time: 215 us
  waiting for transfers between devices  115 us (53%)
  starting transfers between devices  65 us (30%)
  Pallas kernels  24.7 us (11%)
  local copies, waits for them, and re-layouts  9.38 us (4%)
    all_to_all x3, waiting for transfers between devices, exchange(): return lax.all_to_all(pieces, axes, split_axis=0, concat_axis=0, tiled=True)  46.9 us
    ppermute x3, waiting for transfers between devices, exchange_side(): lax.ppermute(pieces[r], ('xh', 'core'), [(i, i ^ r) for i in range(4)])  35.1 us
    all_to_all x3, starting transfers between devices, exchange(): return lax.all_to_all(pieces, axes, split_axis=0, concat_axis=0, tiled=True)  34.2 us
    ppermute x7, waiting for transfers between devices, exchange_z(): lax.ppermute(pieces[s], 'z', [(i, (i + s) % DEEP) for i in range(DEEP)])  29.3 us
    ppermute x7, starting transfers between devices, exchange_z(): lax.ppermute(pieces[s], 'z', [(i, (i + s) % DEEP) for i in range(DEEP)])  20.5 us
    unnamed x30, local copies, waits for them, and re-layouts  9.38 us
    pallas_call x2, Pallas kernels, first_mix(): pl.pallas_call(functools.partial(first_kernel, begin), grid=(2,), out_sha...  7.47 us
    pallas_call x2, Pallas kernels, last_mix(): pl.pallas_call(functools.partial(last_kernel, with_heads), grid=(2,), out...  6.26 us
  transfers between devices with their start and end apart: 15, of which 11 were waited for; matrix products, arithmetic and copies ran while one was open for 0% of the time, Pallas kernels for 6%

profile of v2, /device:TPU:25, one launch (start us, length us, event | category | flops | bytes accessed | tf_op | source)
XLA Modules:
  0.0 214.7 jit_solution(10136742003187952385)
XLA Ops:
  0.6 5.3 %pick_columns.1 = bf16[16,32,4224]{2,1,0:T(8,128)(2,1)} custom-call(s32[8,8]{1,0:T(8,128)} %heads_ref.1, s32[8,28]{1,0:T(8,128)} %order_ref.3, f32[32]{0:T(128)} %attn_ref.1, f32[32]{0:T(128)} %ffn_ref.1, bf16[32,8192]{1,0:T(8,128)(2,1)} %q_ref.1, bf16[32,1024]{1,0:T(8,128)(2,1)} %k_ref.1, bf16[32,1024]{1,0:T(8,128)(2,1)} %v_ref.1, ...), custom_call_target="tpu_custom_call" | custom-call | flops 865075200 | bytes 8650752 | tf_op jit(solution)/shard_map/pick_columns/pallas_call | solution.py:177
  6.0 0.0 copy-start.10
  6.0 6.7 %all-to-all-start = ((bf16[16,32,4224]{2,1,0:T(8,128)(2,1)}), bf16[16,32,4224]{2,1,0:T(8,128)(2,1)}, u32[]{:S(2)}, u32[]{:S(2)}) async-start(bf16[16,32,4224]{2,1,0:T(8,128)(2,1)} %pick_columns.1), calls=%async_computation | async-start | bytes 8650752 | tf_op jit(solution)/shard_map/all_to_all | solution.py:313
  12.7 0.0 copy-done.10
  12.7 0.0 copy-done.14
  12.7 0.0 copy-start.2
  12.7 2.9 %down_rotate.1 = (bf16[4,112,256]{2,1,0:T(8,128)(2,1)S(1)}, bf16[4,112,256]{2,1,0:T(8,128)(2,1)S(1)}, bf16[4,112,256]{2,1,0:T(8,128)(2,1)S(1)}, bf16[4,112,256]{...) custom-call(bf16[112,8192]{1,0:T(8,128)(2,1)S(1)} %copy-done.10, ...), custom_call_target="tpu_custom_call" | custom-call | flops 939524096 | bytes 3670016 | tf_op jit(solution)/shard_map/down_rotate/pallas_call | solution.py:108
  15.6 1.7 collective-permute-start
  17.3 3.0 %collective-permute-start.1 = (bf16[4,112,256]{2,1,0:T(8,128)(2,1)S(1)}, bf16[4,112,256]{2,1,0:T(8,128)(2,1)S(1)}, u32[]{:S(2)}, u32[]{:S(2)}) collective-permute-start(bf16[4,112,256]{2,1,0:T(8,128)(2,1)S(1)} %get-tuple-element.34), channel_id=1, source_target_pairs={{0,32},{16,48},{32,64},{48,80},{64,96},{80,112},{96,0},{112,16},{1... | collective-permute-start | bytes 688136 | tf_op jit(solution)/shard_map/ppermute | solution.py:319
  20.3 3.8 %collective-permute-start.2 = (bf16[4,112,256]{2,1,0:T(8,128)(2,1)S(1)}, bf16[4,112,256]{2,1,0:T(8,128)(2,1)S(1)}, u32[]{:S(2)}, u32[]{:S(2)}) collective-permute-start(bf16[4,112,256]{2,1,0:T(8,128)(2,1)S(1)} %get-tuple-element.35), channel_id=1, source_target_pairs={{0,48},{16,64},{32,80},{48,96},{64,112},{80,0},{96,16},{112,32},{1... | collective-permute-start | bytes 688136 | tf_op jit(solution)/shard_map/ppermute | solution.py:319
  24.1 0.5 collective-permute-start.3
  24.5 4.5 %collective-permute-start.4 = (bf16[4,112,256]{2,1,0:T(8,128)(2,1)S(1)}, bf16[4,112,256]{2,1,0:T(8,128)(2,1)S(1)}, u32[]{:S(2)}, u32[]{:S(2)}) collective-permute-start(bf16[4,112,256]{2,1,0:T(8,128)(2,1)S(1)} %get-tuple-element.37), channel_id=1, source_target_pairs={{0,80},{16,96},{32,112},{48,0},{64,16},{80,32},{96,48},{112,64},{1... | collective-permute-start | bytes 688136 | tf_op jit(solution)/shard_map/ppermute | solution.py:319
  29.0 0.0 collective-permute-done.refs_1_
  29.0 2.4 %collective-permute-start.5 = (bf16[4,112,256]{2,1,0:T(8,128)(2,1)S(1)}, bf16[4,112,256]{2,1,0:T(8,128)(2,1)S(1)}, u32[]{:S(2)}, u32[]{:S(2)}) collective-permute-start(bf16[4,112,256]{2,1,0:T(8,128)(2,1)S(1)} %get-tuple-element.38), channel_id=1, source_target_pairs={{0,96},{16,112},{32,0},{48,16},{64,32},{80,48},{96,64},{112,80},{1... | collective-permute-start | bytes 688136 | tf_op jit(solution)/shard_map/ppermute | solution.py:319
  31.4 2.0 collective-permute-done.1.refs_2_
  33.3 4.8 %collective-permute-start.6 = (bf16[4,112,256]{2,1,0:T(8,128)(2,1)S(1)}, bf16[4,112,256]{2,1,0:T(8,128)(2,1)S(1)}, u32[]{:S(2)}, u32[]{:S(2)}) collective-permute-start(bf16[4,112,256]{2,1,0:T(8,128)(2,1)S(1)} %get-tuple-element.39), channel_id=1, source_target_pairs={{0,112},{16,0},{32,16},{48,32},{64,48},{80,64},{96,80},{112,96},{1... | collective-permute-start | bytes 688136 | tf_op jit(solution)/shard_map/ppermute | solution.py:319
  38.1 10.6 %collective-permute-done.2.refs_3_ = bf16[4,112,256]{2,1,0:T(8,128)(2,1)S(1)} collective-permute-done((bf16[4,112,256]{2,1,0:T(8,128)(2,1)S(1)}, bf16[4,112,256]{2,1,0:T(8,128)(2,1)S(1)}, u32[]{:S(2)}, u32[]{:S(2)}) %collective-permute-start.2) | collective-permute-done | bytes 229408 | tf_op jit(solution)/shard_map/ppermute | solution.py:319
  48.7 6.5 %collective-permute-done.3.refs_4_ = bf16[4,112,256]{2,1,0:T(8,128)(2,1)S(1)} collective-permute-done((bf16[4,112,256]{2,1,0:T(8,128)(2,1)S(1)}, bf16[4,112,256]{2,1,0:T(8,128)(2,1)S(1)}, u32[]{:S(2)}, u32[]{:S(2)}) %collective-permute-start.3) | collective-permute-done | bytes 229408 | tf_op jit(solution)/shard_map/ppermute | solution.py:319
  55.2 0.0 collective-permute-done.4.refs_5_
  55.2 8.4 %collective-permute-done.5.refs_6_ = bf16[4,112,256]{2,1,0:T(8,128)(2,1)S(1)} collective-permute-done((bf16[4,112,256]{2,1,0:T(8,128)(2,1)S(1)}, bf16[4,112,256]{2,1,0:T(8,128)(2,1)S(1)}, u32[]{:S(2)}, u32[]{:S(2)}) %collective-permute-start.5) | collective-permute-done | bytes 229408 | tf_op jit(solution)/shard_map/ppermute | solution.py:319
  63.6 1.9 collective-permute-done.6.refs_7_
  65.5 0.1 repack_down.1
  65.6 0.0 copy-start.11
  65.6 0.8 copy-done.11
  66.4 0.0 copy-start.12
  66.4 0.8 copy-done.12
  67.2 0.0 copy-start.13
  67.2 0.8 copy-done.13
  67.9 1.9 all-to-all-done.in_ref
  69.8 0.0 copy-done.2
  69.8 3.9 %first_mix.3 = bf16[16,32,2432]{2,1,0:T(8,128)(2,1)S(1)} custom-call(bf16[512,512]{1,0:T(8,128)(2,1)S(1)} %copy-done.2, bf16[16,32,4224]{2,1,0:T(8,128)(2,1)} %all-to-all-done.in_ref), custom_call_target="tpu_custom_call" | custom-call | flops 1275068416 | bytes 4980736 | tf_op jit(solution)/shard_map/first_mix/pallas_call | solution.py:202
  73.8 0.0 copy-start
  73.8 1.4 copy-done
  75.2 21.4 %all-to-all-start.1 = ((bf16[16,32,2432]{2,1,0:T(8,128)(2,1)}), bf16[16,32,2432]{2,1,0:T(8,128)(2,1)S(1)}, u32[]{:S(2)}, u32[]{:S(2)}) async-start(bf16[16,32,2432]{2,1,0:T(8,128)(2,1)} %copy-done), calls=%async_computation.1 | async-start | bytes 4980736 | tf_op jit(solution)/shard_map/all_to_all | solution.py:313
  96.7 2.5 %collective-permute-start.7 = (bf16[8,112,256]{2,1,0:T(8,128)(2,1)}, bf16[8,112,256]{2,1,0:T(8,128)(2,1)S(1)}, u32[]{:S(2)}, u32[]{:S(2)}) collective-permute-start(bf16[8,112,256]{2,1,0:T(8,128)(2,1)} %copy-done.13), channel_id=1, source_target_pairs={{0,8},{8,0},{128,136},{136,128},{1,9},{9,1},{129,137},{137,129},{2... | collective-permute-start | bytes 1376264 | tf_op jit(solution)/shard_map/ppermute | solution.py:326
  99.2 3.1 %collective-permute-start.8 = (bf16[8,112,256]{2,1,0:T(8,128)(2,1)}, bf16[8,112,256]{2,1,0:T(8,128)(2,1)S(1)}, u32[]{:S(2)}, u32[]{:S(2)}) collective-permute-start(bf16[8,112,256]{2,1,0:T(8,128)(2,1)} %copy-done.12), channel_id=1, source_target_pairs={{0,128},{8,136},{128,0},{136,8},{1,129},{9,137},{129,1},{137,9},{2... | collective-permute-start | bytes 1376264 | tf_op jit(solution)/shard_map/ppermute | solution.py:326
  102.3 0.2 collective-permute-start.9
  102.4 3.5 %first_mix.2 = bf16[16,32,1792]{2,1,0:T(8,128)(2,1)S(1)} custom-call(bf16[512,512]{1,0:T(8,128)(2,1)S(1)} %copy-done.2, bf16[16,32,4224]{2,1,0:T(8,128)(2,1)} %all-to-all-done.in_ref), custom_call_target="tpu_custom_call" | custom-call | flops 939524096 | bytes 3670016 | tf_op jit(solution)/shard_map/first_mix/pallas_call | solution.py:202
  106.0 0.0 copy-start.1
  106.0 1.2 copy-done.1
  107.2 0.0 copy-start.9
  107.2 0.0 collective-permute-done.7.refs_1_
  107.2 0.0 copy-start.3
  107.2 0.8 copy-done.3
  108.0 12.6 %collective-permute-done.8.refs_2_ = bf16[8,112,256]{2,1,0:T(8,128)(2,1)S(1)} collective-permute-done((bf16[8,112,256]{2,1,0:T(8,128)(2,1)}, bf16[8,112,256]{2,1,0:T(8,128)(2,1)S(1)}, u32[]{:S(2)}, u32[]{:S(2)}) %collective-permute-start.8) | collective-permute-done | bytes 458784 | tf_op jit(solution)/shard_map/ppermute | solution.py:326
  120.5 0.0 copy-start.5
  120.5 0.8 copy-done.5
  121.3 0.0 copy-start.4
  121.3 22.6 %collective-permute-done.9.refs_3_ = bf16[8,112,256]{2,1,0:T(8,128)(2,1)S(1)} collective-permute-done((bf16[8,112,256]{2,1,0:T(8,128)(2,1)}, bf16[8,112,256]{2,1,0:T(8,128)(2,1)S(1)}, u32[]{:S(2)}, u32[]{:S(2)}) %collective-permute-start.9) | collective-permute-done | bytes 458784 | tf_op jit(solution)/shard_map/ppermute | solution.py:326
  143.9 0.8 copy-done.7
  144.6 10.7 %all-to-all-done.1.own_ref = bf16[16,32,2432]{2,1,0:T(8,128)(2,1)S(1)} async-done(((bf16[16,32,2432]{2,1,0:T(8,128)(2,1)}), bf16[16,32,2432]{2,1,0:T(8,128)(2,1)S(1)}, u32[]{:S(2)}, u32[]{:S(2)}) %all-to-all-start.1) | async-done | bytes 2490400 | tf_op jit(solution)/shard_map/all_to_all | solution.py:313
  155.4 6.0 %all-to-all-start.2 = ((bf16[16,32,1792]{2,1,0:T(8,128)(2,1)}), bf16[16,32,1792]{2,1,0:T(8,128)(2,1)}, u32[]{:S(2)}, u32[]{:S(2)}) async-start(bf16[16,32,1792]{2,1,0:T(8,128)(2,1)} %copy-done.1), calls=%async_computation.2 | async-start | bytes 3670016 | tf_op jit(solution)/shard_map/all_to_all | solution.py:313
  161.4 1.4 collective-permute-start.10
  162.7 0.0 copy-done.9
  162.7 0.0 copy-done.4
  162.8 1.0 copy-done.6
  163.8 1.0 copy-done.8
  164.8 2.6 %order_rows.1 = bf16[3584,256]{1,0:T(8,128)(2,1)} custom-call(s32[8,28]{1,0:T(8,128)S(1)} %copy-done.9, bf16[8,112,256]{2,1,0:T(8,128)(2,1)S(1)} %get-tuple-element.53.refs_0_, bf16[8,112,256]{2,1,0:T(8,128)(2,1)S(1)} %copy-done.4, bf16[8,112,256]{2,1,0:T(8,128)(2,1)S(1)} %copy-done.6, bf16[8,112,256]{2,1,0:T(8,128)(2,1)S(1)} %copy-done.8), custom_call_target="tpu_custom_call" | custom-call | flops 917504 | bytes 3670016 | tf_op jit(solution)/shard_map/order_rows/pallas_call | solution.py:300
  167.4 0.0 collective-permute-done.10.other_ref
  167.4 2.7 %last_mix.2 = (bf16[256,7168]{1,0:T(8,128)(2,1)}, bf16[256,1280]{1,0:T(8,128)(2,1)}) custom-call(bf16[16,32,2432]{2,1,0:T(8,128)(2,1)S(1)} %all-to-all-done.1.own_ref, bf16[16,32,2432]{2,1,0:T(8,128)(2,1)S(1)} %collective-permute-done.10.other_ref), custom_call_target="tpu_custom_call" | custom-call | flops 24903680 | bytes 7471104 | tf_op jit(solution)/shard_map/last_mix/pallas_call | solution.py:266
  170.1 34.3 %all-to-all-done.2.own_ref = bf16[16,32,1792]{2,1,0:T(8,128)(2,1)} async-done(((bf16[16,32,1792]{2,1,0:T(8,128)(2,1)}), bf16[16,32,1792]{2,1,0:T(8,128)(2,1)}, u32[]{:S(2)}, u32[]{:S(2)}) %all-to-all-start.2) | async-done | bytes 1835040 | tf_op jit(solution)/shard_map/all_to_all | solution.py:313
  204.4 3.2 %collective-permute-start.11 = (bf16[16,32,1792]{2,1,0:T(8,128)(2,1)}, bf16[16,32,1792]{2,1,0:T(8,128)(2,1)S(1)}, u32[]{:S(2)}, u32[]{:S(2)}) collective-permute-start(bf16[16,32,1792]{2,1,0:T(8,128)(2,1)} %all-to-all-done.2.own_ref), channel_id=1, source_target_pairs={{0,8},{8,0},{1,9},{9,1},{2,10},{10,2},{3,11},{11,3},{4,12},{12,4},... | collective-permute-start | bytes 5505032 | tf_op jit(solution)/shard_map/ppermute | solution.py:331
  207.6 3.6 %collective-permute-done.11.other_ref = bf16[16,32,1792]{2,1,0:T(8,128)(2,1)S(1)} collective-permute-done((bf16[16,32,1792]{2,1,0:T(8,128)(2,1)}, bf16[16,32,1792]{2,1,0:T(8,128)(2,1)S(1)}, u32[]{:S(2)}, u32[]{:S(2)}) %collective-permute-start.11) | collective-permute-done | bytes 1835040 | tf_op jit(solution)/shard_map/ppermute | solution.py:331
  211.2 3.6 %last_mix.3 = bf16[256,7168]{1,0:T(8,128)(2,1)} custom-call(bf16[16,32,1792]{2,1,0:T(8,128)(2,1)} %all-to-all-done.2.own_ref, bf16[16,32,1792]{2,1,0:T(8,128)(2,1)S(1)} %collective-permute-done.11.other_ref, bf16[256,7168]{1,0:T(8,128)(2,1)} %get-tuple-element.59.refs_0_), custom_call_target="tpu_custom_call", output_to_operand_aliasing={{}: (2, {})} | custom-call | flops 18350080 | bytes 5505024 | tf_op jit(solution)/shard_map/last_mix/pallas_call | solution.py:266
  (4 shorter events, 0.0 us)
Async XLA Ops:
  6.0 6.8 %copy-start.10 = (bf16[112,8192]{1,0:T(8,128)(2,1)S(1)}, bf16[112,8192]{1,0:T(8,128)(2,1)}, u32[]{:S(2)}) copy-start(bf16[112,8192]{1,0:T(8,128)(2,1)} %weight_ref.1) | copy-start | bytes 5505028
  6.0 6.8 %copy-start.14 = (bf16[128,128]{1,0:T(8,128)(2,1)S(1)}, bf16[128,128]{1,0:T(8,128)(2,1)}, u32[]{:S(2)}) copy-start(bf16[128,128]{1,0:T(8,128)(2,1)} %constant.4.clone.sign_ref) | copy-start | bytes 98308
  6.0 63.9 %all-to-all-start = ((bf16[16,32,4224]{2,1,0:T(8,128)(2,1)}), bf16[16,32,4224]{2,1,0:T(8,128)(2,1)}, u32[]{:S(2)}, u32[]{:S(2)}) async-start(bf16[16,32,4224]{2,1,0:T(8,128)(2,1)} %pick_columns.1), calls=%async_computation | async-start | bytes 8650752 | tf_op jit(solution)/shard_map/all_to_all | solution.py:313
  12.7 57.1 %copy-start.2 = (bf16[512,512]{1,0:T(8,128)(2,1)S(1)}, bf16[512,512]{1,0:T(8,128)(2,1)}, u32[]{:S(2)}) copy-start(bf16[512,512]{1,0:T(8,128)(2,1)} %constant.5.clone.matrix_ref) | copy-start | bytes 1572868
  15.6 13.4 %collective-permute-start = (bf16[4,112,256]{2,1,0:T(8,128)(2,1)S(1)}, bf16[4,112,256]{2,1,0:T(8,128)(2,1)S(1)}, u32[]{:S(2)}, u32[]{:S(2)}) collective-permute-start(bf16[4,112,256]{2,1,0:T(8,128)(2,1)S(1)} %get-tuple-element.33), channel_id=1, source_target_pairs={{0,16},{16,32},{32,48},{48,64},{64,80},{80,96},{96,112},{112,0},{1... | collective-permute-start | bytes 688136 | tf_op jit(solution)/shard_map/ppermute | solution.py:319
  17.3 16.0 %collective-permute-start.1 = (bf16[4,112,256]{2,1,0:T(8,128)(2,1)S(1)}, bf16[4,112,256]{2,1,0:T(8,128)(2,1)S(1)}, u32[]{:S(2)}, u32[]{:S(2)}) collective-permute-start(bf16[4,112,256]{2,1,0:T(8,128)(2,1)S(1)} %get-tuple-element.34), channel_id=1, source_target_pairs={{0,32},{16,48},{32,64},{48,80},{64,96},{80,112},{96,0},{112,16},{1... | collective-permute-start | bytes 688136 | tf_op jit(solution)/shard_map/ppermute | solution.py:319
  20.3 28.4 %collective-permute-start.2 = (bf16[4,112,256]{2,1,0:T(8,128)(2,1)S(1)}, bf16[4,112,256]{2,1,0:T(8,128)(2,1)S(1)}, u32[]{:S(2)}, u32[]{:S(2)}) collective-permute-start(bf16[4,112,256]{2,1,0:T(8,128)(2,1)S(1)} %get-tuple-element.35), channel_id=1, source_target_pairs={{0,48},{16,64},{32,80},{48,96},{64,112},{80,0},{96,16},{112,32},{1... | collective-permute-start | bytes 688136 | tf_op jit(solution)/shard_map/ppermute | solution.py:319
  24.1 31.1 %collective-permute-start.3 = (bf16[4,112,256]{2,1,0:T(8,128)(2,1)S(1)}, bf16[4,112,256]{2,1,0:T(8,128)(2,1)S(1)}, u32[]{:S(2)}, u32[]{:S(2)}) collective-permute-start(bf16[4,112,256]{2,1,0:T(8,128)(2,1)S(1)} %get-tuple-element.36), channel_id=1, source_target_pairs={{0,64},{16,80},{32,96},{48,112},{64,0},{80,16},{96,32},{112,48},{1... | collective-permute-start | bytes 688136 | tf_op jit(solution)/shard_map/ppermute | solution.py:319
  24.5 30.6 %collective-permute-start.4 = (bf16[4,112,256]{2,1,0:T(8,128)(2,1)S(1)}, bf16[4,112,256]{2,1,0:T(8,128)(2,1)S(1)}, u32[]{:S(2)}, u32[]{:S(2)}) collective-permute-start(bf16[4,112,256]{2,1,0:T(8,128)(2,1)S(1)} %get-tuple-element.37), channel_id=1, source_target_pairs={{0,80},{16,96},{32,112},{48,0},{64,16},{80,32},{96,48},{112,64},{1... | collective-permute-start | bytes 688136 | tf_op jit(solution)/shard_map/ppermute | solution.py:319
  29.0 34.6 %collective-permute-start.5 = (bf16[4,112,256]{2,1,0:T(8,128)(2,1)S(1)}, bf16[4,112,256]{2,1,0:T(8,128)(2,1)S(1)}, u32[]{:S(2)}, u32[]{:S(2)}) collective-permute-start(bf16[4,112,256]{2,1,0:T(8,128)(2,1)S(1)} %get-tuple-element.38), channel_id=1, source_target_pairs={{0,96},{16,112},{32,0},{48,16},{64,32},{80,48},{96,64},{112,80},{1... | collective-permute-start | bytes 688136 | tf_op jit(solution)/shard_map/ppermute | solution.py:319
  33.3 32.1 %collective-permute-start.6 = (bf16[4,112,256]{2,1,0:T(8,128)(2,1)S(1)}, bf16[4,112,256]{2,1,0:T(8,128)(2,1)S(1)}, u32[]{:S(2)}, u32[]{:S(2)}) collective-permute-start(bf16[4,112,256]{2,1,0:T(8,128)(2,1)S(1)} %get-tuple-element.39), channel_id=1, source_target_pairs={{0,112},{16,0},{32,16},{48,32},{64,48},{80,64},{96,80},{112,96},{1... | collective-permute-start | bytes 688136 | tf_op jit(solution)/shard_map/ppermute | solution.py:319
  65.6 0.8 copy-start.11
  66.4 0.8 copy-start.12
  67.2 0.8 copy-start.13
  73.8 1.5 copy-start
  75.2 80.1 %all-to-all-start.1 = ((bf16[16,32,2432]{2,1,0:T(8,128)(2,1)}), bf16[16,32,2432]{2,1,0:T(8,128)(2,1)S(1)}, u32[]{:S(2)}, u32[]{:S(2)}) async-start(bf16[16,32,2432]{2,1,0:T(8,128)(2,1)} %copy-done), calls=%async_computation.1 | async-start | bytes 4980736 | tf_op jit(solution)/shard_map/all_to_all | solution.py:313
  96.7 10.6 %collective-permute-start.7 = (bf16[8,112,256]{2,1,0:T(8,128)(2,1)}, bf16[8,112,256]{2,1,0:T(8,128)(2,1)S(1)}, u32[]{:S(2)}, u32[]{:S(2)}) collective-permute-start(bf16[8,112,256]{2,1,0:T(8,128)(2,1)} %copy-done.13), channel_id=1, source_target_pairs={{0,8},{8,0},{128,136},{136,128},{1,9},{9,1},{129,137},{137,129},{2... | collective-permute-start | bytes 1376264 | tf_op jit(solution)/shard_map/ppermute | solution.py:326
  99.2 21.4 %collective-permute-start.8 = (bf16[8,112,256]{2,1,0:T(8,128)(2,1)}, bf16[8,112,256]{2,1,0:T(8,128)(2,1)S(1)}, u32[]{:S(2)}, u32[]{:S(2)}) collective-permute-start(bf16[8,112,256]{2,1,0:T(8,128)(2,1)} %copy-done.12), channel_id=1, source_target_pairs={{0,128},{8,136},{128,0},{136,8},{1,129},{9,137},{129,1},{137,9},{2... | collective-permute-start | bytes 1376264 | tf_op jit(solution)/shard_map/ppermute | solution.py:326
  102.3 41.6 %collective-permute-start.9 = (bf16[8,112,256]{2,1,0:T(8,128)(2,1)}, bf16[8,112,256]{2,1,0:T(8,128)(2,1)S(1)}, u32[]{:S(2)}, u32[]{:S(2)}) collective-permute-start(bf16[8,112,256]{2,1,0:T(8,128)(2,1)} %copy-done.11), channel_id=1, source_target_pairs={{0,136},{8,128},{128,8},{136,0},{1,137},{9,129},{129,9},{137,1},{2... | collective-permute-start | bytes 1376264 | tf_op jit(solution)/shard_map/ppermute | solution.py:326
  106.0 1.3 copy-start.1
  107.2 55.5 %copy-start.9 = (s32[8,28]{1,0:T(8,128)S(1)}, s32[8,28]{1,0:T(8,128)}, u32[]{:S(2)}) copy-start(s32[8,28]{1,0:T(8,128)} %order_ref.3) | copy-start | bytes 2692
  107.2 0.8 copy-start.3
  120.5 0.8 copy-start.5
  121.3 41.4 %copy-start.4 = (bf16[8,112,256]{2,1,0:T(8,128)(2,1)S(1)}, bf16[8,112,256]{2,1,0:T(8,128)(2,1)}, u32[]{:S(2)}) copy-start(bf16[8,112,256]{2,1,0:T(8,128)(2,1)} %copy-done.3) | copy-start | bytes 1376260
  143.9 0.8 copy-start.7
  155.4 49.0 %all-to-all-start.2 = ((bf16[16,32,1792]{2,1,0:T(8,128)(2,1)}), bf16[16,32,1792]{2,1,0:T(8,128)(2,1)}, u32[]{:S(2)}, u32[]{:S(2)}) async-start(bf16[16,32,1792]{2,1,0:T(8,128)(2,1)} %copy-done.1), calls=%async_computation.2 | async-start | bytes 3670016 | tf_op jit(solution)/shard_map/all_to_all | solution.py:313
  161.4 6.0 %collective-permute-start.10 = (bf16[16,32,2432]{2,1,0:T(8,128)(2,1)S(1)}, bf16[16,32,2432]{2,1,0:T(8,128)(2,1)S(1)}, u32[]{:S(2)}, u32[]{:S(2)}) collective-permute-start(bf16[16,32,2432]{2,1,0:T(8,128)(2,1)S(1)} %all-to-all-done.1.own_ref), channel_id=1, source_target_pairs={{0,8},{8,0},{1,9},{9,1},{2,10},{10,2},{3,11},{11,3},{4,12},{12,4},... | collective-permute-start | bytes 7471112 | tf_op jit(solution)/shard_map/ppermute | solution.py:331
  162.8 1.0 copy-start.6
  163.8 1.0 copy-start.8
  204.4 6.8 %collective-permute-start.11 = (bf16[16,32,1792]{2,1,0:T(8,128)(2,1)}, bf16[16,32,1792]{2,1,0:T(8,128)(2,1)S(1)}, u32[]{:S(2)}, u32[]{:S(2)}) collective-permute-start(bf16[16,32,1792]{2,1,0:T(8,128)(2,1)} %all-to-all-done.2.own_ref), channel_id=1, source_target_pairs={{0,8},{8,0},{1,9},{9,1},{2,10},{10,2},{3,11},{11,3},{4,12},{12,4},... | collective-permute-start | bytes 5505032 | tf_op jit(solution)/shard_map/ppermute | solution.py:331

commit v3 on v2

v3 whole, which is shorter than its diff:
```python
import functools
import math

import jax
import jax.numpy as jnp
import numpy as np
from jax import lax
from jax.experimental import pallas as pl
from jax.experimental.pallas import tpu as pltpu
from jax.sharding import Mesh
from jax.sharding import PartitionSpec as P

BLK = 128
QPG = 8
FFB = 28
HALF_Q = QPG // 2
HALF_F = FFB // 2
ROWS = 32
PIECES = 16
DEEP = 8
SHIFTS = (0, 1, 7, 3, 5, 2, 6, 4)
FFN_WIDTH = HALF_F * BLK
HEADS_WIDTH = (HALF_Q + 1) * BLK
VMEM_LIMIT = 16 * 1024 * 1024
VMEM_MOST = 56 * 1024 * 1024
PLANE = ("xh", "xl", "y")
DEPTH = ("xh", "z")
FSDP = ("xh", "z", "core")
TP = ("xl", "y")


def signs(order):
    index = np.arange(order)
    common = index[:, None] & index[None, :]
    parity = np.zeros((order, order), np.int64)
    while common.any():
        parity ^= common & 1
        common = common >> 1
    return (1 - 2 * parity).astype(np.float32)


def bf16(values):
    return values.astype(jnp.bfloat16)


def params(limit=VMEM_LIMIT):
    return pltpu.CompilerParams(vmem_limit_bytes=limit)


def cost(flops, moved):
    return pl.CostEstimate(flops=int(flops), bytes_accessed=int(moved), transcendentals=0)


def side_index():
    return lax.axis_index("xh") * 2 + lax.axis_index("core")


def whole(count):
    return [pl.BlockSpec(memory_space=pltpu.VMEM)] * count


def pair_sums(values, span):
    out = list(values)
    for i in range(len(values)):
        if not i & span:
            out[i] = values[i] + values[i | span]
            out[i | span] = values[i] - values[i | span]
    return out


def down_kernel(weight_ref, sign_ref, *refs):
    out_refs, held_ref = refs[:DEEP], refs[DEEP]
    sign = sign_ref[...]
    groups = weight_ref.shape[1] // BLK
    side, z = side_index(), lax.axis_index("z")

    @pl.loop(0, weight_ref.shape[0] // 16)
    def _(step):
        rows = pl.ds(pl.multiple_of(step * 16, 16), 16)
        tall = jnp.concatenate(
            [weight_ref[rows, a * BLK : (a + 1) * BLK] for a in range(groups)], axis=0
        )
        half = jnp.dot(tall, sign, preferred_element_type=jnp.float32)
        half = bf16(half * (1.0 / math.sqrt(BLK))).astype(jnp.float32)
        parts = [half[a * 16 : (a + 1) * 16] for a in range(groups)]
        span = 1
        while span < groups:
            parts = pair_sums(parts, span)
            span *= 2
        for a in range(groups):
            held_ref[a] = bf16(parts[a] * (1.0 / math.sqrt(groups)))
        for at, s in enumerate(SHIFTS):
            for r in range(4):
                there = side ^ r
                shard = (there >> 1) * 2 * DEEP + ((z + s) & (DEEP - 1)) * 2 + (there & 1)
                for a in range(2):
                    out_refs[at][r, rows, a * BLK : (a + 1) * BLK] = held_ref[shard * 2 + a]


def rotate_down(weight, shards):
    rows, width = weight.shape
    groups = width // BLK
    return pl.pallas_call(
        down_kernel,
        out_shape=[jax.ShapeDtypeStruct((4, rows, width // shards), jnp.bfloat16)] * DEEP,
        in_specs=whole(2),
        out_specs=whole(DEEP),
        scratch_shapes=[pltpu.VMEM((groups, 16, BLK), jnp.bfloat16)],
        compiler_params=params(),
        cost_estimate=cost(2 * rows * width * BLK * 4, 4 * rows * width),
        name="down_rotate",
    )(weight, jnp.asarray(signs(BLK), jnp.bfloat16))


def repack_kernel(*refs):
    in_refs, out_refs = refs[:DEEP], refs[DEEP:]
    for r in range(4):
        for s in range(DEEP):
            out_refs[r][s] = in_refs[s][r]


def repack(pieces):
    _, rows, width = pieces[0].shape
    return pl.pallas_call(
        repack_kernel,
        out_shape=[jax.ShapeDtypeStruct((DEEP, rows, width), jnp.bfloat16)] * 4,
        in_specs=whole(DEEP),
        out_specs=whole(4),
        compiler_params=params(),
        cost_estimate=cost(4 * DEEP * rows * width, 16 * DEEP * rows * width),
        name="repack_down",
    )(*pieces)


def spread(gain_ref):
    row = lax.broadcasted_iota(jnp.int32, (ROWS, BLK), 0)
    spread_gain = jnp.zeros((ROWS, BLK), jnp.float32)
    for i in range(ROWS):
        spread_gain = jnp.where(row == i, gain_ref[i], spread_gain)
    return spread_gain


def scaled(ref, block, gain):
    columns = pl.ds(pl.multiple_of(block * BLK, BLK), BLK)
    return bf16(ref[:, columns].astype(jnp.float32) * gain)


def pick_kernel(with_heads, order_ref, ffn_gain_ref, ffn_ref, *refs):
    out_ref = refs[-1]
    ffn_gain = spread(ffn_gain_ref)
    if with_heads:
        heads_ref, attn_gain_ref, q_ref, k_ref, v_ref = refs[:-1]
        attn_gain = spread(attn_gain_ref)
    each = out_ref.shape[0]
    for j in range(each):
        piece = pl.program_id(0) * each + j
        owner, half = piece & 7, piece >> 3
        for slot in range(HALF_F):
            block = owner * FFB + order_ref[owner, half * HALF_F + slot]
            out_ref[j, :, slot * BLK : (slot + 1) * BLK] = scaled(ffn_ref, block, ffn_gain)
        if with_heads:
            for slot in range(HALF_Q):
                head = owner * QPG + heads_ref[owner, half * HALF_Q + slot]
                columns = slice(FFN_WIDTH + slot * BLK, FFN_WIDTH + (slot + 1) * BLK)
                out_ref[j, :, columns] = scaled(q_ref, head, attn_gain)
            out_ref[j, :, FFN_WIDTH + HALF_Q * BLK :] = jnp.where(
                half == 1, scaled(v_ref, owner, attn_gain), scaled(k_ref, owner, attn_gain)
            )


def pick(order, gain, weight, heads=()):
    each = 4
    width = FFN_WIDTH + (HEADS_WIDTH if heads else 0)
    small = pl.BlockSpec(memory_space=pltpu.SMEM)
    in_specs = [
        small if array.size < 1024 else pl.BlockSpec(array.shape, lambda i: (0, 0))
        for array in (order, gain, weight, *heads)
    ]
    return pl.pallas_call(
        functools.partial(pick_kernel, bool(heads)),
        grid=(PIECES // each,),
        out_shape=jax.ShapeDtypeStruct((PIECES, ROWS, width), jnp.bfloat16),
        in_specs=in_specs,
        out_specs=pl.BlockSpec((each, ROWS, width), lambda i: (i, 0, 0)),
        compiler_params=params(VMEM_MOST),
        cost_estimate=cost(PIECES * ROWS * width * 400, 4 * PIECES * ROWS * width),
        name="pick_columns",
    )(order, gain, weight, *heads)


def column_groups(widths, count):
    groups, begin = [], 0
    for at, width in enumerate(widths):
        step = -(-width // (count * BLK)) * BLK
        for start in range(0, width, step):
            groups.append((at, start, min(step, width - start), begin + start))
        begin += width
    return groups


def first_kernel(groups, matrix_ref, gates_ref, rest_ref, out_ref, in_held, out_held, in_sems, out_sems):
    in_copies, out_copies = [], []
    for at, (array, start, width, begin) in enumerate(groups):
        source = (gates_ref, rest_ref)[array].at[:, :, pl.ds(start, width)]
        there = pl.ds(begin, width)
        in_copies.append(
            pltpu.make_async_copy(source, in_held.at[:, :, there], in_sems.at[at])
        )
        out_copies.append(
            pltpu.make_async_copy(
                out_held.at[:, :, there], out_ref.at[:, :, there], out_sems.at[at]
            )
        )
    for copy in in_copies:
        copy.start()
    matrix = matrix_ref[...]
    for at, (_, _, width, begin) in enumerate(groups):
        in_copies[at].wait()
        for start in range(begin, begin + width, 2 * BLK):
            stop = min(start + 2 * BLK, begin + width)
            sides = [
                jnp.dot(
                    matrix,
                    in_held[side * 8 : side * 8 + 8, :, start:stop].reshape(8 * ROWS, -1),
                    preferred_element_type=jnp.float32,
                )
                for side in range(2)
            ]
            for which, mixed in enumerate((sides[0] + sides[1], sides[0] - sides[1])):
                mixed = bf16(mixed).reshape(8, ROWS, -1)
                for group in range(8):
                    out_held[2 * group + which, :, start:stop] = mixed[group]
        out_copies[at].start()
    for copy in out_copies:
        copy.wait()


def first_mix(gates, rest):
    rows = 8 * ROWS
    widths = (gates.shape[2], rest.shape[2])
    width = sum(widths)
    groups = column_groups(widths, 2)
    held = pltpu.VMEM((PIECES, ROWS, width), jnp.bfloat16)
    sems = pltpu.SemaphoreType.DMA((len(groups),))
    return pl.pallas_call(
        functools.partial(first_kernel, groups),
        out_shape=jax.ShapeDtypeStruct((PIECES, ROWS, width), jnp.bfloat16),
        in_specs=whole(1) + [pl.BlockSpec(memory_space=pl.ANY)] * 2,
        out_specs=pl.BlockSpec(memory_space=pl.ANY),
        scratch_shapes=[held, held, sems, sems],
        compiler_params=params(VMEM_MOST),
        cost_estimate=cost(4 * rows * rows * width, 8 * rows * width),
        name="first_mix",
    )(jnp.asarray(signs(rows) / 16.0, jnp.bfloat16), gates, rest)


def core_sign():
    return (1 - 2 * lax.axis_index("core")).astype(jnp.float32)


def side_sums(sign, ref, part, columns):
    rows = [ref[part * 8 + j, :, columns].astype(jnp.float32) for j in range(8)]
    rows = [rows[j] + sign * rows[j + 4] for j in range(4)]
    return pair_sums(pair_sums(rows, 2), 1)


def own_kernel(own_ref, out_ref, held, sems):
    sign = core_sign()
    copies = [
        pltpu.make_async_copy(
            own_ref.at[pl.ds(part * 8, 8)], held.at[pl.ds(part * 8, 8)], sems.at[part]
        )
        for part in range(2)
    ]
    for copy in copies:
        copy.start()
    for part in range(2):
        copies[part].wait()

        @pl.loop(0, held.shape[2] // BLK)
        def _(step):
            columns = pl.ds(pl.multiple_of(step * BLK, BLK), BLK)
            for j, value in enumerate(side_sums(sign, held, part, columns)):
                out_ref[part * 4 + j, :, columns] = value


def own_sums(own):
    width = own.shape[2]
    return pl.pallas_call(
        own_kernel,
        out_shape=jax.ShapeDtypeStruct((8, ROWS, width), jnp.float32),
        in_specs=[pl.BlockSpec(memory_space=pl.ANY)],
        out_specs=whole(1)[0],
        scratch_shapes=[pltpu.VMEM(own.shape, jnp.bfloat16), pltpu.SemaphoreType.DMA((2,))],
        compiler_params=params(),
        cost_estimate=cost(40 * own.size, 4 * own.size),
        name="own_sums",
    )(own)


def last_columns(sign, sums_ref, other_ref, part, columns):
    theirs = side_sums(sign, other_ref, part, columns)
    scale = 16.0 / math.sqrt(8192.0)
    parts = []
    for j in range(4):
        mine = sums_ref[part * 4 + j, :, columns]
        parts.append(bf16((mine + theirs[j]) * scale))
        parts.append(bf16((mine - theirs[j]) * (scale * sign)))
    return jnp.concatenate(parts, axis=0)


def last_kernel(sums_ref, other_ref, ffn_ref, heads_ref):
    sign = core_sign()
    part = pl.program_id(0) & 1
    begin = (pl.program_id(0) >> 1) * HALF_F

    @pl.loop(0, HALF_F // 2)
    def _(step):
        columns = pl.ds(pl.multiple_of(step * 2 * BLK, 2 * BLK), 2 * BLK)
        source = pl.ds(pl.multiple_of((begin + step * 2) * BLK, 2 * BLK), 2 * BLK)
        ffn_ref[:, columns] = last_columns(sign, sums_ref, other_ref, part, source)

    @pl.when(pl.program_id(0) == 0)
    def _():
        for half in range(2):
            for slot in range(HALF_Q + 1):
                block = half * HALF_Q + slot if slot < HALF_Q else QPG + half
                source = slice(2 * FFN_WIDTH + slot * BLK, 2 * FFN_WIDTH + (slot + 1) * BLK)
                heads_ref[:, block * BLK : (block + 1) * BLK] = last_columns(
                    sign, sums_ref, other_ref, half, source
                )


def last_mix(sums, other):
    rows = 8 * ROWS
    width = 4 * FFN_WIDTH
    return pl.pallas_call(
        last_kernel,
        grid=(4,),
        out_shape=[
            jax.ShapeDtypeStruct((rows, width), jnp.bfloat16),
            jax.ShapeDtypeStruct((rows, 2 * HEADS_WIDTH), jnp.bfloat16),
        ],
        in_specs=whole(2),
        out_specs=[
            pl.BlockSpec((rows, FFN_WIDTH), lambda i: (0, i)),
            pl.BlockSpec((rows, 2 * HEADS_WIDTH), lambda i: (0, 0)),
        ],
        compiler_params=params(),
        cost_estimate=cost(40 * rows * width, 6 * rows * width),
        name="last_mix",
    )(sums, other)


def order_kernel(order_ref, *refs):
    in_refs, (out_ref, slot_ref) = refs[:4], refs[4:]
    owner = lax.axis_index("xl") * 4 + lax.axis_index("y")
    side, z = side_index(), lax.axis_index("z")
    for slot in range(FFB):
        slot_ref[order_ref[owner, slot]] = slot
    groups = in_refs[0].shape[1] // 16
    for r in range(4):
        there = side ^ r
        for place, s in enumerate(SHIFTS):
            shard = (there >> 1) * 2 * DEEP + ((z - s) & (DEEP - 1)) * 2 + (there & 1)
            for group in range(groups):
                at = shard * groups + group
                row = slot_ref[at >> 3] * BLK + (at & 7) * 16
                out_ref[pl.ds(pl.multiple_of(row, 16), 16), :] = in_refs[r][
                    place, group * 16 : (group + 1) * 16, :
                ]


def order_rows(ffn_order, pieces):
    count, rows, width = pieces[0].shape
    return pl.pallas_call(
        order_kernel,
        out_shape=jax.ShapeDtypeStruct((4 * count * rows, width), jnp.bfloat16),
        in_specs=[pl.BlockSpec(memory_space=pltpu.SMEM)] + whole(4),
        out_specs=whole(1)[0],
        scratch_shapes=[pltpu.SMEM((FFB,), jnp.int32)],
        compiler_params=params(),
        cost_estimate=cost(4 * count * rows * width, 16 * count * rows * width),
        name="order_rows",
    )(ffn_order, *pieces)


def exchange(pieces, axes):
    return lax.all_to_all(pieces, axes, split_axis=0, concat_axis=0, tiled=True)


def exchange_apart(go, pieces, axes):
    return lax.cond(go, lambda part: exchange(part, axes), jnp.zeros_like, pieces)


def exchange_z(pieces):
    got = list(pieces)
    for at, s in enumerate(SHIFTS):
        if s:
            got[at] = lax.ppermute(pieces[at], "z", [(i, (i + s) % DEEP) for i in range(DEEP)])
    return got


def exchange_side(pieces):
    got = list(pieces)
    for r in (1, 2, 3):
        got[r] = lax.ppermute(pieces[r], ("xh", "core"), [(i, i ^ r) for i in range(4)])
    return got


def exchange_core(got):
    return lax.ppermute(got, "core", [(0, 1), (1, 0)])


def tie(*arrays):
    return lax.optimization_barrier(arrays)


def per_device(
    q_weight,
    k_weight,
    v_weight,
    gate_weight,
    up_weight,
    down_weight,
    attn_gain,
    ffn_gain,
    head_order,
    ffn_order,
):
    shards = math.prod(lax.axis_size(name) for name in FSDP)
    go = lax.axis_index("z") >= 0
    gates = exchange(pick(ffn_order, ffn_gain, gate_weight), PLANE)
    heads = (head_order, attn_gain, q_weight, k_weight, v_weight)
    rest = pick(ffn_order, ffn_gain, up_weight, heads)
    shifted = exchange_z(rotate_down(down_weight, shards))
    rest, gates = tie(rest, gates)
    rest, *shifted = tie(exchange_apart(go, rest, PLANE), *shifted)
    mixed, *packed = tie(first_mix(gates, rest), *repack(shifted))
    mixed = exchange_apart(go, mixed, DEPTH)
    moved = exchange_side(packed)
    mixed, *moved = tie(mixed, *moved)
    other = exchange_core(mixed)
    merged_down = order_rows(ffn_order, moved)
    merged_ffn, merged_attn = last_mix(own_sums(mixed), other)
    return (merged_attn, merged_ffn, merged_down)


def solution(mesh):
    split = Mesh(mesh.devices.reshape(2, 8, 2, 2, 4), ("xh", "z", "core", "xl", "y"))
    rows = TP + FSDP
    placed = (P(rows, None),) * 6 + (P(rows),) * 2 + (P(), P())
    return jax.shard_map(
        per_device,
        mesh=split,
        in_specs=placed,
        out_specs=(P(FSDP, TP), P(FSDP, TP), P(TP, FSDP)),
        check_vma=False,
    )
```

time: 215 us -> 205 us (0.953); the launches traced: 215 us -> 202 us
  blocking collectives: 0 us -> 139 us
  waiting for transfers between devices: 115 us -> 1.98 us
  starting transfers between devices: 65 us -> 34.8 us
  local copies, waits for them, and re-layouts: 9.38 us -> 0.01 us
    all_to_all x0 -> x2, blocking collectives: none -> 139 us  [exchange(): return lax.all_to_all(pieces, axes, split_axis=0, concat_axis=0, tiled=True)]
    all_to_all x3 -> x1, waiting for transfers between devices: 46.9 us -> 0.01 us  [exchange(): return lax.all_to_all(pieces, axes, split_axis=0, concat_axis=0, tiled=True)]
    ppermute x3, waiting for transfers between devices: 35.1 us -> 0.01 us  [exchange_side(): lax.ppermute(pieces[r], ('xh', 'core'), [(i, i ^ r) for i in range(4)])]
    ppermute x7, waiting for transfers between devices: 29.3 us -> 0.27 us  [exchange_z(): lax.ppermute(pieces[at], 'z', [(i, (i + s) % DEEP) for i in range(DEEP)])]
    all_to_all x3 -> x1, starting transfers between devices: 34.2 us -> 6.74 us  [exchange(): return lax.all_to_all(pieces, axes, split_axis=0, concat_axis=0, tiled=True)]
    unnamed x30 -> x6, local copies, waits for them, and re-layouts: 9.38 us -> 0.01 us
    ppermute x7, starting transfers between devices: 20.5 us -> 17.5 us  [exchange_z(): lax.ppermute(pieces[at], 'z', [(i, (i + s) % DEEP) for i in range(DEEP)])]
    ppermute x2 -> x1, starting transfers between devices: 4.54 us -> 3.06 us  [exchange_core(): return lax.ppermute(got, 'core', [(0, 1), (1, 0)])]
  transfers between devices with their start and end apart: 15 -> 12, of which waited for: 11 -> 2; matrix products, arithmetic and copies ran while one was open for 0% -> 0% of each run, Pallas kernels for 6% -> 6%
where the time goes in v3:
time: 205 us; the launch traced here: 202 us
  blocking collectives  139 us (68%)
  starting transfers between devices  34.8 us (17%)
  Pallas kernels  25.7 us (13%)
    all_to_all x2, blocking collectives, exchange(): return lax.all_to_all(pieces, axes, split_axis=0, concat_axis=0, tiled=True)  139 us
    ppermute x7, starting transfers between devices, exchange_z(): lax.ppermute(pieces[at], 'z', [(i, (i + s) % DEEP) for i in range(DEEP)])  17.5 us
    pallas_call x2, Pallas kernels, pick(): pl.pallas_call(functools.partial(pick_kernel, bool(heads)), grid=(PIECES...  7.93 us
    ppermute x3, starting transfers between devices, exchange_side(): lax.ppermute(pieces[r], ('xh', 'core'), [(i, i ^ r) for i in range(4)])  7.54 us
    all_to_all x1, starting transfers between devices, exchange(): return lax.all_to_all(pieces, axes, split_axis=0, concat_axis=0, tiled=True)  6.74 us
    pallas_call x1, Pallas kernels, first_mix(): pl.pallas_call(functools.partial(first_kernel, groups), out_shape=jax.Sha...  5.13 us
  transfers between devices with their start and end apart: 12, of which 2 were waited for; matrix products, arithmetic and copies ran while one was open for 0% of the time, Pallas kernels for 6%

profile of v3, /device:TPU:25, one launch (start us, length us, event | category | flops | bytes accessed | tf_op | source)
XLA Modules:
  0.0 201.8 jit_solution(5490171941749696093)
XLA Ops:
  0.6 3.7 %pick_columns.3 = bf16[16,32,1792]{2,1,0:T(8,128)(2,1)} custom-call(s32[8,28]{1,0:T(8,128)} %order_ref.5, f32[32]{0:T(128)} %ffn_gain_ref.3, bf16[32,28672]{1,0:T(8,128)(2,1)} %ffn_ref.3), custom_call_target="tpu_custom_call" | custom-call | flops 367001600 | bytes 3670016 | tf_op jit(solution)/shard_map/pick_columns/pallas_call | solution.py:179
  4.3 0.0 copy-start.1
  4.3 0.0 copy-start.2
  4.3 6.7 %all-to-all-start.2 = ((bf16[16,32,1792]{2,1,0:T(8,128)(2,1)}), bf16[16,32,1792]{2,1,0:T(8,128)(2,1)}, u32[]{:S(2)}, u32[]{:S(2)}) async-start(bf16[16,32,1792]{2,1,0:T(8,128)(2,1)} %pick_columns.3), calls=%async_computation.2 | async-start | bytes 3670016 | tf_op jit(solution)/shard_map/all_to_all | solution.py:389
  11.1 0.0 copy-done.1
  11.1 0.0 copy-done.2
  11.1 2.9 %down_rotate.1 = (bf16[4,112,256]{2,1,0:T(8,128)(2,1)S(1)}, bf16[4,112,256]{2,1,0:T(8,128)(2,1)S(1)}, bf16[4,112,256]{2,1,0:T(8,128)(2,1)S(1)}, bf16[4,112,256]{...) custom-call(bf16[112,8192]{1,0:T(8,128)(2,1)S(1)} %copy-done.1, ...), custom_call_target="tpu_custom_call" | custom-call | flops 939524096 | bytes 3670016 | tf_op jit(solution)/shard_map/down_rotate/pallas_call | solution.py:103
  14.0 1.7 collective-permute-start
  15.7 4.1 %collective-permute-start.1 = (bf16[4,112,256]{2,1,0:T(8,128)(2,1)S(1)}, bf16[4,112,256]{2,1,0:T(8,128)(2,1)S(1)}, u32[]{:S(2)}, u32[]{:S(2)}) collective-permute-start(bf16[4,112,256]{2,1,0:T(8,128)(2,1)S(1)} %get-tuple-element.50), channel_id=1, source_target_pairs={{0,112},{16,0},{32,16},{48,32},{64,48},{80,64},{96,80},{112,96},{1... | collective-permute-start | bytes 688136 | tf_op jit(solution)/shard_map/ppermute | solution.py:400
  19.7 1.5 collective-permute-start.2
  21.2 3.0 %collective-permute-start.3 = (bf16[4,112,256]{2,1,0:T(8,128)(2,1)S(1)}, bf16[4,112,256]{2,1,0:T(8,128)(2,1)S(1)}, u32[]{:S(2)}, u32[]{:S(2)}) collective-permute-start(bf16[4,112,256]{2,1,0:T(8,128)(2,1)S(1)} %get-tuple-element.52), channel_id=1, source_target_pairs={{0,80},{16,96},{32,112},{48,0},{64,16},{80,32},{96,48},{112,64},{1... | collective-permute-start | bytes 688136 | tf_op jit(solution)/shard_map/ppermute | solution.py:400
  24.2 0.0 collective-permute-start.4
  24.2 0.3 collective-permute-done.refs_1_
  24.5 3.3 %collective-permute-start.5 = (bf16[4,112,256]{2,1,0:T(8,128)(2,1)S(1)}, bf16[4,112,256]{2,1,0:T(8,128)(2,1)S(1)}, u32[]{:S(2)}, u32[]{:S(2)}) collective-permute-start(bf16[4,112,256]{2,1,0:T(8,128)(2,1)S(1)} %get-tuple-element.54), channel_id=1, source_target_pairs={{0,96},{16,112},{32,0},{48,16},{64,32},{80,48},{96,64},{112,80},{1... | collective-permute-start | bytes 688136 | tf_op jit(solution)/shard_map/ppermute | solution.py:400
  27.8 0.0 collective-permute-done.1.refs_2_
  27.8 3.9 %collective-permute-start.6 = (bf16[4,112,256]{2,1,0:T(8,128)(2,1)S(1)}, bf16[4,112,256]{2,1,0:T(8,128)(2,1)S(1)}, u32[]{:S(2)}, u32[]{:S(2)}) collective-permute-start(bf16[4,112,256]{2,1,0:T(8,128)(2,1)S(1)} %get-tuple-element.55), channel_id=1, source_target_pairs={{0,64},{16,80},{32,96},{48,112},{64,0},{80,16},{96,32},{112,48},{1... | collective-permute-start | bytes 688136 | tf_op jit(solution)/shard_map/ppermute | solution.py:400
  31.7 4.2 %pick_columns.2 = bf16[16,32,2432]{2,1,0:T(8,128)(2,1)} custom-call(s32[8,28]{1,0:T(8,128)} %order_ref.5, f32[32]{0:T(128)} %ffn_gain_ref.3, bf16[32,28672]{1,0:T(8,128)(2,1)} %ffn_ref.2, s32[8,8]{1,0:T(8,128)} %refs_0_.1, f32[32]{0:T(128)} %refs_1_.1, bf16[32,8192]{1,0:T(8,128)(2,1)} %refs_2_.1, bf16[32,1024]{1,0:T(8,128)(2,1)} %refs_3_.1, ...), custom_call_target="tpu_custom_call" | custom-call | flops 498073600 | bytes 4980736 | tf_op jit(solution)/shard_map/pick_columns/pallas_call | solution.py:179
  35.9 0.0 all-to-all-done.2.gates_ref
  35.9 33.7 %conditional.2 = (bf16[16,32,2432]{2,1,0:T(8,128)(2,1)}) conditional(s32[]{:T(128)} %convert_element_type.4, () %tuple.26, bf16[16,32,2432]{2,1,0:T(8,128)(2,1)} %pick_columns.2), branch_computations={%region_0.0_spmd, %region_1.0_spmd} | conditional | bytes 4980744 | solution.py:393
  35.9 33.7 %all_to_all.13 = bf16[16,32,2432]{2,1,0:T(8,128)(2,1)} all-to-all(bf16[16,32,2432]{2,1,0:T(8,128)(2,1)} %param.1), channel_id=1, replica_groups=mesh['xh'=2,'z'=8,'core'=2,'xl'=2,'y'=4] {'xh','xl','y'}, dimensions={0} | all-to-all | bytes 4980736 | tf_op jit(solution)/shard_map/cond/branch_1_fun/all_to_all | solution.py:389
  69.6 0.0 collective-permute-done.2.refs_3_
  69.6 0.0 collective-permute-done.3.refs_4_
  69.6 0.0 collective-permute-done.4.refs_5_
  69.6 0.0 collective-permute-done.5.refs_6_
  69.6 0.0 collective-permute-done.6.refs_7_
  69.6 5.1 %first_mix.1 = bf16[16,32,4224]{2,1,0:T(8,128)(2,1)} custom-call(bf16[256,256]{1,0:T(8,128)(2,1)} %constant.17.clone.matrix_ref, bf16[16,32,1792]{2,1,0:T(8,128)(2,1)} %all-to-all-done.2.gates_ref, bf16[16,32,2432]{2,1,0:T(8,128)(2,1)} %get-tuple-element.81.rest_ref), custom_call_target="tpu_custom_call" | custom-call | flops 1107296256 | bytes 8650752 | tf_op jit(solution)/shard_map/first_mix/pallas_call | solution.py:245
  74.8 0.9 repack_down.1
  75.7 4.4 %collective-permute-start.7 = (bf16[8,112,256]{2,1,0:T(8,128)(2,1)}, bf16[8,112,256]{2,1,0:T(8,128)(2,1)S(1)}, u32[]{:S(2)}, u32[]{:S(2)}) collective-permute-start(bf16[8,112,256]{2,1,0:T(8,128)(2,1)} %get-tuple-element.71), channel_id=1, source_target_pairs={{0,8},{8,0},{128,136},{136,128},{1,9},{9,1},{129,137},{137,129},{2... | collective-permute-start | bytes 1376264 | tf_op jit(solution)/shard_map/ppermute | solution.py:407
  80.1 1.3 collective-permute-start.8
  81.3 1.8 collective-permute-start.9
  83.2 0.0 copy-start
  83.2 104.9 %conditional.3 = (bf16[16,32,4224]{2,1,0:T(8,128)(2,1)}) conditional(s32[]{:T(128)} %convert_element_type.4, () %tuple.24, bf16[16,32,4224]{2,1,0:T(8,128)(2,1)} %first_mix.1), branch_computations={%region_2.0_spmd, %region_3.0_spmd} | conditional | bytes 8650760 | solution.py:393
  83.2 104.9 %all_to_all.14 = bf16[16,32,4224]{2,1,0:T(8,128)(2,1)} all-to-all(bf16[16,32,4224]{2,1,0:T(8,128)(2,1)} %param.3), channel_id=1, replica_groups=mesh['xh'=2,'z'=8,'core'=2,'xl'=2,'y'=4] {'xh','z'}, dimensions={0} | all-to-all | bytes 8650752 | tf_op jit(solution)/shard_map/cond/branch_1_fun/all_to_all | solution.py:389
  188.1 0.0 collective-permute-done.7.refs_1_
  188.1 0.0 collective-permute-done.8.refs_2_
  188.1 0.0 collective-permute-done.9.refs_3_
  188.1 3.1 %collective-permute-start.10 = (bf16[16,32,4224]{2,1,0:T(8,128)(2,1)}, bf16[16,32,4224]{2,1,0:T(8,128)(2,1)S(1)}, u32[]{:S(2)}, u32[]{:S(2)}) collective-permute-start(bf16[16,32,4224]{2,1,0:T(8,128)(2,1)} %get-tuple-element.82.own_ref), channel_id=1, source_target_pairs={{0,8},{8,0},{1,9},{9,1},{2,10},{10,2},{3,11},{11,3},{4,12},{12,4},... | collective-permute-start | bytes 12976136 | tf_op jit(solution)/shard_map/ppermute | solution.py:412
  191.2 0.0 copy-done
  191.2 2.6 %order_rows.1 = bf16[3584,256]{1,0:T(8,128)(2,1)} custom-call(s32[8,28]{1,0:T(8,128)S(1)} %copy-done, bf16[8,112,256]{2,1,0:T(8,128)(2,1)S(1)} %get-tuple-element.77.refs_0_, bf16[8,112,256]{2,1,0:T(8,128)(2,1)S(1)} %collective-permute-done.7.refs_1_, bf16[8,112,256]{2,1,0:T(8,128)(2,1)S(1)} %collective-permute-done.8.refs_2_, ...), custom_call_target="tpu_custom_call" | custom-call | flops 917504 | bytes 3670016 | tf_op jit(solution)/shard_map/order_rows/pallas_call | solution.py:376
  193.8 2.8 %own_sums.1.sums_ref = f32[8,32,4224]{2,1,0:T(8,128)S(1)} custom-call(bf16[16,32,4224]{2,1,0:T(8,128)(2,1)} %get-tuple-element.82.own_ref), custom_call_target="tpu_custom_call" | custom-call | flops 86507520 | bytes 8650752 | tf_op jit(solution)/shard_map/own_sums/pallas_call | solution.py:289
  196.7 1.7 collective-permute-done.10.other_ref
  198.4 3.5 %last_mix.1 = (bf16[256,7168]{1,0:T(8,128)(2,1)}, bf16[256,1280]{1,0:T(8,128)(2,1)}) custom-call(f32[8,32,4224]{2,1,0:T(8,128)S(1)} %own_sums.1.sums_ref, bf16[16,32,4224]{2,1,0:T(8,128)(2,1)S(1)} %collective-permute-done.10.other_ref), custom_call_target="tpu_custom_call" | custom-call | flops 73400320 | bytes 11010048 | tf_op jit(solution)/shard_map/last_mix/pallas_call | solution.py:337
Async XLA Ops:
  4.3 6.7 %copy-start.1 = (bf16[112,8192]{1,0:T(8,128)(2,1)S(1)}, bf16[112,8192]{1,0:T(8,128)(2,1)}, u32[]{:S(2)}) copy-start(bf16[112,8192]{1,0:T(8,128)(2,1)} %weight_ref.1) | copy-start | bytes 5505028
  4.3 6.7 %copy-start.2 = (bf16[128,128]{1,0:T(8,128)(2,1)S(1)}, bf16[128,128]{1,0:T(8,128)(2,1)}, u32[]{:S(2)}) copy-start(bf16[128,128]{1,0:T(8,128)(2,1)} %constant.16.clone.sign_ref) | copy-start | bytes 98308
  4.3 31.6 %all-to-all-start.2 = ((bf16[16,32,1792]{2,1,0:T(8,128)(2,1)}), bf16[16,32,1792]{2,1,0:T(8,128)(2,1)}, u32[]{:S(2)}, u32[]{:S(2)}) async-start(bf16[16,32,1792]{2,1,0:T(8,128)(2,1)} %pick_columns.3), calls=%async_computation.2 | async-start | bytes 3670016 | tf_op jit(solution)/shard_map/all_to_all | solution.py:389
  14.0 10.5 %collective-permute-start = (bf16[4,112,256]{2,1,0:T(8,128)(2,1)S(1)}, bf16[4,112,256]{2,1,0:T(8,128)(2,1)S(1)}, u32[]{:S(2)}, u32[]{:S(2)}) collective-permute-start(bf16[4,112,256]{2,1,0:T(8,128)(2,1)S(1)} %get-tuple-element.49), channel_id=1, source_target_pairs={{0,16},{16,32},{32,48},{48,64},{64,80},{80,96},{96,112},{112,0},{1... | collective-permute-start | bytes 688136 | tf_op jit(solution)/shard_map/ppermute | solution.py:400
  15.7 12.1 %collective-permute-start.1 = (bf16[4,112,256]{2,1,0:T(8,128)(2,1)S(1)}, bf16[4,112,256]{2,1,0:T(8,128)(2,1)S(1)}, u32[]{:S(2)}, u32[]{:S(2)}) collective-permute-start(bf16[4,112,256]{2,1,0:T(8,128)(2,1)S(1)} %get-tuple-element.50), channel_id=1, source_target_pairs={{0,112},{16,0},{32,16},{48,32},{64,48},{80,64},{96,80},{112,96},{1... | collective-permute-start | bytes 688136 | tf_op jit(solution)/shard_map/ppermute | solution.py:400
  19.7 49.9 %collective-permute-start.2 = (bf16[4,112,256]{2,1,0:T(8,128)(2,1)S(1)}, bf16[4,112,256]{2,1,0:T(8,128)(2,1)S(1)}, u32[]{:S(2)}, u32[]{:S(2)}) collective-permute-start(bf16[4,112,256]{2,1,0:T(8,128)(2,1)S(1)} %get-tuple-element.51), channel_id=1, source_target_pairs={{0,48},{16,64},{32,80},{48,96},{64,112},{80,0},{96,16},{112,32},{1... | collective-permute-start | bytes 688136 | tf_op jit(solution)/shard_map/ppermute | solution.py:400
  21.2 48.4 %collective-permute-start.3 = (bf16[4,112,256]{2,1,0:T(8,128)(2,1)S(1)}, bf16[4,112,256]{2,1,0:T(8,128)(2,1)S(1)}, u32[]{:S(2)}, u32[]{:S(2)}) collective-permute-start(bf16[4,112,256]{2,1,0:T(8,128)(2,1)S(1)} %get-tuple-element.52), channel_id=1, source_target_pairs={{0,80},{16,96},{32,112},{48,0},{64,16},{80,32},{96,48},{112,64},{1... | collective-permute-start | bytes 688136 | tf_op jit(solution)/shard_map/ppermute | solution.py:400
  24.2 45.4 %collective-permute-start.4 = (bf16[4,112,256]{2,1,0:T(8,128)(2,1)S(1)}, bf16[4,112,256]{2,1,0:T(8,128)(2,1)S(1)}, u32[]{:S(2)}, u32[]{:S(2)}) collective-permute-start(bf16[4,112,256]{2,1,0:T(8,128)(2,1)S(1)} %get-tuple-element.53), channel_id=1, source_target_pairs={{0,32},{16,48},{32,64},{48,80},{64,96},{80,112},{96,0},{112,16},{1... | collective-permute-start | bytes 688136 | tf_op jit(solution)/shard_map/ppermute | solution.py:400
  24.5 45.2 %collective-permute-start.5 = (bf16[4,112,256]{2,1,0:T(8,128)(2,1)S(1)}, bf16[4,112,256]{2,1,0:T(8,128)(2,1)S(1)}, u32[]{:S(2)}, u32[]{:S(2)}) collective-permute-start(bf16[4,112,256]{2,1,0:T(8,128)(2,1)S(1)} %get-tuple-element.54), channel_id=1, source_target_pairs={{0,96},{16,112},{32,0},{48,16},{64,32},{80,48},{96,64},{112,80},{1... | collective-permute-start | bytes 688136 | tf_op jit(solution)/shard_map/ppermute | solution.py:400
  27.8 41.8 %collective-permute-start.6 = (bf16[4,112,256]{2,1,0:T(8,128)(2,1)S(1)}, bf16[4,112,256]{2,1,0:T(8,128)(2,1)S(1)}, u32[]{:S(2)}, u32[]{:S(2)}) collective-permute-start(bf16[4,112,256]{2,1,0:T(8,128)(2,1)S(1)} %get-tuple-element.55), channel_id=1, source_target_pairs={{0,64},{16,80},{32,96},{48,112},{64,0},{80,16},{96,32},{112,48},{1... | collective-permute-start | bytes 688136 | tf_op jit(solution)/shard_map/ppermute | solution.py:400
  75.7 112.5 %collective-permute-start.7 = (bf16[8,112,256]{2,1,0:T(8,128)(2,1)}, bf16[8,112,256]{2,1,0:T(8,128)(2,1)S(1)}, u32[]{:S(2)}, u32[]{:S(2)}) collective-permute-start(bf16[8,112,256]{2,1,0:T(8,128)(2,1)} %get-tuple-element.71), channel_id=1, source_target_pairs={{0,8},{8,0},{128,136},{136,128},{1,9},{9,1},{129,137},{137,129},{2... | collective-permute-start | bytes 1376264 | tf_op jit(solution)/shard_map/ppermute | solution.py:407
  80.1 108.1 %collective-permute-start.8 = (bf16[8,112,256]{2,1,0:T(8,128)(2,1)S(1)}, bf16[8,112,256]{2,1,0:T(8,128)(2,1)S(1)}, u32[]{:S(2)}, u32[]{:S(2)}) collective-permute-start(bf16[8,112,256]{2,1,0:T(8,128)(2,1)S(1)} %get-tuple-element.72), channel_id=1, source_target_pairs={{0,128},{8,136},{128,0},{136,8},{1,129},{9,137},{129,1},{137,9},{2... | collective-permute-start | bytes 1376264 | tf_op jit(solution)/shard_map/ppermute | solution.py:407
  81.3 106.8 %collective-permute-start.9 = (bf16[8,112,256]{2,1,0:T(8,128)(2,1)S(1)}, bf16[8,112,256]{2,1,0:T(8,128)(2,1)S(1)}, u32[]{:S(2)}, u32[]{:S(2)}) collective-permute-start(bf16[8,112,256]{2,1,0:T(8,128)(2,1)S(1)} %get-tuple-element.73), channel_id=1, source_target_pairs={{0,136},{8,128},{128,8},{136,0},{1,137},{9,129},{129,9},{137,1},{2... | collective-permute-start | bytes 1376264 | tf_op jit(solution)/shard_map/ppermute | solution.py:407
  83.2 108.0 %copy-start = (s32[8,28]{1,0:T(8,128)S(1)}, s32[8,28]{1,0:T(8,128)}, u32[]{:S(2)}) copy-start(s32[8,28]{1,0:T(8,128)} %order_ref.5) | copy-start | bytes 2692
  188.1 10.2 %collective-permute-start.10 = (bf16[16,32,4224]{2,1,0:T(8,128)(2,1)}, bf16[16,32,4224]{2,1,0:T(8,128)(2,1)S(1)}, u32[]{:S(2)}, u32[]{:S(2)}) collective-permute-start(bf16[16,32,4224]{2,1,0:T(8,128)(2,1)} %get-tuple-element.82.own_ref), channel_id=1, source_target_pairs={{0,8},{8,0},{1,9},{9,1},{2,10},{10,2},{3,11},{11,3},{4,12},{12,4},... | collective-permute-start | bytes 12976136 | tf_op jit(solution)/shard_map/ppermute | solution.py:412

commit v4 on v3

--- a/solution.py
+++ b/solution.py
@@ -153,8 +153,7 @@
         attn_gain = spread(attn_gain_ref)
     each = out_ref.shape[0]
     for j in range(each):
-        piece = pl.program_id(0) * each + j
-        owner, half = piece & 7, piece >> 3
+        owner, half = j, pl.program_id(0)
         for slot in range(HALF_F):
             block = owner * FFB + order_ref[owner, half * HALF_F + slot]
             out_ref[j, :, slot * BLK : (slot + 1) * BLK] = scaled(ffn_ref, block, ffn_gain)
@@ -169,7 +168,7 @@
 
 
 def pick(order, gain, weight, heads=()):
-    each = 4
+    each = 8
     width = FFN_WIDTH + (HEADS_WIDTH if heads else 0)
     small = pl.BlockSpec(memory_space=pltpu.SMEM)
     in_specs = [
@@ -314,11 +313,11 @@
     part = pl.program_id(0) & 1
     begin = (pl.program_id(0) >> 1) * HALF_F
 
-    @pl.loop(0, HALF_F // 2)
-    def _(step):
-        columns = pl.ds(pl.multiple_of(step * 2 * BLK, 2 * BLK), 2 * BLK)
-        source = pl.ds(pl.multiple_of((begin + step * 2) * BLK, 2 * BLK), 2 * BLK)
-        ffn_ref[:, columns] = last_columns(sign, sums_ref, other_ref, part, source)
+    for step in range(0, HALF_F, 2):
+        source = pl.ds(pl.multiple_of((begin + step) * BLK, 2 * BLK), 2 * BLK)
+        ffn_ref[:, step * BLK : (step + 2) * BLK] = last_columns(
+            sign, sums_ref, other_ref, part, source
+        )
 
     @pl.when(pl.program_id(0) == 0)
     def _():
@@ -401,9 +400,9 @@
     return got
 
 
-def exchange_side(pieces):
+def exchange_side(pieces, sides):
     got = list(pieces)
-    for r in (1, 2, 3):
+    for r in sides:
         got[r] = lax.ppermute(pieces[r], ("xh", "core"), [(i, i ^ r) for i in range(4)])
     return got
 
@@ -438,9 +437,10 @@
     rest, *shifted = tie(exchange_apart(go, rest, PLANE), *shifted)
     mixed, *packed = tie(first_mix(gates, rest), *repack(shifted))
     mixed = exchange_apart(go, mixed, DEPTH)
-    moved = exchange_side(packed)
+    moved = exchange_side(packed, (2, 3))
     mixed, *moved = tie(mixed, *moved)
     other = exchange_core(mixed)
+    moved = exchange_side(moved, (1,))
     merged_down = order_rows(ffn_order, moved)
     merged_ffn, merged_attn = last_mix(own_sums(mixed), other)
     return (merged_attn, merged_ffn, merged_down)

time: 205 us -> 204 us (level)
  starting transfers between devices: 34.8 us -> 32.3 us
    ppermute x3, waiting for transfers between devices: 0.01 us -> 3.51 us  [exchange_side(): lax.ppermute(pieces[r], ('xh', 'core'), [(i, i ^ r) for i in range(4)])]
    ppermute x1, starting transfers between devices: 3.06 us -> 0.12 us  [exchange_core(): return lax.ppermute(got, 'core', [(0, 1), (1, 0)])]
where the time goes in v4:
time: 204 us; the launch traced here: 202 us
  blocking collectives  140 us (69%)
  starting transfers between devices  32.3 us (16%)
  Pallas kernels  24.5 us (12%)
  waiting for transfers between devices  3.79 us (2%)
    all_to_all x2, blocking collectives, exchange(): return lax.all_to_all(pieces, axes, split_axis=0, concat_axis=0, tiled=True)  140 us
    ppermute x7, starting transfers between devices, exchange_z(): lax.ppermute(pieces[at], 'z', [(i, (i + s) % DEEP) for i in range(DEEP)])  17.5 us
    ppermute x3, starting transfers between devices, exchange_side(): lax.ppermute(pieces[r], ('xh', 'core'), [(i, i ^ r) for i in range(4)])  8.01 us
    pallas_call x2, Pallas kernels, pick(): pl.pallas_call(functools.partial(pick_kernel, bool(heads)), grid=(PIECES...  6.76 us
    all_to_all x1, starting transfers between devices, exchange(): return lax.all_to_all(pieces, axes, split_axis=0, concat_axis=0, tiled=True)  6.74 us
    pallas_call x1, Pallas kernels, first_mix(): pl.pallas_call(functools.partial(first_kernel, groups), out_shape=jax.Sha...  5.13 us
  transfers between devices with their start and end apart: 12, of which 2 were waited for; matrix products, arithmetic and copies ran while one was open for 0% of the time, Pallas kernels for 6%

profile of v4, /device:TPU:25, one launch (start us, length us, event | category | flops | bytes accessed | tf_op | source)
XLA Modules:
  0.0 201.6 jit_solution(3486147945776684258)
XLA Ops:
  0.6 3.1 %pick_columns.3 = bf16[16,32,1792]{2,1,0:T(8,128)(2,1)} custom-call(s32[8,28]{1,0:T(8,128)} %order_ref.5, f32[32]{0:T(128)} %ffn_gain_ref.3, bf16[32,28672]{1,0:T(8,128)(2,1)} %ffn_ref.3), custom_call_target="tpu_custom_call" | custom-call | flops 367001600 | bytes 3670016 | tf_op jit(solution)/shard_map/pick_columns/pallas_call | solution.py:178
  3.8 0.0 copy-start.1
  3.8 0.0 copy-start.2
  3.8 6.7 %all-to-all-start.2 = ((bf16[16,32,1792]{2,1,0:T(8,128)(2,1)}), bf16[16,32,1792]{2,1,0:T(8,128)(2,1)}, u32[]{:S(2)}, u32[]{:S(2)}) async-start(bf16[16,32,1792]{2,1,0:T(8,128)(2,1)} %pick_columns.3), calls=%async_computation.2 | async-start | bytes 3670016 | tf_op jit(solution)/shard_map/all_to_all | solution.py:388
  10.5 0.0 copy-done.1
  10.5 0.0 copy-done.2
  10.5 2.9 %down_rotate.1 = (bf16[4,112,256]{2,1,0:T(8,128)(2,1)S(1)}, bf16[4,112,256]{2,1,0:T(8,128)(2,1)S(1)}, bf16[4,112,256]{2,1,0:T(8,128)(2,1)S(1)}, bf16[4,112,256]{...) custom-call(bf16[112,8192]{1,0:T(8,128)(2,1)S(1)} %copy-done.1, ...), custom_call_target="tpu_custom_call" | custom-call | flops 939524096 | bytes 3670016 | tf_op jit(solution)/shard_map/down_rotate/pallas_call | solution.py:103
  13.4 1.7 collective-permute-start
  15.1 4.1 %collective-permute-start.1 = (bf16[4,112,256]{2,1,0:T(8,128)(2,1)S(1)}, bf16[4,112,256]{2,1,0:T(8,128)(2,1)S(1)}, u32[]{:S(2)}, u32[]{:S(2)}) collective-permute-start(bf16[4,112,256]{2,1,0:T(8,128)(2,1)S(1)} %get-tuple-element.50), channel_id=1, source_target_pairs={{0,112},{16,0},{32,16},{48,32},{64,48},{80,64},{96,80},{112,96},{1... | collective-permute-start | bytes 688136 | tf_op jit(solution)/shard_map/ppermute | solution.py:399
  19.1 1.5 collective-permute-start.2
  20.7 3.0 %collective-permute-start.3 = (bf16[4,112,256]{2,1,0:T(8,128)(2,1)S(1)}, bf16[4,112,256]{2,1,0:T(8,128)(2,1)S(1)}, u32[]{:S(2)}, u32[]{:S(2)}) collective-permute-start(bf16[4,112,256]{2,1,0:T(8,128)(2,1)S(1)} %get-tuple-element.52), channel_id=1, source_target_pairs={{0,80},{16,96},{32,112},{48,0},{64,16},{80,32},{96,48},{112,64},{1... | collective-permute-start | bytes 688136 | tf_op jit(solution)/shard_map/ppermute | solution.py:399
  23.6 0.0 collective-permute-start.4
  23.6 0.3 collective-permute-done.refs_1_
  23.9 3.3 %collective-permute-start.5 = (bf16[4,112,256]{2,1,0:T(8,128)(2,1)S(1)}, bf16[4,112,256]{2,1,0:T(8,128)(2,1)S(1)}, u32[]{:S(2)}, u32[]{:S(2)}) collective-permute-start(bf16[4,112,256]{2,1,0:T(8,128)(2,1)S(1)} %get-tuple-element.54), channel_id=1, source_target_pairs={{0,96},{16,112},{32,0},{48,16},{64,32},{80,48},{96,64},{112,80},{1... | collective-permute-start | bytes 688136 | tf_op jit(solution)/shard_map/ppermute | solution.py:399
  27.2 0.0 collective-permute-done.1.refs_2_
  27.2 3.9 %collective-permute-start.6 = (bf16[4,112,256]{2,1,0:T(8,128)(2,1)S(1)}, bf16[4,112,256]{2,1,0:T(8,128)(2,1)S(1)}, u32[]{:S(2)}, u32[]{:S(2)}) collective-permute-start(bf16[4,112,256]{2,1,0:T(8,128)(2,1)S(1)} %get-tuple-element.55), channel_id=1, source_target_pairs={{0,64},{16,80},{32,96},{48,112},{64,0},{80,16},{96,32},{112,48},{1... | collective-permute-start | bytes 688136 | tf_op jit(solution)/shard_map/ppermute | solution.py:399
  31.1 3.6 %pick_columns.2 = bf16[16,32,2432]{2,1,0:T(8,128)(2,1)} custom-call(s32[8,28]{1,0:T(8,128)} %order_ref.5, f32[32]{0:T(128)} %ffn_gain_ref.3, bf16[32,28672]{1,0:T(8,128)(2,1)} %ffn_ref.2, s32[8,8]{1,0:T(8,128)} %refs_0_.1, f32[32]{0:T(128)} %refs_1_.1, bf16[32,8192]{1,0:T(8,128)(2,1)} %refs_2_.1, bf16[32,1024]{1,0:T(8,128)(2,1)} %refs_3_.1, ...), custom_call_target="tpu_custom_call" | custom-call | flops 498073600 | bytes 4980736 | tf_op jit(solution)/shard_map/pick_columns/pallas_call | solution.py:178
  34.7 0.0 all-to-all-done.2.gates_ref
  34.7 33.7 %conditional.2 = (bf16[16,32,2432]{2,1,0:T(8,128)(2,1)}) conditional(s32[]{:T(128)} %convert_element_type.4, () %tuple.26, bf16[16,32,2432]{2,1,0:T(8,128)(2,1)} %pick_columns.2), branch_computations={%region_0.0_spmd, %region_1.0_spmd} | conditional | bytes 4980744 | solution.py:392
  34.7 33.7 %all_to_all.13 = bf16[16,32,2432]{2,1,0:T(8,128)(2,1)} all-to-all(bf16[16,32,2432]{2,1,0:T(8,128)(2,1)} %param.1), channel_id=1, replica_groups=mesh['xh'=2,'z'=8,'core'=2,'xl'=2,'y'=4] {'xh','xl','y'}, dimensions={0} | all-to-all | bytes 4980736 | tf_op jit(solution)/shard_map/cond/branch_1_fun/all_to_all | solution.py:388
  68.4 0.0 collective-permute-done.2.refs_3_
  68.4 0.0 collective-permute-done.3.refs_4_
  68.4 0.0 collective-permute-done.4.refs_5_
  68.4 0.0 collective-permute-done.5.refs_6_
  68.5 0.0 collective-permute-done.6.refs_7_
  68.5 5.1 %first_mix.1 = bf16[16,32,4224]{2,1,0:T(8,128)(2,1)} custom-call(bf16[256,256]{1,0:T(8,128)(2,1)} %constant.17.clone.matrix_ref, bf16[16,32,1792]{2,1,0:T(8,128)(2,1)} %all-to-all-done.2.gates_ref, bf16[16,32,2432]{2,1,0:T(8,128)(2,1)} %get-tuple-element.81.rest_ref), custom_call_target="tpu_custom_call" | custom-call | flops 1107296256 | bytes 8650752 | tf_op jit(solution)/shard_map/first_mix/pallas_call | solution.py:244
  73.6 0.9 repack_down.1
  74.5 1.4 collective-permute-start.7
  75.8 6.2 %collective-permute-start.8 = (bf16[8,112,256]{2,1,0:T(8,128)(2,1)S(1)}, bf16[8,112,256]{2,1,0:T(8,128)(2,1)S(1)}, u32[]{:S(2)}, u32[]{:S(2)}) collective-permute-start(bf16[8,112,256]{2,1,0:T(8,128)(2,1)S(1)} %get-tuple-element.73), channel_id=1, source_target_pairs={{0,136},{8,128},{128,8},{136,0},{1,137},{9,129},{129,9},{137,1},{2... | collective-permute-start | bytes 1376264 | tf_op jit(solution)/shard_map/ppermute | solution.py:406
  82.0 106.6 %conditional.3 = (bf16[16,32,4224]{2,1,0:T(8,128)(2,1)}) conditional(s32[]{:T(128)} %convert_element_type.4, () %tuple.24, bf16[16,32,4224]{2,1,0:T(8,128)(2,1)} %first_mix.1), branch_computations={%region_2.0_spmd, %region_3.0_spmd} | conditional | bytes 8650760 | solution.py:392
  82.0 106.6 %all_to_all.14 = bf16[16,32,4224]{2,1,0:T(8,128)(2,1)} all-to-all(bf16[16,32,4224]{2,1,0:T(8,128)(2,1)} %param.3), channel_id=1, replica_groups=mesh['xh'=2,'z'=8,'core'=2,'xl'=2,'y'=4] {'xh','z'}, dimensions={0} | all-to-all | bytes 8650752 | tf_op jit(solution)/shard_map/cond/branch_1_fun/all_to_all | solution.py:388
  188.6 0.0 copy-start
  188.6 0.0 collective-permute-done.7.refs_2_
  188.6 0.0 collective-permute-done.8.refs_3_
  188.6 0.1 collective-permute-start.9
  188.8 0.5 collective-permute-start.10
  189.2 2.8 %own_sums.1.sums_ref = f32[8,32,4224]{2,1,0:T(8,128)S(1)} custom-call(bf16[16,32,4224]{2,1,0:T(8,128)(2,1)} %get-tuple-element.82.own_ref), custom_call_target="tpu_custom_call" | custom-call | flops 86507520 | bytes 8650752 | tf_op jit(solution)/shard_map/own_sums/pallas_call | solution.py:288
  192.1 3.5 %collective-permute-done.10.refs_1_ = bf16[8,112,256]{2,1,0:T(8,128)(2,1)S(1)} collective-permute-done((bf16[8,112,256]{2,1,0:T(8,128)(2,1)S(1)}, bf16[8,112,256]{2,1,0:T(8,128)(2,1)S(1)}, u32[]{:S(2)}, u32[]{:S(2)}) %collective-permute-start.10) | collective-permute-done | bytes 458784 | tf_op jit(solution)/shard_map/ppermute | solution.py:406
  195.6 0.0 copy-done
  195.6 2.6 %order_rows.1 = bf16[3584,256]{1,0:T(8,128)(2,1)} custom-call(s32[8,28]{1,0:T(8,128)S(1)} %copy-done, bf16[8,112,256]{2,1,0:T(8,128)(2,1)S(1)} %get-tuple-element.77.refs_0_, bf16[8,112,256]{2,1,0:T(8,128)(2,1)S(1)} %collective-permute-done.10.refs_1_, bf16[8,112,256]{2,1,0:T(8,128)(2,1)S(1)} %collective-permute-done.7.refs_2_, ...), custom_call_target="tpu_custom_call" | custom-call | flops 917504 | bytes 3670016 | tf_op jit(solution)/shard_map/order_rows/pallas_call | solution.py:375
  198.2 0.0 collective-permute-done.9.other_ref
  198.2 3.3 %last_mix.1 = (bf16[256,7168]{1,0:T(8,128)(2,1)}, bf16[256,1280]{1,0:T(8,128)(2,1)}) custom-call(f32[8,32,4224]{2,1,0:T(8,128)S(1)} %own_sums.1.sums_ref, bf16[16,32,4224]{2,1,0:T(8,128)(2,1)S(1)} %collective-permute-done.9.other_ref), custom_call_target="tpu_custom_call" | custom-call | flops 73400320 | bytes 11010048 | tf_op jit(solution)/shard_map/last_mix/pallas_call | solution.py:336
Async XLA Ops:
  3.8 6.7 %copy-start.1 = (bf16[112,8192]{1,0:T(8,128)(2,1)S(1)}, bf16[112,8192]{1,0:T(8,128)(2,1)}, u32[]{:S(2)}) copy-start(bf16[112,8192]{1,0:T(8,128)(2,1)} %weight_ref.1) | copy-start | bytes 5505028
  3.8 6.7 %copy-start.2 = (bf16[128,128]{1,0:T(8,128)(2,1)S(1)}, bf16[128,128]{1,0:T(8,128)(2,1)}, u32[]{:S(2)}) copy-start(bf16[128,128]{1,0:T(8,128)(2,1)} %constant.16.clone.sign_ref) | copy-start | bytes 98308
  3.8 31.0 %all-to-all-start.2 = ((bf16[16,32,1792]{2,1,0:T(8,128)(2,1)}), bf16[16,32,1792]{2,1,0:T(8,128)(2,1)}, u32[]{:S(2)}, u32[]{:S(2)}) async-start(bf16[16,32,1792]{2,1,0:T(8,128)(2,1)} %pick_columns.3), calls=%async_computation.2 | async-start | bytes 3670016 | tf_op jit(solution)/shard_map/all_to_all | solution.py:388
  13.4 10.5 %collective-permute-start = (bf16[4,112,256]{2,1,0:T(8,128)(2,1)S(1)}, bf16[4,112,256]{2,1,0:T(8,128)(2,1)S(1)}, u32[]{:S(2)}, u32[]{:S(2)}) collective-permute-start(bf16[4,112,256]{2,1,0:T(8,128)(2,1)S(1)} %get-tuple-element.49), channel_id=1, source_target_pairs={{0,16},{16,32},{32,48},{48,64},{64,80},{80,96},{96,112},{112,0},{1... | collective-permute-start | bytes 688136 | tf_op jit(solution)/shard_map/ppermute | solution.py:399
  15.1 12.1 %collective-permute-start.1 = (bf16[4,112,256]{2,1,0:T(8,128)(2,1)S(1)}, bf16[4,112,256]{2,1,0:T(8,128)(2,1)S(1)}, u32[]{:S(2)}, u32[]{:S(2)}) collective-permute-start(bf16[4,112,256]{2,1,0:T(8,128)(2,1)S(1)} %get-tuple-element.50), channel_id=1, source_target_pairs={{0,112},{16,0},{32,16},{48,32},{64,48},{80,64},{96,80},{112,96},{1... | collective-permute-start | bytes 688136 | tf_op jit(solution)/shard_map/ppermute | solution.py:399
  19.1 49.3 %collective-permute-start.2 = (bf16[4,112,256]{2,1,0:T(8,128)(2,1)S(1)}, bf16[4,112,256]{2,1,0:T(8,128)(2,1)S(1)}, u32[]{:S(2)}, u32[]{:S(2)}) collective-permute-start(bf16[4,112,256]{2,1,0:T(8,128)(2,1)S(1)} %get-tuple-element.51), channel_id=1, source_target_pairs={{0,48},{16,64},{32,80},{48,96},{64,112},{80,0},{96,16},{112,32},{1... | collective-permute-start | bytes 688136 | tf_op jit(solution)/shard_map/ppermute | solution.py:399
  20.7 47.8 %collective-permute-start.3 = (bf16[4,112,256]{2,1,0:T(8,128)(2,1)S(1)}, bf16[4,112,256]{2,1,0:T(8,128)(2,1)S(1)}, u32[]{:S(2)}, u32[]{:S(2)}) collective-permute-start(bf16[4,112,256]{2,1,0:T(8,128)(2,1)S(1)} %get-tuple-element.52), channel_id=1, source_target_pairs={{0,80},{16,96},{32,112},{48,0},{64,16},{80,32},{96,48},{112,64},{1... | collective-permute-start | bytes 688136 | tf_op jit(solution)/shard_map/ppermute | solution.py:399
  23.6 44.8 %collective-permute-start.4 = (bf16[4,112,256]{2,1,0:T(8,128)(2,1)S(1)}, bf16[4,112,256]{2,1,0:T(8,128)(2,1)S(1)}, u32[]{:S(2)}, u32[]{:S(2)}) collective-permute-start(bf16[4,112,256]{2,1,0:T(8,128)(2,1)S(1)} %get-tuple-element.53), channel_id=1, source_target_pairs={{0,32},{16,48},{32,64},{48,80},{64,96},{80,112},{96,0},{112,16},{1... | collective-permute-start | bytes 688136 | tf_op jit(solution)/shard_map/ppermute | solution.py:399
  23.9 44.6 %collective-permute-start.5 = (bf16[4,112,256]{2,1,0:T(8,128)(2,1)S(1)}, bf16[4,112,256]{2,1,0:T(8,128)(2,1)S(1)}, u32[]{:S(2)}, u32[]{:S(2)}) collective-permute-start(bf16[4,112,256]{2,1,0:T(8,128)(2,1)S(1)} %get-tuple-element.54), channel_id=1, source_target_pairs={{0,96},{16,112},{32,0},{48,16},{64,32},{80,48},{96,64},{112,80},{1... | collective-permute-start | bytes 688136 | tf_op jit(solution)/shard_map/ppermute | solution.py:399
  27.2 41.2 %collective-permute-start.6 = (bf16[4,112,256]{2,1,0:T(8,128)(2,1)S(1)}, bf16[4,112,256]{2,1,0:T(8,128)(2,1)S(1)}, u32[]{:S(2)}, u32[]{:S(2)}) collective-permute-start(bf16[4,112,256]{2,1,0:T(8,128)(2,1)S(1)} %get-tuple-element.55), channel_id=1, source_target_pairs={{0,64},{16,80},{32,96},{48,112},{64,0},{80,16},{96,32},{112,48},{1... | collective-permute-start | bytes 688136 | tf_op jit(solution)/shard_map/ppermute | solution.py:399
  74.5 114.1 %collective-permute-start.7 = (bf16[8,112,256]{2,1,0:T(8,128)(2,1)}, bf16[8,112,256]{2,1,0:T(8,128)(2,1)S(1)}, u32[]{:S(2)}, u32[]{:S(2)}) collective-permute-start(bf16[8,112,256]{2,1,0:T(8,128)(2,1)} %get-tuple-element.72), channel_id=1, source_target_pairs={{0,128},{8,136},{128,0},{136,8},{1,129},{9,137},{129,1},{137,9},{2... | collective-permute-start | bytes 1376264 | tf_op jit(solution)/shard_map/ppermute | solution.py:406
  75.8 112.8 %collective-permute-start.8 = (bf16[8,112,256]{2,1,0:T(8,128)(2,1)S(1)}, bf16[8,112,256]{2,1,0:T(8,128)(2,1)S(1)}, u32[]{:S(2)}, u32[]{:S(2)}) collective-permute-start(bf16[8,112,256]{2,1,0:T(8,128)(2,1)S(1)} %get-tuple-element.73), channel_id=1, source_target_pairs={{0,136},{8,128},{128,8},{136,0},{1,137},{9,129},{129,9},{137,1},{2... | collective-permute-start | bytes 1376264 | tf_op jit(solution)/shard_map/ppermute | solution.py:406
  188.6 7.0 %copy-start = (s32[8,28]{1,0:T(8,128)S(1)}, s32[8,28]{1,0:T(8,128)}, u32[]{:S(2)}) copy-start(s32[8,28]{1,0:T(8,128)} %order_ref.5) | copy-start | bytes 2692
  188.6 9.6 %collective-permute-start.9 = (bf16[16,32,4224]{2,1,0:T(8,128)(2,1)}, bf16[16,32,4224]{2,1,0:T(8,128)(2,1)S(1)}, u32[]{:S(2)}, u32[]{:S(2)}) collective-permute-start(bf16[16,32,4224]{2,1,0:T(8,128)(2,1)} %get-tuple-element.82.own_ref), channel_id=1, source_target_pairs={{0,8},{8,0},{1,9},{9,1},{2,10},{10,2},{3,11},{11,3},{4,12},{12,4},... | collective-permute-start | bytes 12976136 | tf_op jit(solution)/shard_map/ppermute | solution.py:411
  188.8 6.8 %collective-permute-start.10 = (bf16[8,112,256]{2,1,0:T(8,128)(2,1)S(1)}, bf16[8,112,256]{2,1,0:T(8,128)(2,1)S(1)}, u32[]{:S(2)}, u32[]{:S(2)}) collective-permute-start(bf16[8,112,256]{2,1,0:T(8,128)(2,1)S(1)} %get-tuple-element.78), channel_id=1, source_target_pairs={{0,8},{8,0},{128,136},{136,128},{1,9},{9,1},{129,137},{137,129},{2... | collective-permute-start | bytes 1376264 | tf_op jit(solution)/shard_map/ppermute | solution.py:406

commit v5 on v4

--- a/solution.py
+++ b/solution.py
@@ -257,98 +257,107 @@
     return (1 - 2 * lax.axis_index("core")).astype(jnp.float32)
 
 
-def side_sums(sign, ref, part, columns):
-    rows = [ref[part * 8 + j, :, columns].astype(jnp.float32) for j in range(8)]
-    rows = [rows[j] + sign * rows[j + 4] for j in range(4)]
-    return pair_sums(pair_sums(rows, 2), 1)
-
-
-def own_kernel(own_ref, out_ref, held, sems):
+def own_kernel(part, own_ref, mine_ref, send_ref, held, sem):
     sign = core_sign()
-    copies = [
-        pltpu.make_async_copy(
-            own_ref.at[pl.ds(part * 8, 8)], held.at[pl.ds(part * 8, 8)], sems.at[part]
-        )
-        for part in range(2)
-    ]
-    for copy in copies:
-        copy.start()
-    for part in range(2):
-        copies[part].wait()
-
-        @pl.loop(0, held.shape[2] // BLK)
-        def _(step):
-            columns = pl.ds(pl.multiple_of(step * BLK, BLK), BLK)
-            for j, value in enumerate(side_sums(sign, held, part, columns)):
-                out_ref[part * 4 + j, :, columns] = value
-
-
-def own_sums(own):
+    copy = pltpu.make_async_copy(own_ref.at[pl.ds(part * 8, 8)], held, sem)
+    copy.start()
+    copy.wait()
+
+    for step in range(0, held.shape[2], BLK):
+        columns = slice(step, step + BLK)
+        rows = [held[j, :, columns].astype(jnp.float32) for j in range(8)]
+        pairs = [(rows[j], sign * rows[j + 4]) for j in range(4)]
+        mine = pair_sums(pair_sums([low + high for low, high in pairs], 2), 1)
+        theirs = pair_sums(pair_sums([low - high for low, high in pairs], 2), 1)
+        for j in range(4):
+            mine_ref[j, :, columns] = mine[j]
+            send_ref[j, :, columns] = bf16(theirs[j])
+
+
+def own_sums(own, part):
     width = own.shape[2]
     return pl.pallas_call(
-        own_kernel,
-        out_shape=jax.ShapeDtypeStruct((8, ROWS, width), jnp.float32),
+        functools.partial(own_kernel, part),
+        out_shape=[
+            jax.ShapeDtypeStruct((4, ROWS, width), jnp.float32),
+            jax.ShapeDtypeStruct((4, ROWS, width), jnp.bfloat16),
+        ],
         in_specs=[pl.BlockSpec(memory_space=pl.ANY)],
-        out_specs=whole(1)[0],
-        scratch_shapes=[pltpu.VMEM(own.shape, jnp.bfloat16), pltpu.SemaphoreType.DMA((2,))],
+        out_specs=whole(2),
+        scratch_shapes=[pltpu.VMEM((8, ROWS, width), jnp.bfloat16), pltpu.SemaphoreType.DMA],
         compiler_params=params(),
-        cost_estimate=cost(40 * own.size, 4 * own.size),
+        cost_estimate=cost(20 * own.size, 3 * own.size),
         name="own_sums",
     )(own)
 
 
-def last_columns(sign, sums_ref, other_ref, part, columns):
-    theirs = side_sums(sign, other_ref, part, columns)
+def last_columns(sign, mine_ref, other_ref, columns):
     scale = 16.0 / math.sqrt(8192.0)
     parts = []
     for j in range(4):
-        mine = sums_ref[part * 4 + j, :, columns]
-        parts.append(bf16((mine + theirs[j]) * scale))
-        parts.append(bf16((mine - theirs[j]) * (scale * sign)))
+        mine, theirs = mine_ref[j, :, columns], other_ref[j, :, columns].astype(jnp.float32)
+        parts.append(bf16((mine + theirs) * scale))
+        parts.append(bf16((mine - theirs) * (scale * sign)))
     return jnp.concatenate(parts, axis=0)
 
 
-def last_kernel(sums_ref, other_ref, ffn_ref, heads_ref):
+def last_kernel(part, mine_ref, other_ref, *refs):
+    ffn_ref, heads_ref, ffn_held, heads_held, sems = refs[-5:]
     sign = core_sign()
-    part = pl.program_id(0) & 1
-    begin = (pl.program_id(0) >> 1) * HALF_F
-
-    for step in range(0, HALF_F, 2):
-        source = pl.ds(pl.multiple_of((begin + step) * BLK, 2 * BLK), 2 * BLK)
-        ffn_ref[:, step * BLK : (step + 2) * BLK] = last_columns(
-            sign, sums_ref, other_ref, part, source
-        )
-
-    @pl.when(pl.program_id(0) == 0)
-    def _():
-        for half in range(2):
-            for slot in range(HALF_Q + 1):
-                block = half * HALF_Q + slot if slot < HALF_Q else QPG + half
-                source = slice(2 * FFN_WIDTH + slot * BLK, 2 * FFN_WIDTH + (slot + 1) * BLK)
-                heads_ref[:, block * BLK : (block + 1) * BLK] = last_columns(
-                    sign, sums_ref, other_ref, half, source
-                )
-
-
-def last_mix(sums, other):
+    copies = []
+    for at in range(2):
+        there = pl.ds((2 * at + part) * FFN_WIDTH, FFN_WIDTH)
+        copies.append(
+            pltpu.make_async_copy(ffn_held.at[at], ffn_ref.at[:, there], sems.at[at])
+        )
+    for at, (start, count) in enumerate(((part * HALF_Q, HALF_Q), (QPG + part, 1))):
+        copies.append(
+            pltpu.make_async_copy(
+                heads_held.at[:, pl.ds(at * HALF_Q * BLK, count * BLK)],
+                heads_ref.at[:, pl.ds(start * BLK, count * BLK)],
+                sems.at[2 + at],
+            )
+        )
+    for at in range(2):
+        for step in range(0, FFN_WIDTH, 2 * BLK):
+            source = slice(at * FFN_WIDTH + step, at * FFN_WIDTH + step + 2 * BLK)
+            ffn_held[at, :, step : step + 2 * BLK] = last_columns(
+                sign, mine_ref, other_ref, source
+            )
+        copies[at].start()
+    for slot in range(HALF_Q + 1):
+        source = slice(2 * FFN_WIDTH + slot * BLK, 2 * FFN_WIDTH + (slot + 1) * BLK)
+        heads_held[:, slot * BLK : (slot + 1) * BLK] = last_columns(
+            sign, mine_ref, other_ref, source
+        )
+    for copy in copies[2:]:
+        copy.start()
+    for copy in copies:
+        copy.wait()
+
+
+def last_mix(mine, other, part, targets=()):
     rows = 8 * ROWS
     width = 4 * FFN_WIDTH
-    return pl.pallas_call(
-        last_kernel,
-        grid=(4,),
+    anywhere = pl.BlockSpec(memory_space=pl.ANY)
+    return pl.pallas_call(
+        functools.partial(last_kernel, part),
         out_shape=[
             jax.ShapeDtypeStruct((rows, width), jnp.bfloat16),
             jax.ShapeDtypeStruct((rows, 2 * HEADS_WIDTH), jnp.bfloat16),
         ],
-        in_specs=whole(2),
-        out_specs=[
-            pl.BlockSpec((rows, FFN_WIDTH), lambda i: (0, i)),
-            pl.BlockSpec((rows, 2 * HEADS_WIDTH), lambda i: (0, 0)),
+        in_specs=whole(2) + [anywhere] * len(targets),
+        out_specs=[anywhere] * 2,
+        input_output_aliases={2: 0, 3: 1} if targets else {},
+        scratch_shapes=[
+            pltpu.VMEM((2, rows, FFN_WIDTH), jnp.bfloat16),
+            pltpu.VMEM((rows, HEADS_WIDTH), jnp.bfloat16),
+            pltpu.SemaphoreType.DMA((4,)),
         ],
         compiler_params=params(),
-        cost_estimate=cost(40 * rows * width, 6 * rows * width),
+        cost_estimate=cost(20 * rows * width, 3 * rows * width),
         name="last_mix",
-    )(sums, other)
+    )(mine, other, *targets)
 
 
 def order_kernel(order_ref, *refs):
@@ -435,14 +444,17 @@
     shifted = exchange_z(rotate_down(down_weight, shards))
     rest, gates = tie(rest, gates)
     rest, *shifted = tie(exchange_apart(go, rest, PLANE), *shifted)
-    mixed, *packed = tie(first_mix(gates, rest), *repack(shifted))
-    mixed = exchange_apart(go, mixed, DEPTH)
-    moved = exchange_side(packed, (2, 3))
-    mixed, *moved = tie(mixed, *moved)
-    other = exchange_core(mixed)
-    moved = exchange_side(moved, (1,))
+    mixed = exchange(first_mix(gates, rest), DEPTH)
+    moved = exchange_side(repack(shifted), (2, 3, 1))
     merged_down = order_rows(ffn_order, moved)
-    merged_ffn, merged_attn = last_mix(own_sums(mixed), other)
+    mixed, merged_down = tie(mixed, merged_down)
+    mine, send = own_sums(mixed, 0)
+    other = exchange_core(send)
+    mixed, mine = tie(mixed, mine)
+    mine_next, send = own_sums(mixed, 1)
+    other_next = exchange_core(send)
+    merged = last_mix(mine, other, 0)
+    merged_ffn, merged_attn = last_mix(mine_next, other_next, 1, merged)
     return (merged_attn, merged_ffn, merged_down)
 
 

time: 204 us -> 194 us (0.951)
  blocking collectives: 140 us -> 33.7 us
  waiting for transfers between devices: 3.79 us -> 89.6 us
  starting transfers between devices: 32.3 us -> 41.4 us
    all_to_all x2 -> x1, blocking collectives: 140 us -> 33.7 us  [exchange(): return lax.all_to_all(pieces, axes, split_axis=0, concat_axis=0, tiled=True)]
    all_to_all x1 -> x2, waiting for transfers between devices: 0.01 us -> 48.9 us  [exchange(): return lax.all_to_all(pieces, axes, split_axis=0, concat_axis=0, tiled=True)]
    ppermute x3, waiting for transfers between devices: 3.51 us -> 39.2 us  [exchange_side(): lax.ppermute(pieces[r], ('xh', 'core'), [(i, i ^ r) for i in range(4)])]
    all_to_all x1 -> x2, starting transfers between devices: 6.74 us -> 14.2 us  [exchange(): return lax.all_to_all(pieces, axes, split_axis=0, concat_axis=0, tiled=True)]
    pallas_call x2 -> x4, Pallas kernels: 6.19 us -> 7.75 us  [the longest x2 4.68 us: own_sums(): pl.pallas_call(functools.partial(own_kernel, part), out_shape=[jax.ShapeD...]
  transfers between devices with their start and end apart: 12 -> 14, of which waited for: 2 -> 5; matrix products, arithmetic and copies ran while one was open for 0% -> 0% of each run, Pallas kernels for 6% -> 7%
where the time goes in v5:
time: 194 us; the launch traced here: 191 us
  waiting for transfers between devices  89.6 us (46%)
  starting transfers between devices  41.4 us (21%)
  blocking collectives  33.7 us (17%)
  Pallas kernels  25.3 us (13%)
    all_to_all x2, waiting for transfers between devices, exchange(): return lax.all_to_all(pieces, axes, split_axis=0, concat_axis=0, tiled=True)  48.9 us
    ppermute x3, waiting for transfers between devices, exchange_side(): lax.ppermute(pieces[r], ('xh', 'core'), [(i, i ^ r) for i in range(4)])  39.2 us
    all_to_all x1, blocking collectives, exchange(): return lax.all_to_all(pieces, axes, split_axis=0, concat_axis=0, tiled=True)  33.7 us
    ppermute x7, starting transfers between devices, exchange_z(): lax.ppermute(pieces[at], 'z', [(i, (i + s) % DEEP) for i in range(DEEP)])  17.5 us
    all_to_all x2, starting transfers between devices, exchange(): return lax.all_to_all(pieces, axes, split_axis=0, concat_axis=0, tiled=True)  14.2 us
    ppermute x3, starting transfers between devices, exchange_side(): lax.ppermute(pieces[r], ('xh', 'core'), [(i, i ^ r) for i in range(4)])  8.03 us
    pallas_call x2, Pallas kernels, pick(): pl.pallas_call(functools.partial(pick_kernel, bool(heads)), grid=(PIECES...  6.76 us
    pallas_call x1, Pallas kernels, first_mix(): pl.pallas_call(functools.partial(first_kernel, groups), out_shape=jax.Sha...  5.15 us
  transfers between devices with their start and end apart: 14, of which 5 were waited for; matrix products, arithmetic and copies ran while one was open for 0% of the time, Pallas kernels for 7%

profile of v5, /device:TPU:25, one launch (start us, length us, event | category | flops | bytes accessed | tf_op | source)
XLA Modules:
  0.0 190.8 jit_solution(326944174212056209)
XLA Ops:
  0.6 3.1 %pick_columns.3 = bf16[16,32,1792]{2,1,0:T(8,128)(2,1)} custom-call(s32[8,28]{1,0:T(8,128)} %order_ref.5, f32[32]{0:T(128)} %ffn_gain_ref.3, bf16[32,28672]{1,0:T(8,128)(2,1)} %ffn_ref.3), custom_call_target="tpu_custom_call" | custom-call | flops 367001600 | bytes 3670016 | tf_op jit(solution)/shard_map/pick_columns/pallas_call | solution.py:178
  3.8 0.0 copy-start.1
  3.8 0.0 copy-start.2
  3.8 6.7 %all-to-all-start.1 = ((bf16[16,32,1792]{2,1,0:T(8,128)(2,1)}), bf16[16,32,1792]{2,1,0:T(8,128)(2,1)}, u32[]{:S(2)}, u32[]{:S(2)}) async-start(bf16[16,32,1792]{2,1,0:T(8,128)(2,1)} %pick_columns.3), calls=%async_computation.1 | async-start | bytes 3670016 | tf_op jit(solution)/shard_map/all_to_all | solution.py:397
  10.5 0.0 copy-done.1
  10.5 0.0 copy-done.2
  10.5 2.8 %down_rotate.1 = (bf16[4,112,256]{2,1,0:T(8,128)(2,1)S(1)}, bf16[4,112,256]{2,1,0:T(8,128)(2,1)S(1)}, bf16[4,112,256]{2,1,0:T(8,128)(2,1)S(1)}, bf16[4,112,256]{...) custom-call(bf16[112,8192]{1,0:T(8,128)(2,1)S(1)} %copy-done.1, ...), custom_call_target="tpu_custom_call" | custom-call | flops 939524096 | bytes 3670016 | tf_op jit(solution)/shard_map/down_rotate/pallas_call | solution.py:103
  13.4 1.7 collective-permute-start
  15.1 4.0 %collective-permute-start.1 = (bf16[4,112,256]{2,1,0:T(8,128)(2,1)S(1)}, bf16[4,112,256]{2,1,0:T(8,128)(2,1)S(1)}, u32[]{:S(2)}, u32[]{:S(2)}) collective-permute-start(bf16[4,112,256]{2,1,0:T(8,128)(2,1)S(1)} %get-tuple-element.46), channel_id=1, source_target_pairs={{0,112},{16,0},{32,16},{48,32},{64,48},{80,64},{96,80},{112,96},{1... | collective-permute-start | bytes 688136 | tf_op jit(solution)/shard_map/ppermute | solution.py:408
  19.1 1.5 collective-permute-start.2
  20.6 3.0 %collective-permute-start.3 = (bf16[4,112,256]{2,1,0:T(8,128)(2,1)S(1)}, bf16[4,112,256]{2,1,0:T(8,128)(2,1)S(1)}, u32[]{:S(2)}, u32[]{:S(2)}) collective-permute-start(bf16[4,112,256]{2,1,0:T(8,128)(2,1)S(1)} %get-tuple-element.48), channel_id=1, source_target_pairs={{0,80},{16,96},{32,112},{48,0},{64,16},{80,32},{96,48},{112,64},{1... | collective-permute-start | bytes 688136 | tf_op jit(solution)/shard_map/ppermute | solution.py:408
  23.6 0.0 collective-permute-start.4
  23.6 0.2 collective-permute-done.refs_1_
  23.9 3.3 %collective-permute-start.5 = (bf16[4,112,256]{2,1,0:T(8,128)(2,1)S(1)}, bf16[4,112,256]{2,1,0:T(8,128)(2,1)S(1)}, u32[]{:S(2)}, u32[]{:S(2)}) collective-permute-start(bf16[4,112,256]{2,1,0:T(8,128)(2,1)S(1)} %get-tuple-element.50), channel_id=1, source_target_pairs={{0,96},{16,112},{32,0},{48,16},{64,32},{80,48},{96,64},{112,80},{1... | collective-permute-start | bytes 688136 | tf_op jit(solution)/shard_map/ppermute | solution.py:408
  27.2 0.0 collective-permute-done.1.refs_2_
  27.2 3.9 %collective-permute-start.6 = (bf16[4,112,256]{2,1,0:T(8,128)(2,1)S(1)}, bf16[4,112,256]{2,1,0:T(8,128)(2,1)S(1)}, u32[]{:S(2)}, u32[]{:S(2)}) collective-permute-start(bf16[4,112,256]{2,1,0:T(8,128)(2,1)S(1)} %get-tuple-element.51), channel_id=1, source_target_pairs={{0,64},{16,80},{32,96},{48,112},{64,0},{80,16},{96,32},{112,48},{1... | collective-permute-start | bytes 688136 | tf_op jit(solution)/shard_map/ppermute | solution.py:408
  31.1 3.6 %pick_columns.2 = bf16[16,32,2432]{2,1,0:T(8,128)(2,1)} custom-call(s32[8,28]{1,0:T(8,128)} %order_ref.5, f32[32]{0:T(128)} %ffn_gain_ref.3, bf16[32,28672]{1,0:T(8,128)(2,1)} %ffn_ref.2, s32[8,8]{1,0:T(8,128)} %refs_0_.1, f32[32]{0:T(128)} %refs_1_.1, bf16[32,8192]{1,0:T(8,128)(2,1)} %refs_2_.1, bf16[32,1024]{1,0:T(8,128)(2,1)} %refs_3_.1, ...), custom_call_target="tpu_custom_call" | custom-call | flops 498073600 | bytes 4980736 | tf_op jit(solution)/shard_map/pick_columns/pallas_call | solution.py:178
  34.7 0.0 all-to-all-done.1.gates_ref
  34.7 33.7 %conditional.1 = (bf16[16,32,2432]{2,1,0:T(8,128)(2,1)}) conditional(s32[]{:T(128)} %convert_element_type.3, () %tuple.19, bf16[16,32,2432]{2,1,0:T(8,128)(2,1)} %pick_columns.2), branch_computations={%region_0.0_spmd, %region_1.0_spmd} | conditional | bytes 4980744 | solution.py:401
  34.7 33.7 %all_to_all.14 = bf16[16,32,2432]{2,1,0:T(8,128)(2,1)} all-to-all(bf16[16,32,2432]{2,1,0:T(8,128)(2,1)} %param.1), channel_id=1, replica_groups=mesh['xh'=2,'z'=8,'core'=2,'xl'=2,'y'=4] {'xh','xl','y'}, dimensions={0} | all-to-all | bytes 4980736 | tf_op jit(solution)/shard_map/cond/branch_1_fun/all_to_all | solution.py:397
  68.4 0.0 collective-permute-done.2.refs_3_
  68.4 0.0 collective-permute-done.3.refs_4_
  68.4 0.0 collective-permute-done.4.refs_5_
  68.4 0.0 collective-permute-done.5.refs_6_
  68.4 0.0 collective-permute-done.6.refs_7_
  68.4 5.1 %first_mix.1 = bf16[16,32,4224]{2,1,0:T(8,128)(2,1)} custom-call(bf16[256,256]{1,0:T(8,128)(2,1)} %constant.15.clone.matrix_ref, bf16[16,32,1792]{2,1,0:T(8,128)(2,1)} %all-to-all-done.1.gates_ref, bf16[16,32,2432]{2,1,0:T(8,128)(2,1)} %get-tuple-element.77.rest_ref), custom_call_target="tpu_custom_call" | custom-call | flops 1107296256 | bytes 8650752 | tf_op jit(solution)/shard_map/first_mix/pallas_call | solution.py:244
  73.6 0.0 copy-start
  73.6 7.5 %all-to-all-start.2 = ((bf16[16,32,4224]{2,1,0:T(8,128)(2,1)}), bf16[16,32,4224]{2,1,0:T(8,128)(2,1)}, u32[]{:S(2)}, u32[]{:S(2)}) async-start(bf16[16,32,4224]{2,1,0:T(8,128)(2,1)} %first_mix.1), calls=%async_computation.2 | async-start | bytes 8650752 | tf_op jit(solution)/shard_map/all_to_all | solution.py:397
  81.1 0.1 repack_down.1
  81.2 4.7 %collective-permute-start.7 = (bf16[8,112,256]{2,1,0:T(8,128)(2,1)S(1)}, bf16[8,112,256]{2,1,0:T(8,128)(2,1)S(1)}, u32[]{:S(2)}, u32[]{:S(2)}) collective-permute-start(bf16[8,112,256]{2,1,0:T(8,128)(2,1)S(1)} %get-tuple-element.62), channel_id=1, source_target_pairs={{0,8},{8,0},{128,136},{136,128},{1,9},{9,1},{129,137},{137,129},{2... | collective-permute-start | bytes 1376264 | tf_op jit(solution)/shard_map/ppermute | solution.py:415
  85.9 3.1 %collective-permute-start.8 = (bf16[8,112,256]{2,1,0:T(8,128)(2,1)S(1)}, bf16[8,112,256]{2,1,0:T(8,128)(2,1)S(1)}, u32[]{:S(2)}, u32[]{:S(2)}) collective-permute-start(bf16[8,112,256]{2,1,0:T(8,128)(2,1)S(1)} %get-tuple-element.63), channel_id=1, source_target_pairs={{0,128},{8,136},{128,0},{136,8},{1,129},{9,137},{129,1},{137,9},{2... | collective-permute-start | bytes 1376264 | tf_op jit(solution)/shard_map/ppermute | solution.py:415
  89.0 0.2 collective-permute-start.9
  89.2 0.0 collective-permute-done.7.refs_1_
  89.2 21.2 %collective-permute-done.8.refs_2_ = bf16[8,112,256]{2,1,0:T(8,128)(2,1)S(1)} collective-permute-done((bf16[8,112,256]{2,1,0:T(8,128)(2,1)S(1)}, bf16[8,112,256]{2,1,0:T(8,128)(2,1)S(1)}, u32[]{:S(2)}, u32[]{:S(2)}) %collective-permute-start.8) | collective-permute-done | bytes 458784 | tf_op jit(solution)/shard_map/ppermute | solution.py:415
  110.5 18.0 %collective-permute-done.9.refs_3_ = bf16[8,112,256]{2,1,0:T(8,128)(2,1)S(1)} collective-permute-done((bf16[8,112,256]{2,1,0:T(8,128)(2,1)S(1)}, bf16[8,112,256]{2,1,0:T(8,128)(2,1)S(1)}, u32[]{:S(2)}, u32[]{:S(2)}) %collective-permute-start.9) | collective-permute-done | bytes 458784 | tf_op jit(solution)/shard_map/ppermute | solution.py:415
  128.5 0.0 copy-done
  128.5 2.6 %order_rows.1 = bf16[3584,256]{1,0:T(8,128)(2,1)} custom-call(s32[8,28]{1,0:T(8,128)S(1)} %copy-done, bf16[8,112,256]{2,1,0:T(8,128)(2,1)S(1)} %get-tuple-element.61.refs_0_, bf16[8,112,256]{2,1,0:T(8,128)(2,1)S(1)} %collective-permute-done.7.refs_1_, bf16[8,112,256]{2,1,0:T(8,128)(2,1)S(1)} %collective-permute-done.8.refs_2_, ...), custom_call_target="tpu_custom_call" | custom-call | flops 917504 | bytes 3670016 | tf_op jit(solution)/shard_map/order_rows/pallas_call | solution.py:384
  131.1 48.9 %all-to-all-done.2.own_ref = bf16[16,32,4224]{2,1,0:T(8,128)(2,1)} async-done(((bf16[16,32,4224]{2,1,0:T(8,128)(2,1)}), bf16[16,32,4224]{2,1,0:T(8,128)(2,1)}, u32[]{:S(2)}, u32[]{:S(2)}) %all-to-all-start.2) | async-done | bytes 4325408 | tf_op jit(solution)/shard_map/all_to_all | solution.py:397
  180.1 2.3 %own_sums.2 = (f32[4,32,4224]{2,1,0:T(8,128)S(1)}, bf16[4,32,4224]{2,1,0:T(8,128)(2,1)S(1)}) custom-call(bf16[16,32,4224]{2,1,0:T(8,128)(2,1)} %all-to-all-done.2.own_ref), custom_call_target="tpu_custom_call" | custom-call | flops 43253760 | bytes 6488064 | tf_op jit(solution)/shard_map/own_sums/pallas_call | solution.py:279
  182.4 1.6 collective-permute-start.11
  184.0 2.3 %own_sums.3 = (f32[4,32,4224]{2,1,0:T(8,128)S(1)}, bf16[4,32,4224]{2,1,0:T(8,128)(2,1)S(1)}) custom-call(bf16[16,32,4224]{2,1,0:T(8,128)(2,1)} %all-to-all-done.2.own_ref), custom_call_target="tpu_custom_call" | custom-call | flops 43253760 | bytes 6488064 | tf_op jit(solution)/shard_map/own_sums/pallas_call | solution.py:279
  186.3 0.1 collective-permute-start.10
  186.4 0.0 collective-permute-done.11.other_ref
  186.4 1.5 last_mix.2
  188.0 1.1 collective-permute-done.10.other_ref
  189.1 1.5 last_mix.3
Async XLA Ops:
  3.8 6.7 %copy-start.1 = (bf16[112,8192]{1,0:T(8,128)(2,1)S(1)}, bf16[112,8192]{1,0:T(8,128)(2,1)}, u32[]{:S(2)}) copy-start(bf16[112,8192]{1,0:T(8,128)(2,1)} %weight_ref.1) | copy-start | bytes 5505028
  3.8 6.7 %copy-start.2 = (bf16[128,128]{1,0:T(8,128)(2,1)S(1)}, bf16[128,128]{1,0:T(8,128)(2,1)}, u32[]{:S(2)}) copy-start(bf16[128,128]{1,0:T(8,128)(2,1)} %constant.14.clone.sign_ref) | copy-start | bytes 98308
  3.8 31.0 %all-to-all-start.1 = ((bf16[16,32,1792]{2,1,0:T(8,128)(2,1)}), bf16[16,32,1792]{2,1,0:T(8,128)(2,1)}, u32[]{:S(2)}, u32[]{:S(2)}) async-start(bf16[16,32,1792]{2,1,0:T(8,128)(2,1)} %pick_columns.3), calls=%async_computation.1 | async-start | bytes 3670016 | tf_op jit(solution)/shard_map/all_to_all | solution.py:397
  13.4 10.5 %collective-permute-start = (bf16[4,112,256]{2,1,0:T(8,128)(2,1)S(1)}, bf16[4,112,256]{2,1,0:T(8,128)(2,1)S(1)}, u32[]{:S(2)}, u32[]{:S(2)}) collective-permute-start(bf16[4,112,256]{2,1,0:T(8,128)(2,1)S(1)} %get-tuple-element.45), channel_id=1, source_target_pairs={{0,16},{16,32},{32,48},{48,64},{64,80},{80,96},{96,112},{112,0},{1... | collective-permute-start | bytes 688136 | tf_op jit(solution)/shard_map/ppermute | solution.py:408
  15.1 12.1 %collective-permute-start.1 = (bf16[4,112,256]{2,1,0:T(8,128)(2,1)S(1)}, bf16[4,112,256]{2,1,0:T(8,128)(2,1)S(1)}, u32[]{:S(2)}, u32[]{:S(2)}) collective-permute-start(bf16[4,112,256]{2,1,0:T(8,128)(2,1)S(1)} %get-tuple-element.46), channel_id=1, source_target_pairs={{0,112},{16,0},{32,16},{48,32},{64,48},{80,64},{96,80},{112,96},{1... | collective-permute-start | bytes 688136 | tf_op jit(solution)/shard_map/ppermute | solution.py:408
  19.1 49.3 %collective-permute-start.2 = (bf16[4,112,256]{2,1,0:T(8,128)(2,1)S(1)}, bf16[4,112,256]{2,1,0:T(8,128)(2,1)S(1)}, u32[]{:S(2)}, u32[]{:S(2)}) collective-permute-start(bf16[4,112,256]{2,1,0:T(8,128)(2,1)S(1)} %get-tuple-element.47), channel_id=1, source_target_pairs={{0,48},{16,64},{32,80},{48,96},{64,112},{80,0},{96,16},{112,32},{1... | collective-permute-start | bytes 688136 | tf_op jit(solution)/shard_map/ppermute | solution.py:408
  20.6 47.8 %collective-permute-start.3 = (bf16[4,112,256]{2,1,0:T(8,128)(2,1)S(1)}, bf16[4,112,256]{2,1,0:T(8,128)(2,1)S(1)}, u32[]{:S(2)}, u32[]{:S(2)}) collective-permute-start(bf16[4,112,256]{2,1,0:T(8,128)(2,1)S(1)} %get-tuple-element.48), channel_id=1, source_target_pairs={{0,80},{16,96},{32,112},{48,0},{64,16},{80,32},{96,48},{112,64},{1... | collective-permute-start | bytes 688136 | tf_op jit(solution)/shard_map/ppermute | solution.py:408
  23.6 44.8 %collective-permute-start.4 = (bf16[4,112,256]{2,1,0:T(8,128)(2,1)S(1)}, bf16[4,112,256]{2,1,0:T(8,128)(2,1)S(1)}, u32[]{:S(2)}, u32[]{:S(2)}) collective-permute-start(bf16[4,112,256]{2,1,0:T(8,128)(2,1)S(1)} %get-tuple-element.49), channel_id=1, source_target_pairs={{0,32},{16,48},{32,64},{48,80},{64,96},{80,112},{96,0},{112,16},{1... | collective-permute-start | bytes 688136 | tf_op jit(solution)/shard_map/ppermute | solution.py:408
  23.9 44.6 %collective-permute-start.5 = (bf16[4,112,256]{2,1,0:T(8,128)(2,1)S(1)}, bf16[4,112,256]{2,1,0:T(8,128)(2,1)S(1)}, u32[]{:S(2)}, u32[]{:S(2)}) collective-permute-start(bf16[4,112,256]{2,1,0:T(8,128)(2,1)S(1)} %get-tuple-element.50), channel_id=1, source_target_pairs={{0,96},{16,112},{32,0},{48,16},{64,32},{80,48},{96,64},{112,80},{1... | collective-permute-start | bytes 688136 | tf_op jit(solution)/shard_map/ppermute | solution.py:408
  27.2 41.2 %collective-permute-start.6 = (bf16[4,112,256]{2,1,0:T(8,128)(2,1)S(1)}, bf16[4,112,256]{2,1,0:T(8,128)(2,1)S(1)}, u32[]{:S(2)}, u32[]{:S(2)}) collective-permute-start(bf16[4,112,256]{2,1,0:T(8,128)(2,1)S(1)} %get-tuple-element.51), channel_id=1, source_target_pairs={{0,64},{16,80},{32,96},{48,112},{64,0},{80,16},{96,32},{112,48},{1... | collective-permute-start | bytes 688136 | tf_op jit(solution)/shard_map/ppermute | solution.py:408
  73.6 54.9 %copy-start = (s32[8,28]{1,0:T(8,128)S(1)}, s32[8,28]{1,0:T(8,128)}, u32[]{:S(2)}) copy-start(s32[8,28]{1,0:T(8,128)} %order_ref.5) | copy-start | bytes 2692
  73.6 106.4 %all-to-all-start.2 = ((bf16[16,32,4224]{2,1,0:T(8,128)(2,1)}), bf16[16,32,4224]{2,1,0:T(8,128)(2,1)}, u32[]{:S(2)}, u32[]{:S(2)}) async-start(bf16[16,32,4224]{2,1,0:T(8,128)(2,1)} %first_mix.1), calls=%async_computation.2 | async-start | bytes 8650752 | tf_op jit(solution)/shard_map/all_to_all | solution.py:397
  81.2 8.0 %collective-permute-start.7 = (bf16[8,112,256]{2,1,0:T(8,128)(2,1)S(1)}, bf16[8,112,256]{2,1,0:T(8,128)(2,1)S(1)}, u32[]{:S(2)}, u32[]{:S(2)}) collective-permute-start(bf16[8,112,256]{2,1,0:T(8,128)(2,1)S(1)} %get-tuple-element.62), channel_id=1, source_target_pairs={{0,8},{8,0},{128,136},{136,128},{1,9},{9,1},{129,137},{137,129},{2... | collective-permute-start | bytes 1376264 | tf_op jit(solution)/shard_map/ppermute | solution.py:415
  85.9 24.6 %collective-permute-start.8 = (bf16[8,112,256]{2,1,0:T(8,128)(2,1)S(1)}, bf16[8,112,256]{2,1,0:T(8,128)(2,1)S(1)}, u32[]{:S(2)}, u32[]{:S(2)}) collective-permute-start(bf16[8,112,256]{2,1,0:T(8,128)(2,1)S(1)} %get-tuple-element.63), channel_id=1, source_target_pairs={{0,128},{8,136},{128,0},{136,8},{1,129},{9,137},{129,1},{137,9},{2... | collective-permute-start | bytes 1376264 | tf_op jit(solution)/shard_map/ppermute | solution.py:415
  89.0 39.5 %collective-permute-start.9 = (bf16[8,112,256]{2,1,0:T(8,128)(2,1)S(1)}, bf16[8,112,256]{2,1,0:T(8,128)(2,1)S(1)}, u32[]{:S(2)}, u32[]{:S(2)}) collective-permute-start(bf16[8,112,256]{2,1,0:T(8,128)(2,1)S(1)} %get-tuple-element.64), channel_id=1, source_target_pairs={{0,136},{8,128},{128,8},{136,0},{1,137},{9,129},{129,9},{137,1},{2... | collective-permute-start | bytes 1376264 | tf_op jit(solution)/shard_map/ppermute | solution.py:415
  182.4 4.0 %collective-permute-start.11 = (bf16[4,32,4224]{2,1,0:T(8,128)(2,1)S(1)}, bf16[4,32,4224]{2,1,0:T(8,128)(2,1)S(1)}, u32[]{:S(2)}, u32[]{:S(2)}) collective-permute-start(bf16[4,32,4224]{2,1,0:T(8,128)(2,1)S(1)} %get-tuple-element.71), channel_id=1, source_target_pairs={{0,8},{8,0},{1,9},{9,1},{2,10},{10,2},{3,11},{11,3},{4,12},{12,4},... | collective-permute-start | bytes 3244040 | tf_op jit(solution)/shard_map/ppermute | solution.py:420
  186.3 2.8 %collective-permute-start.10 = (bf16[4,32,4224]{2,1,0:T(8,128)(2,1)S(1)}, bf16[4,32,4224]{2,1,0:T(8,128)(2,1)S(1)}, u32[]{:S(2)}, u32[]{:S(2)}) collective-permute-start(bf16[4,32,4224]{2,1,0:T(8,128)(2,1)S(1)} %get-tuple-element.69), channel_id=1, source_target_pairs={{0,8},{8,0},{1,9},{9,1},{2,10},{10,2},{3,11},{11,3},{4,12},{12,4},... | collective-permute-start | bytes 3244040 | tf_op jit(solution)/shard_map/ppermute | solution.py:420

commit v6 on v5

--- a/solution.py
+++ b/solution.py
@@ -187,17 +187,9 @@
     )(order, gain, weight, *heads)
 
 
-def column_groups(widths, count):
-    groups, begin = [], 0
-    for at, width in enumerate(widths):
-        step = -(-width // (count * BLK)) * BLK
-        for start in range(0, width, step):
-            groups.append((at, start, min(step, width - start), begin + start))
-        begin += width
-    return groups
-
-
-def first_kernel(groups, matrix_ref, gates_ref, rest_ref, out_ref, in_held, out_held, in_sems, out_sems):
+def first_kernel(
+    groups, matrix_ref, gates_ref, rest_ref, out_ref, held, in_held, out_held, sem, in_sems, out_sems
+):
     in_copies, out_copies = [], []
     for at, (array, start, width, begin) in enumerate(groups):
         source = (gates_ref, rest_ref)[array].at[:, :, pl.ds(start, width)]
@@ -210,9 +202,12 @@
                 out_held.at[:, :, there], out_ref.at[:, :, there], out_sems.at[at]
             )
         )
+    whole_matrix = pltpu.make_async_copy(matrix_ref, held, sem)
+    whole_matrix.start()
     for copy in in_copies:
         copy.start()
-    matrix = matrix_ref[...]
+    whole_matrix.wait()
+    matrix = held[...]
     for at, (_, _, width, begin) in enumerate(groups):
         in_copies[at].wait()
         for start in range(begin, begin + width, 2 * BLK):
@@ -236,17 +231,28 @@
 
 def first_mix(gates, rest):
     rows = 8 * ROWS
-    widths = (gates.shape[2], rest.shape[2])
-    width = sum(widths)
-    groups = column_groups(widths, 2)
+    width = gates.shape[2] + rest.shape[2]
+    groups = []
+    for array, blocks in ((0, 4), (0, 10), (1, 10), (1, 6), (1, 3)):
+        begin = sum(group[2] for group in groups)
+        start = begin - array * gates.shape[2]
+        groups.append((array, start, blocks * BLK, begin))
+    assert sum(group[2] for group in groups) == width
     held = pltpu.VMEM((PIECES, ROWS, width), jnp.bfloat16)
     sems = pltpu.SemaphoreType.DMA((len(groups),))
     return pl.pallas_call(
         functools.partial(first_kernel, groups),
         out_shape=jax.ShapeDtypeStruct((PIECES, ROWS, width), jnp.bfloat16),
-        in_specs=whole(1) + [pl.BlockSpec(memory_space=pl.ANY)] * 2,
+        in_specs=[pl.BlockSpec(memory_space=pl.ANY)] * 3,
         out_specs=pl.BlockSpec(memory_space=pl.ANY),
-        scratch_shapes=[held, held, sems, sems],
+        scratch_shapes=[
+            pltpu.VMEM((rows, rows), jnp.bfloat16),
+            held,
+            held,
+            pltpu.SemaphoreType.DMA,
+            sems,
+            sems,
+        ],
         compiler_params=params(VMEM_MOST),
         cost_estimate=cost(4 * rows * rows * width, 8 * rows * width),
         name="first_mix",
@@ -257,13 +263,20 @@
     return (1 - 2 * lax.axis_index("core")).astype(jnp.float32)
 
 
-def own_kernel(part, own_ref, mine_ref, send_ref, held, sem):
+def own_kernel(part, own_ref, mine_ref, send_ref, held, sems):
     sign = core_sign()
-    copy = pltpu.make_async_copy(own_ref.at[pl.ds(part * 8, 8)], held, sem)
-    copy.start()
-    copy.wait()
+    third = held.shape[2] // 3
+    copies = []
+    for at in range(3):
+        there = pl.ds(at * third, third)
+        source = own_ref.at[pl.ds(part * 8, 8), :, there]
+        copies.append(pltpu.make_async_copy(source, held.at[:, :, there], sems.at[at]))
+    for copy in copies:
+        copy.start()
 
     for step in range(0, held.shape[2], BLK):
+        if step % third == 0:
+            copies[step // third].wait()
         columns = slice(step, step + BLK)
         rows = [held[j, :, columns].astype(jnp.float32) for j in range(8)]
         pairs = [(rows[j], sign * rows[j + 4]) for j in range(4)]
@@ -284,7 +297,7 @@
         ],
         in_specs=[pl.BlockSpec(memory_space=pl.ANY)],
         out_specs=whole(2),
-        scratch_shapes=[pltpu.VMEM((8, ROWS, width), jnp.bfloat16), pltpu.SemaphoreType.DMA],
+        scratch_shapes=[pltpu.VMEM((8, ROWS, width), jnp.bfloat16), pltpu.SemaphoreType.DMA((3,))],
         compiler_params=params(),
         cost_estimate=cost(20 * own.size, 3 * own.size),
         name="own_sums",

time: 194 us -> 193 us (level)
  transfers between devices with their start and end apart: 14 -> 14, of which waited for: 5 -> 6; matrix products, arithmetic and copies ran while one was open for 0% -> 0% of each run, Pallas kernels for 7% -> 7%
where the time goes in v6:
time: 193 us; the launch traced here: 190 us
  waiting for transfers between devices  89.6 us (46%)
  starting transfers between devices  41.4 us (21%)
  blocking collectives  33.7 us (17%)
  Pallas kernels  24.2 us (13%)
    all_to_all x2, waiting for transfers between devices, exchange(): return lax.all_to_all(pieces, axes, split_axis=0, concat_axis=0, tiled=True)  48.9 us
    ppermute x3, waiting for transfers between devices, exchange_side(): lax.ppermute(pieces[r], ('xh', 'core'), [(i, i ^ r) for i in range(4)])  39.2 us
    all_to_all x1, blocking collectives, exchange(): return lax.all_to_all(pieces, axes, split_axis=0, concat_axis=0, tiled=True)  33.7 us
    ppermute x7, starting transfers between devices, exchange_z(): lax.ppermute(pieces[at], 'z', [(i, (i + s) % DEEP) for i in range(DEEP)])  17.5 us
    all_to_all x2, starting transfers between devices, exchange(): return lax.all_to_all(pieces, axes, split_axis=0, concat_axis=0, tiled=True)  14.2 us
    ppermute x3, starting transfers between devices, exchange_side(): lax.ppermute(pieces[r], ('xh', 'core'), [(i, i ^ r) for i in range(4)])  8.03 us
    pallas_call x2, Pallas kernels, pick(): pl.pallas_call(functools.partial(pick_kernel, bool(heads)), grid=(PIECES...  6.76 us
    pallas_call x1, Pallas kernels, first_mix(): pl.pallas_call(functools.partial(first_kernel, groups), out_shape=jax.Sha...  5.02 us
  transfers between devices with their start and end apart: 14, of which 6 were waited for; matrix products, arithmetic and copies ran while one was open for 0% of the time, Pallas kernels for 7%

profile of v6, /device:TPU:25, one launch (start us, length us, event | category | flops | bytes accessed | tf_op | source)
XLA Modules:
  0.0 189.8 jit_solution(9005646198698784508)
XLA Ops:
  0.6 3.1 %pick_columns.3 = bf16[16,32,1792]{2,1,0:T(8,128)(2,1)} custom-call(s32[8,28]{1,0:T(8,128)} %order_ref.5, f32[32]{0:T(128)} %ffn_gain_ref.3, bf16[32,28672]{1,0:T(8,128)(2,1)} %ffn_ref.3), custom_call_target="tpu_custom_call" | custom-call | flops 367001600 | bytes 3670016 | tf_op jit(solution)/shard_map/pick_columns/pallas_call | solution.py:178
  3.8 0.0 copy-start.1
  3.8 0.0 copy-start.2
  3.8 6.7 %all-to-all-start.1 = ((bf16[16,32,1792]{2,1,0:T(8,128)(2,1)}), bf16[16,32,1792]{2,1,0:T(8,128)(2,1)}, u32[]{:S(2)}, u32[]{:S(2)}) async-start(bf16[16,32,1792]{2,1,0:T(8,128)(2,1)} %pick_columns.3), calls=%async_computation.1 | async-start | bytes 3670016 | tf_op jit(solution)/shard_map/all_to_all | solution.py:410
  10.5 0.0 copy-done.1
  10.5 0.0 copy-done.2
  10.5 2.8 %down_rotate.1 = (bf16[4,112,256]{2,1,0:T(8,128)(2,1)S(1)}, bf16[4,112,256]{2,1,0:T(8,128)(2,1)S(1)}, bf16[4,112,256]{2,1,0:T(8,128)(2,1)S(1)}, bf16[4,112,256]{...) custom-call(bf16[112,8192]{1,0:T(8,128)(2,1)S(1)} %copy-done.1, ...), custom_call_target="tpu_custom_call" | custom-call | flops 939524096 | bytes 3670016 | tf_op jit(solution)/shard_map/down_rotate/pallas_call | solution.py:103
  13.4 1.7 collective-permute-start
  15.1 4.0 %collective-permute-start.1 = (bf16[4,112,256]{2,1,0:T(8,128)(2,1)S(1)}, bf16[4,112,256]{2,1,0:T(8,128)(2,1)S(1)}, u32[]{:S(2)}, u32[]{:S(2)}) collective-permute-start(bf16[4,112,256]{2,1,0:T(8,128)(2,1)S(1)} %get-tuple-element.46), channel_id=1, source_target_pairs={{0,112},{16,0},{32,16},{48,32},{64,48},{80,64},{96,80},{112,96},{1... | collective-permute-start | bytes 688136 | tf_op jit(solution)/shard_map/ppermute | solution.py:421
  19.1 1.5 collective-permute-start.2
  20.6 3.0 %collective-permute-start.3 = (bf16[4,112,256]{2,1,0:T(8,128)(2,1)S(1)}, bf16[4,112,256]{2,1,0:T(8,128)(2,1)S(1)}, u32[]{:S(2)}, u32[]{:S(2)}) collective-permute-start(bf16[4,112,256]{2,1,0:T(8,128)(2,1)S(1)} %get-tuple-element.48), channel_id=1, source_target_pairs={{0,80},{16,96},{32,112},{48,0},{64,16},{80,32},{96,48},{112,64},{1... | collective-permute-start | bytes 688136 | tf_op jit(solution)/shard_map/ppermute | solution.py:421
  23.6 0.0 collective-permute-start.4
  23.6 0.2 collective-permute-done.refs_1_
  23.9 3.3 %collective-permute-start.5 = (bf16[4,112,256]{2,1,0:T(8,128)(2,1)S(1)}, bf16[4,112,256]{2,1,0:T(8,128)(2,1)S(1)}, u32[]{:S(2)}, u32[]{:S(2)}) collective-permute-start(bf16[4,112,256]{2,1,0:T(8,128)(2,1)S(1)} %get-tuple-element.50), channel_id=1, source_target_pairs={{0,96},{16,112},{32,0},{48,16},{64,32},{80,48},{96,64},{112,80},{1... | collective-permute-start | bytes 688136 | tf_op jit(solution)/shard_map/ppermute | solution.py:421
  27.2 0.0 collective-permute-done.1.refs_2_
  27.2 3.9 %collective-permute-start.6 = (bf16[4,112,256]{2,1,0:T(8,128)(2,1)S(1)}, bf16[4,112,256]{2,1,0:T(8,128)(2,1)S(1)}, u32[]{:S(2)}, u32[]{:S(2)}) collective-permute-start(bf16[4,112,256]{2,1,0:T(8,128)(2,1)S(1)} %get-tuple-element.51), channel_id=1, source_target_pairs={{0,64},{16,80},{32,96},{48,112},{64,0},{80,16},{96,32},{112,48},{1... | collective-permute-start | bytes 688136 | tf_op jit(solution)/shard_map/ppermute | solution.py:421
  31.1 3.6 %pick_columns.2 = bf16[16,32,2432]{2,1,0:T(8,128)(2,1)} custom-call(s32[8,28]{1,0:T(8,128)} %order_ref.5, f32[32]{0:T(128)} %ffn_gain_ref.3, bf16[32,28672]{1,0:T(8,128)(2,1)} %ffn_ref.2, s32[8,8]{1,0:T(8,128)} %refs_0_.1, f32[32]{0:T(128)} %refs_1_.1, bf16[32,8192]{1,0:T(8,128)(2,1)} %refs_2_.1, bf16[32,1024]{1,0:T(8,128)(2,1)} %refs_3_.1, ...), custom_call_target="tpu_custom_call" | custom-call | flops 498073600 | bytes 4980736 | tf_op jit(solution)/shard_map/pick_columns/pallas_call | solution.py:178
  34.7 0.0 all-to-all-done.1.gates_ref
  34.7 33.7 %conditional.1 = (bf16[16,32,2432]{2,1,0:T(8,128)(2,1)}) conditional(s32[]{:T(128)} %convert_element_type.3, () %tuple.19, bf16[16,32,2432]{2,1,0:T(8,128)(2,1)} %pick_columns.2), branch_computations={%region_0.0_spmd, %region_1.0_spmd} | conditional | bytes 4980744 | solution.py:414
  34.7 33.7 %all_to_all.14 = bf16[16,32,2432]{2,1,0:T(8,128)(2,1)} all-to-all(bf16[16,32,2432]{2,1,0:T(8,128)(2,1)} %param.1), channel_id=1, replica_groups=mesh['xh'=2,'z'=8,'core'=2,'xl'=2,'y'=4] {'xh','xl','y'}, dimensions={0} | all-to-all | bytes 4980736 | tf_op jit(solution)/shard_map/cond/branch_1_fun/all_to_all | solution.py:410
  68.4 0.0 collective-permute-done.2.refs_3_
  68.4 0.0 collective-permute-done.3.refs_4_
  68.4 0.0 collective-permute-done.4.refs_5_
  68.4 0.0 collective-permute-done.5.refs_6_
  68.4 0.0 collective-permute-done.6.refs_7_
  68.4 5.0 %first_mix.1 = bf16[16,32,4224]{2,1,0:T(8,128)(2,1)} custom-call(bf16[256,256]{1,0:T(8,128)(2,1)} %constant.15.clone.matrix_ref, bf16[16,32,1792]{2,1,0:T(8,128)(2,1)} %all-to-all-done.1.gates_ref, bf16[16,32,2432]{2,1,0:T(8,128)(2,1)} %get-tuple-element.77.rest_ref), custom_call_target="tpu_custom_call" | custom-call | flops 1107296256 | bytes 8650752 | tf_op jit(solution)/shard_map/first_mix/pallas_call | solution.py:243
  73.5 0.0 copy-start
  73.5 7.5 %all-to-all-start.2 = ((bf16[16,32,4224]{2,1,0:T(8,128)(2,1)}), bf16[16,32,4224]{2,1,0:T(8,128)(2,1)}, u32[]{:S(2)}, u32[]{:S(2)}) async-start(bf16[16,32,4224]{2,1,0:T(8,128)(2,1)} %first_mix.1), calls=%async_computation.2 | async-start | bytes 8650752 | tf_op jit(solution)/shard_map/all_to_all | solution.py:410
  80.9 0.1 repack_down.1
  81.1 4.7 %collective-permute-start.7 = (bf16[8,112,256]{2,1,0:T(8,128)(2,1)S(1)}, bf16[8,112,256]{2,1,0:T(8,128)(2,1)S(1)}, u32[]{:S(2)}, u32[]{:S(2)}) collective-permute-start(bf16[8,112,256]{2,1,0:T(8,128)(2,1)S(1)} %get-tuple-element.62), channel_id=1, source_target_pairs={{0,8},{8,0},{128,136},{136,128},{1,9},{9,1},{129,137},{137,129},{2... | collective-permute-start | bytes 1376264 | tf_op jit(solution)/shard_map/ppermute | solution.py:428
  85.7 3.1 %collective-permute-start.8 = (bf16[8,112,256]{2,1,0:T(8,128)(2,1)S(1)}, bf16[8,112,256]{2,1,0:T(8,128)(2,1)S(1)}, u32[]{:S(2)}, u32[]{:S(2)}) collective-permute-start(bf16[8,112,256]{2,1,0:T(8,128)(2,1)S(1)} %get-tuple-element.63), channel_id=1, source_target_pairs={{0,128},{8,136},{128,0},{136,8},{1,129},{9,137},{129,1},{137,9},{2... | collective-permute-start | bytes 1376264 | tf_op jit(solution)/shard_map/ppermute | solution.py:428
  88.9 0.2 collective-permute-start.9
  89.1 0.0 collective-permute-done.7.refs_1_
  89.1 21.2 %collective-permute-done.8.refs_2_ = bf16[8,112,256]{2,1,0:T(8,128)(2,1)S(1)} collective-permute-done((bf16[8,112,256]{2,1,0:T(8,128)(2,1)S(1)}, bf16[8,112,256]{2,1,0:T(8,128)(2,1)S(1)}, u32[]{:S(2)}, u32[]{:S(2)}) %collective-permute-start.8) | collective-permute-done | bytes 458784 | tf_op jit(solution)/shard_map/ppermute | solution.py:428
  110.3 18.0 %collective-permute-done.9.refs_3_ = bf16[8,112,256]{2,1,0:T(8,128)(2,1)S(1)} collective-permute-done((bf16[8,112,256]{2,1,0:T(8,128)(2,1)S(1)}, bf16[8,112,256]{2,1,0:T(8,128)(2,1)S(1)}, u32[]{:S(2)}, u32[]{:S(2)}) %collective-permute-start.9) | collective-permute-done | bytes 458784 | tf_op jit(solution)/shard_map/ppermute | solution.py:428
  128.3 0.0 copy-done
  128.3 2.6 %order_rows.1 = bf16[3584,256]{1,0:T(8,128)(2,1)} custom-call(s32[8,28]{1,0:T(8,128)S(1)} %copy-done, bf16[8,112,256]{2,1,0:T(8,128)(2,1)S(1)} %get-tuple-element.61.refs_0_, bf16[8,112,256]{2,1,0:T(8,128)(2,1)S(1)} %collective-permute-done.7.refs_1_, bf16[8,112,256]{2,1,0:T(8,128)(2,1)S(1)} %collective-permute-done.8.refs_2_, ...), custom_call_target="tpu_custom_call" | custom-call | flops 917504 | bytes 3670016 | tf_op jit(solution)/shard_map/order_rows/pallas_call | solution.py:397
  131.0 48.9 %all-to-all-done.2.own_ref = bf16[16,32,4224]{2,1,0:T(8,128)(2,1)} async-done(((bf16[16,32,4224]{2,1,0:T(8,128)(2,1)}), bf16[16,32,4224]{2,1,0:T(8,128)(2,1)}, u32[]{:S(2)}, u32[]{:S(2)}) %all-to-all-start.2) | async-done | bytes 4325408 | tf_op jit(solution)/shard_map/all_to_all | solution.py:410
  179.9 1.9 own_sums.2
  181.8 1.6 collective-permute-start.11
  183.4 1.9 own_sums.3
  185.3 0.1 collective-permute-start.10
  185.4 0.4 collective-permute-done.11.other_ref
  185.7 1.5 last_mix.2
  187.3 0.8 collective-permute-done.10.other_ref
  188.1 1.5 last_mix.3
Async XLA Ops:
  3.8 6.7 %copy-start.1 = (bf16[112,8192]{1,0:T(8,128)(2,1)S(1)}, bf16[112,8192]{1,0:T(8,128)(2,1)}, u32[]{:S(2)}) copy-start(bf16[112,8192]{1,0:T(8,128)(2,1)} %weight_ref.1) | copy-start | bytes 5505028
  3.8 6.7 %copy-start.2 = (bf16[128,128]{1,0:T(8,128)(2,1)S(1)}, bf16[128,128]{1,0:T(8,128)(2,1)}, u32[]{:S(2)}) copy-start(bf16[128,128]{1,0:T(8,128)(2,1)} %constant.14.clone.sign_ref) | copy-start | bytes 98308
  3.8 31.0 %all-to-all-start.1 = ((bf16[16,32,1792]{2,1,0:T(8,128)(2,1)}), bf16[16,32,1792]{2,1,0:T(8,128)(2,1)}, u32[]{:S(2)}, u32[]{:S(2)}) async-start(bf16[16,32,1792]{2,1,0:T(8,128)(2,1)} %pick_columns.3), calls=%async_computation.1 | async-start | bytes 3670016 | tf_op jit(solution)/shard_map/all_to_all | solution.py:410
  13.4 10.5 %collective-permute-start = (bf16[4,112,256]{2,1,0:T(8,128)(2,1)S(1)}, bf16[4,112,256]{2,1,0:T(8,128)(2,1)S(1)}, u32[]{:S(2)}, u32[]{:S(2)}) collective-permute-start(bf16[4,112,256]{2,1,0:T(8,128)(2,1)S(1)} %get-tuple-element.45), channel_id=1, source_target_pairs={{0,16},{16,32},{32,48},{48,64},{64,80},{80,96},{96,112},{112,0},{1... | collective-permute-start | bytes 688136 | tf_op jit(solution)/shard_map/ppermute | solution.py:421
  15.1 12.1 %collective-permute-start.1 = (bf16[4,112,256]{2,1,0:T(8,128)(2,1)S(1)}, bf16[4,112,256]{2,1,0:T(8,128)(2,1)S(1)}, u32[]{:S(2)}, u32[]{:S(2)}) collective-permute-start(bf16[4,112,256]{2,1,0:T(8,128)(2,1)S(1)} %get-tuple-element.46), channel_id=1, source_target_pairs={{0,112},{16,0},{32,16},{48,32},{64,48},{80,64},{96,80},{112,96},{1... | collective-permute-start | bytes 688136 | tf_op jit(solution)/shard_map/ppermute | solution.py:421
  19.1 49.3 %collective-permute-start.2 = (bf16[4,112,256]{2,1,0:T(8,128)(2,1)S(1)}, bf16[4,112,256]{2,1,0:T(8,128)(2,1)S(1)}, u32[]{:S(2)}, u32[]{:S(2)}) collective-permute-start(bf16[4,112,256]{2,1,0:T(8,128)(2,1)S(1)} %get-tuple-element.47), channel_id=1, source_target_pairs={{0,48},{16,64},{32,80},{48,96},{64,112},{80,0},{96,16},{112,32},{1... | collective-permute-start | bytes 688136 | tf_op jit(solution)/shard_map/ppermute | solution.py:421
  20.6 47.8 %collective-permute-start.3 = (bf16[4,112,256]{2,1,0:T(8,128)(2,1)S(1)}, bf16[4,112,256]{2,1,0:T(8,128)(2,1)S(1)}, u32[]{:S(2)}, u32[]{:S(2)}) collective-permute-start(bf16[4,112,256]{2,1,0:T(8,128)(2,1)S(1)} %get-tuple-element.48), channel_id=1, source_target_pairs={{0,80},{16,96},{32,112},{48,0},{64,16},{80,32},{96,48},{112,64},{1... | collective-permute-start | bytes 688136 | tf_op jit(solution)/shard_map/ppermute | solution.py:421
  23.6 44.8 %collective-permute-start.4 = (bf16[4,112,256]{2,1,0:T(8,128)(2,1)S(1)}, bf16[4,112,256]{2,1,0:T(8,128)(2,1)S(1)}, u32[]{:S(2)}, u32[]{:S(2)}) collective-permute-start(bf16[4,112,256]{2,1,0:T(8,128)(2,1)S(1)} %get-tuple-element.49), channel_id=1, source_target_pairs={{0,32},{16,48},{32,64},{48,80},{64,96},{80,112},{96,0},{112,16},{1... | collective-permute-start | bytes 688136 | tf_op jit(solution)/shard_map/ppermute | solution.py:421
  23.9 44.6 %collective-permute-start.5 = (bf16[4,112,256]{2,1,0:T(8,128)(2,1)S(1)}, bf16[4,112,256]{2,1,0:T(8,128)(2,1)S(1)}, u32[]{:S(2)}, u32[]{:S(2)}) collective-permute-start(bf16[4,112,256]{2,1,0:T(8,128)(2,1)S(1)} %get-tuple-element.50), channel_id=1, source_target_pairs={{0,96},{16,112},{32,0},{48,16},{64,32},{80,48},{96,64},{112,80},{1... | collective-permute-start | bytes 688136 | tf_op jit(solution)/shard_map/ppermute | solution.py:421
  27.2 41.2 %collective-permute-start.6 = (bf16[4,112,256]{2,1,0:T(8,128)(2,1)S(1)}, bf16[4,112,256]{2,1,0:T(8,128)(2,1)S(1)}, u32[]{:S(2)}, u32[]{:S(2)}) collective-permute-start(bf16[4,112,256]{2,1,0:T(8,128)(2,1)S(1)} %get-tuple-element.51), channel_id=1, source_target_pairs={{0,64},{16,80},{32,96},{48,112},{64,0},{80,16},{96,32},{112,48},{1... | collective-permute-start | bytes 688136 | tf_op jit(solution)/shard_map/ppermute | solution.py:421
  73.5 54.9 %copy-start = (s32[8,28]{1,0:T(8,128)S(1)}, s32[8,28]{1,0:T(8,128)}, u32[]{:S(2)}) copy-start(s32[8,28]{1,0:T(8,128)} %order_ref.5) | copy-start | bytes 2692
  73.5 106.4 %all-to-all-start.2 = ((bf16[16,32,4224]{2,1,0:T(8,128)(2,1)}), bf16[16,32,4224]{2,1,0:T(8,128)(2,1)}, u32[]{:S(2)}, u32[]{:S(2)}) async-start(bf16[16,32,4224]{2,1,0:T(8,128)(2,1)} %first_mix.1), calls=%async_computation.2 | async-start | bytes 8650752 | tf_op jit(solution)/shard_map/all_to_all | solution.py:410
  81.1 8.0 %collective-permute-start.7 = (bf16[8,112,256]{2,1,0:T(8,128)(2,1)S(1)}, bf16[8,112,256]{2,1,0:T(8,128)(2,1)S(1)}, u32[]{:S(2)}, u32[]{:S(2)}) collective-permute-start(bf16[8,112,256]{2,1,0:T(8,128)(2,1)S(1)} %get-tuple-element.62), channel_id=1, source_target_pairs={{0,8},{8,0},{128,136},{136,128},{1,9},{9,1},{129,137},{137,129},{2... | collective-permute-start | bytes 1376264 | tf_op jit(solution)/shard_map/ppermute | solution.py:428
  85.7 24.6 %collective-permute-start.8 = (bf16[8,112,256]{2,1,0:T(8,128)(2,1)S(1)}, bf16[8,112,256]{2,1,0:T(8,128)(2,1)S(1)}, u32[]{:S(2)}, u32[]{:S(2)}) collective-permute-start(bf16[8,112,256]{2,1,0:T(8,128)(2,1)S(1)} %get-tuple-element.63), channel_id=1, source_target_pairs={{0,128},{8,136},{128,0},{136,8},{1,129},{9,137},{129,1},{137,9},{2... | collective-permute-start | bytes 1376264 | tf_op jit(solution)/shard_map/ppermute | solution.py:428
  88.9 39.5 %collective-permute-start.9 = (bf16[8,112,256]{2,1,0:T(8,128)(2,1)S(1)}, bf16[8,112,256]{2,1,0:T(8,128)(2,1)S(1)}, u32[]{:S(2)}, u32[]{:S(2)}) collective-permute-start(bf16[8,112,256]{2,1,0:T(8,128)(2,1)S(1)} %get-tuple-element.64), channel_id=1, source_target_pairs={{0,136},{8,128},{128,8},{136,0},{1,137},{9,129},{129,9},{137,1},{2... | collective-permute-start | bytes 1376264 | tf_op jit(solution)/shard_map/ppermute | solution.py:428
  181.8 3.9 %collective-permute-start.11 = (bf16[4,32,4224]{2,1,0:T(8,128)(2,1)S(1)}, bf16[4,32,4224]{2,1,0:T(8,128)(2,1)S(1)}, u32[]{:S(2)}, u32[]{:S(2)}) collective-permute-start(bf16[4,32,4224]{2,1,0:T(8,128)(2,1)S(1)} %get-tuple-element.71), channel_id=1, source_target_pairs={{0,8},{8,0},{1,9},{9,1},{2,10},{10,2},{3,11},{11,3},{4,12},{12,4},... | collective-permute-start | bytes 3244040 | tf_op jit(solution)/shard_map/ppermute | solution.py:433
  185.3 2.8 %collective-permute-start.10 = (bf16[4,32,4224]{2,1,0:T(8,128)(2,1)S(1)}, bf16[4,32,4224]{2,1,0:T(8,128)(2,1)S(1)}, u32[]{:S(2)}, u32[]{:S(2)}) collective-permute-start(bf16[4,32,4224]{2,1,0:T(8,128)(2,1)S(1)} %get-tuple-element.69), channel_id=1, source_target_pairs={{0,8},{8,0},{1,9},{9,1},{2,10},{10,2},{3,11},{11,3},{4,12},{12,4},... | collective-permute-start | bytes 3244040 | tf_op jit(solution)/shard_map/ppermute | solution.py:433

commit v7 on v6

--- a/solution.py
+++ b/solution.py
@@ -18,7 +18,7 @@
 ROWS = 32
 PIECES = 16
 DEEP = 8
-SHIFTS = (0, 1, 7, 3, 5, 2, 6, 4)
+SHIFTS = (0, 1, 7, 2, 6, 3, 5, 4)
 FFN_WIDTH = HALF_F * BLK
 HEADS_WIDTH = (HALF_Q + 1) * BLK
 VMEM_LIMIT = 16 * 1024 * 1024
@@ -192,11 +192,14 @@
 ):
     in_copies, out_copies = [], []
     for at, (array, start, width, begin) in enumerate(groups):
-        source = (gates_ref, rest_ref)[array].at[:, :, pl.ds(start, width)]
         there = pl.ds(begin, width)
-        in_copies.append(
-            pltpu.make_async_copy(source, in_held.at[:, :, there], in_sems.at[at])
-        )
+        if array:
+            source = rest_ref.at[:, :, pl.ds(start, width)]
+            in_copies.append(
+                pltpu.make_async_copy(source, in_held.at[:, :, pl.ds(start, width)], in_sems.at[at])
+            )
+        else:
+            in_copies.append(None)
         out_copies.append(
             pltpu.make_async_copy(
                 out_held.at[:, :, there], out_ref.at[:, :, there], out_sems.at[at]
@@ -205,17 +208,21 @@
     whole_matrix = pltpu.make_async_copy(matrix_ref, held, sem)
     whole_matrix.start()
     for copy in in_copies:
-        copy.start()
+        if copy is not None:
+            copy.start()
     whole_matrix.wait()
     matrix = held[...]
-    for at, (_, _, width, begin) in enumerate(groups):
-        in_copies[at].wait()
+    for at, (array, first, width, begin) in enumerate(groups):
+        if array:
+            in_copies[at].wait()
+        tall_ref = in_held if array else gates_ref
         for start in range(begin, begin + width, 2 * BLK):
             stop = min(start + 2 * BLK, begin + width)
+            columns = slice(start - begin + first, stop - begin + first)
             sides = [
                 jnp.dot(
                     matrix,
-                    in_held[side * 8 : side * 8 + 8, :, start:stop].reshape(8 * ROWS, -1),
+                    tall_ref[side * 8 : side * 8 + 8, :, columns].reshape(8 * ROWS, -1),
                     preferred_element_type=jnp.float32,
                 )
                 for side in range(2)
@@ -243,17 +250,21 @@
     return pl.pallas_call(
         functools.partial(first_kernel, groups),
         out_shape=jax.ShapeDtypeStruct((PIECES, ROWS, width), jnp.bfloat16),
-        in_specs=[pl.BlockSpec(memory_space=pl.ANY)] * 3,
+        in_specs=[
+            pl.BlockSpec(memory_space=pl.ANY),
+            *whole(1),
+            pl.BlockSpec(memory_space=pl.ANY),
+        ],
         out_specs=pl.BlockSpec(memory_space=pl.ANY),
         scratch_shapes=[
             pltpu.VMEM((rows, rows), jnp.bfloat16),
-            held,
+            pltpu.VMEM(rest.shape, jnp.bfloat16),
             held,
             pltpu.SemaphoreType.DMA,
             sems,
             sems,
         ],
-        compiler_params=params(VMEM_MOST),
+        compiler_params=params(),
         cost_estimate=cost(4 * rows * rows * width, 8 * rows * width),
         name="first_mix",
     )(jnp.asarray(signs(rows) / 16.0, jnp.bfloat16), gates, rest)

time: 193 us -> 193 us (level)
  local copies, waits for them, and re-layouts: 0.01 us -> 4.47 us
  waiting for transfers between devices: 89.6 us -> 87.2 us
    unnamed x6 -> x10, local copies, waits for them, and re-layouts: 0.01 us -> 4.47 us
    ppermute x3, waiting for transfers between devices: 39.2 us -> 37 us  [exchange_side(): lax.ppermute(pieces[r], ('xh', 'core'), [(i, i ^ r) for i in range(4)])]
    pallas_call x1, Pallas kernels: 5.02 us -> 2.94 us  [first_mix(): pl.pallas_call(functools.partial(first_kernel, groups), out_shape=jax.Sha...]
    all_to_all x2, starting transfers between devices: 14.2 us -> 12.3 us  [exchange(): return lax.all_to_all(pieces, axes, split_axis=0, concat_axis=0, tiled=True)]
  transfers between devices with their start and end apart: 14 -> 14, of which waited for: 6 -> 6; matrix products, arithmetic and copies ran while one was open for 0% -> 0% of each run, Pallas kernels for 7% -> 8%
where the time goes in v7:
time: 193 us; the launch traced here: 190 us
  waiting for transfers between devices  87.2 us (45%)
  starting transfers between devices  40.8 us (21%)
  blocking collectives  32.4 us (17%)
  Pallas kernels  24 us (12%)
  local copies, waits for them, and re-layouts  4.47 us (2%)
    all_to_all x2, waiting for transfers between devices, exchange(): return lax.all_to_all(pieces, axes, split_axis=0, concat_axis=0, tiled=True)  48.4 us
    ppermute x3, waiting for transfers between devices, exchange_side(): lax.ppermute(pieces[r], ('xh', 'core'), [(i, i ^ r) for i in range(4)])  37 us
    all_to_all x1, blocking collectives, exchange(): return lax.all_to_all(pieces, axes, split_axis=0, concat_axis=0, tiled=True)  32.4 us
    ppermute x7, starting transfers between devices, exchange_z(): lax.ppermute(pieces[at], 'z', [(i, (i + s) % DEEP) for i in range(DEEP)])  16.9 us
    all_to_all x2, starting transfers between devices, exchange(): return lax.all_to_all(pieces, axes, split_axis=0, concat_axis=0, tiled=True)  12.3 us
    ppermute x3, starting transfers between devices, exchange_side(): lax.ppermute(pieces[r], ('xh', 'core'), [(i, i ^ r) for i in range(4)])  8.88 us
    pallas_call x2, Pallas kernels, pick(): pl.pallas_call(functools.partial(pick_kernel, bool(heads)), grid=(PIECES...  6.76 us
    unnamed x10, local copies, waits for them, and re-layouts  4.47 us
  transfers between devices with their start and end apart: 14, of which 6 were waited for; matrix products, arithmetic and copies ran while one was open for 0% of the time, Pallas kernels for 8%

profile of v7, /device:TPU:25, one launch (start us, length us, event | category | flops | bytes accessed | tf_op | source)
XLA Modules:
  0.0 189.8 jit_solution(2727760738411079281)
XLA Ops:
  0.6 3.1 %pick_columns.3 = bf16[16,32,1792]{2,1,0:T(8,128)(2,1)} custom-call(s32[8,28]{1,0:T(8,128)} %order_ref.5, f32[32]{0:T(128)} %ffn_gain_ref.3, bf16[32,28672]{1,0:T(8,128)(2,1)} %ffn_ref.3), custom_call_target="tpu_custom_call" | custom-call | flops 367001600 | bytes 3670016 | tf_op jit(solution)/shard_map/pick_columns/pallas_call | solution.py:178
  3.8 0.0 copy-start.4
  3.8 6.7 %all-to-all-start.1 = ((bf16[16,32,1792]{2,1,0:T(8,128)(2,1)}), bf16[16,32,1792]{2,1,0:T(8,128)(2,1)S(1)}, u32[]{:S(2)}, u32[]{:S(2)}) async-start(bf16[16,32,1792]{2,1,0:T(8,128)(2,1)} %pick_columns.3), calls=%async_computation.1 | async-start | bytes 3670016 | tf_op jit(solution)/shard_map/all_to_all | solution.py:421
  10.5 0.0 copy-done.4
  10.5 0.0 copy-start.3
  10.5 1.5 copy-done.3
  12.0 3.8 %down_rotate.1 = (bf16[4,112,256]{2,1,0:T(8,128)(2,1)S(1)}, bf16[4,112,256]{2,1,0:T(8,128)(2,1)S(1)}, bf16[4,112,256]{2,1,0:T(8,128)(2,1)S(1)}, bf16[4,112,256]{...) custom-call(bf16[112,8192]{1,0:T(8,128)(2,1)S(1)} %copy-done.3, ...), custom_call_target="tpu_custom_call" | custom-call | flops 939524096 | bytes 3670016 | tf_op jit(solution)/shard_map/down_rotate/pallas_call | solution.py:103
  15.9 1.6 collective-permute-start
  17.5 4.0 %collective-permute-start.1 = (bf16[4,112,256]{2,1,0:T(8,128)(2,1)S(1)}, bf16[4,112,256]{2,1,0:T(8,128)(2,1)S(1)}, u32[]{:S(2)}, u32[]{:S(2)}) collective-permute-start(bf16[4,112,256]{2,1,0:T(8,128)(2,1)S(1)} %get-tuple-element.46), channel_id=1, source_target_pairs={{0,112},{16,0},{32,16},{48,32},{64,48},{80,64},{96,80},{112,96},{1... | collective-permute-start | bytes 688136 | tf_op jit(solution)/shard_map/ppermute | solution.py:432
  21.4 0.0 collective-permute-start.2
  21.4 3.6 %collective-permute-start.3 = (bf16[4,112,256]{2,1,0:T(8,128)(2,1)}, bf16[4,112,256]{2,1,0:T(8,128)(2,1)S(1)}, u32[]{:S(2)}, u32[]{:S(2)}) collective-permute-start(bf16[4,112,256]{2,1,0:T(8,128)(2,1)} %get-tuple-element.48), channel_id=1, source_target_pairs={{0,96},{16,112},{32,0},{48,16},{64,32},{80,48},{96,64},{112,80},{1... | collective-permute-start | bytes 688136 | tf_op jit(solution)/shard_map/ppermute | solution.py:432
  25.0 0.4 collective-permute-start.4
  25.4 0.7 collective-permute-done.refs_1_
  26.1 3.4 %collective-permute-start.5 = (bf16[4,112,256]{2,1,0:T(8,128)(2,1)}, bf16[4,112,256]{2,1,0:T(8,128)(2,1)S(1)}, u32[]{:S(2)}, u32[]{:S(2)}) collective-permute-start(bf16[4,112,256]{2,1,0:T(8,128)(2,1)} %get-tuple-element.50), channel_id=1, source_target_pairs={{0,80},{16,96},{32,112},{48,0},{64,16},{80,32},{96,48},{112,64},{1... | collective-permute-start | bytes 688136 | tf_op jit(solution)/shard_map/ppermute | solution.py:432
  29.5 0.0 collective-permute-done.1.refs_2_
  29.5 4.0 %collective-permute-start.6 = (bf16[4,112,256]{2,1,0:T(8,128)(2,1)}, bf16[4,112,256]{2,1,0:T(8,128)(2,1)}, u32[]{:S(2)}, u32[]{:S(2)}) collective-permute-start(bf16[4,112,256]{2,1,0:T(8,128)(2,1)} %get-tuple-element.51), channel_id=1, source_target_pairs={{0,64},{16,80},{32,96},{48,112},{64,0},{80,16},{96,32},{112,48},{1... | collective-permute-start | bytes 688136 | tf_op jit(solution)/shard_map/ppermute | solution.py:432
  33.5 3.6 %pick_columns.2 = bf16[16,32,2432]{2,1,0:T(8,128)(2,1)} custom-call(s32[8,28]{1,0:T(8,128)} %order_ref.5, f32[32]{0:T(128)} %ffn_gain_ref.3, bf16[32,28672]{1,0:T(8,128)(2,1)} %ffn_ref.2, s32[8,8]{1,0:T(8,128)} %refs_0_.1, f32[32]{0:T(128)} %refs_1_.1, bf16[32,8192]{1,0:T(8,128)(2,1)} %refs_2_.1, bf16[32,1024]{1,0:T(8,128)(2,1)} %refs_3_.1, ...), custom_call_target="tpu_custom_call" | custom-call | flops 498073600 | bytes 4980736 | tf_op jit(solution)/shard_map/pick_columns/pallas_call | solution.py:178
  37.1 0.0 all-to-all-done.1.gates_ref
  37.1 32.4 %conditional.1 = (bf16[16,32,2432]{2,1,0:T(8,128)(2,1)}) conditional(s32[]{:T(128)} %convert_element_type.3, () %tuple.19, bf16[16,32,2432]{2,1,0:T(8,128)(2,1)} %pick_columns.2), branch_computations={%region_0.0_spmd, %region_1.0_spmd} | conditional | bytes 4980744 | solution.py:425
  37.1 32.4 %all_to_all.14 = bf16[16,32,2432]{2,1,0:T(8,128)(2,1)} all-to-all(bf16[16,32,2432]{2,1,0:T(8,128)(2,1)} %param.1), channel_id=1, replica_groups=mesh['xh'=2,'z'=8,'core'=2,'xl'=2,'y'=4] {'xh','xl','y'}, dimensions={0} | all-to-all | bytes 4980736 | tf_op jit(solution)/shard_map/cond/branch_1_fun/all_to_all | solution.py:421
  69.5 0.0 collective-permute-done.2.refs_3_
  69.5 0.0 collective-permute-done.3.refs_4_
  69.5 0.0 collective-permute-done.4.refs_5_
  69.5 0.0 collective-permute-done.5.refs_6_
  69.5 0.0 collective-permute-done.6.refs_7_
  69.5 0.0 copy-start.1
  69.5 0.9 copy-done.1
  70.4 2.9 %first_mix.1 = bf16[16,32,4224]{2,1,0:T(8,128)(2,1)S(1)} custom-call(bf16[256,256]{1,0:T(8,128)(2,1)S(1)} %copy-done.1, bf16[16,32,1792]{2,1,0:T(8,128)(2,1)S(1)} %all-to-all-done.1.gates_ref, bf16[16,32,2432]{2,1,0:T(8,128)(2,1)} %get-tuple-element.77.rest_ref), custom_call_target="tpu_custom_call" | custom-call | flops 1107296256 | bytes 8650752 | tf_op jit(solution)/shard_map/first_mix/pallas_call | solution.py:250
  73.4 0.0 copy-start
  73.4 2.1 %copy-done = bf16[16,32,4224]{2,1,0:T(8,128)(2,1)} copy-done((bf16[16,32,4224]{2,1,0:T(8,128)(2,1)}, bf16[16,32,4224]{2,1,0:T(8,128)(2,1)S(1)}, u32[]{:S(2)}) %copy-start) | copy-done | bytes 4325400
  75.4 0.0 copy-start.2
  75.5 5.5 %all-to-all-start.2 = ((bf16[16,32,4224]{2,1,0:T(8,128)(2,1)}), bf16[16,32,4224]{2,1,0:T(8,128)(2,1)}, u32[]{:S(2)}, u32[]{:S(2)}) async-start(bf16[16,32,4224]{2,1,0:T(8,128)(2,1)} %copy-done), calls=%async_computation.2 | async-start | bytes 8650752 | tf_op jit(solution)/shard_map/all_to_all | solution.py:421
  81.0 1.1 repack_down.1
  82.0 5.5 %collective-permute-start.7 = (bf16[8,112,256]{2,1,0:T(8,128)(2,1)S(1)}, bf16[8,112,256]{2,1,0:T(8,128)(2,1)S(1)}, u32[]{:S(2)}, u32[]{:S(2)}) collective-permute-start(bf16[8,112,256]{2,1,0:T(8,128)(2,1)S(1)} %get-tuple-element.62), channel_id=1, source_target_pairs={{0,8},{8,0},{128,136},{136,128},{1,9},{9,1},{129,137},{137,129},{2... | collective-permute-start | bytes 1376264 | tf_op jit(solution)/shard_map/ppermute | solution.py:439
  87.6 3.1 %collective-permute-start.8 = (bf16[8,112,256]{2,1,0:T(8,128)(2,1)S(1)}, bf16[8,112,256]{2,1,0:T(8,128)(2,1)S(1)}, u32[]{:S(2)}, u32[]{:S(2)}) collective-permute-start(bf16[8,112,256]{2,1,0:T(8,128)(2,1)S(1)} %get-tuple-element.63), channel_id=1, source_target_pairs={{0,128},{8,136},{128,0},{136,8},{1,129},{9,137},{129,1},{137,9},{2... | collective-permute-start | bytes 1376264 | tf_op jit(solution)/shard_map/ppermute | solution.py:439
  90.7 0.2 collective-permute-start.9
  90.9 0.0 collective-permute-done.7.refs_1_
  90.9 19.7 %collective-permute-done.8.refs_2_ = bf16[8,112,256]{2,1,0:T(8,128)(2,1)S(1)} collective-permute-done((bf16[8,112,256]{2,1,0:T(8,128)(2,1)S(1)}, bf16[8,112,256]{2,1,0:T(8,128)(2,1)S(1)}, u32[]{:S(2)}, u32[]{:S(2)}) %collective-permute-start.8) | collective-permute-done | bytes 458784 | tf_op jit(solution)/shard_map/ppermute | solution.py:439
  110.6 17.3 %collective-permute-done.9.refs_3_ = bf16[8,112,256]{2,1,0:T(8,128)(2,1)S(1)} collective-permute-done((bf16[8,112,256]{2,1,0:T(8,128)(2,1)S(1)}, bf16[8,112,256]{2,1,0:T(8,128)(2,1)S(1)}, u32[]{:S(2)}, u32[]{:S(2)}) %collective-permute-start.9) | collective-permute-done | bytes 458784 | tf_op jit(solution)/shard_map/ppermute | solution.py:439
  127.9 0.0 copy-done.2
  127.9 2.6 %order_rows.1 = bf16[3584,256]{1,0:T(8,128)(2,1)} custom-call(s32[8,28]{1,0:T(8,128)S(1)} %copy-done.2, bf16[8,112,256]{2,1,0:T(8,128)(2,1)S(1)} %get-tuple-element.61.refs_0_, bf16[8,112,256]{2,1,0:T(8,128)(2,1)S(1)} %collective-permute-done.7.refs_1_, bf16[8,112,256]{2,1,0:T(8,128)(2,1)S(1)} %collective-permute-done.8.refs_2_, ...), custom_call_target="tpu_custom_call" | custom-call | flops 917504 | bytes 3670016 | tf_op jit(solution)/shard_map/order_rows/pallas_call | solution.py:408
  130.5 48.4 %all-to-all-done.2.own_ref = bf16[16,32,4224]{2,1,0:T(8,128)(2,1)} async-done(((bf16[16,32,4224]{2,1,0:T(8,128)(2,1)}), bf16[16,32,4224]{2,1,0:T(8,128)(2,1)}, u32[]{:S(2)}, u32[]{:S(2)}) %all-to-all-start.2) | async-done | bytes 4325408 | tf_op jit(solution)/shard_map/all_to_all | solution.py:421
  178.9 1.9 own_sums.2
  180.8 2.6 %collective-permute-start.11 = (bf16[4,32,4224]{2,1,0:T(8,128)(2,1)S(1)}, bf16[4,32,4224]{2,1,0:T(8,128)(2,1)S(1)}, u32[]{:S(2)}, u32[]{:S(2)}) collective-permute-start(bf16[4,32,4224]{2,1,0:T(8,128)(2,1)S(1)} %get-tuple-element.71), channel_id=1, source_target_pairs={{0,8},{8,0},{1,9},{9,1},{2,10},{10,2},{3,11},{11,3},{4,12},{12,4},... | collective-permute-start | bytes 3244040 | tf_op jit(solution)/shard_map/ppermute | solution.py:444
  183.4 1.9 own_sums.3
  185.3 0.1 collective-permute-start.10
  185.4 0.4 collective-permute-done.11.other_ref
  185.7 1.5 last_mix.2
  187.3 0.8 collective-permute-done.10.other_ref
  188.1 1.5 last_mix.3
Async XLA Ops:
  3.8 6.7 %copy-start.4 = (bf16[128,128]{1,0:T(8,128)(2,1)S(1)}, bf16[128,128]{1,0:T(8,128)(2,1)}, u32[]{:S(2)}) copy-start(bf16[128,128]{1,0:T(8,128)(2,1)} %constant.14.clone.sign_ref) | copy-start | bytes 98308
  3.8 33.4 %all-to-all-start.1 = ((bf16[16,32,1792]{2,1,0:T(8,128)(2,1)}), bf16[16,32,1792]{2,1,0:T(8,128)(2,1)S(1)}, u32[]{:S(2)}, u32[]{:S(2)}) async-start(bf16[16,32,1792]{2,1,0:T(8,128)(2,1)} %pick_columns.3), calls=%async_computation.1 | async-start | bytes 3670016 | tf_op jit(solution)/shard_map/all_to_all | solution.py:421
  10.5 1.5 copy-start.3
  15.9 10.3 %collective-permute-start = (bf16[4,112,256]{2,1,0:T(8,128)(2,1)S(1)}, bf16[4,112,256]{2,1,0:T(8,128)(2,1)S(1)}, u32[]{:S(2)}, u32[]{:S(2)}) collective-permute-start(bf16[4,112,256]{2,1,0:T(8,128)(2,1)S(1)} %get-tuple-element.45), channel_id=1, source_target_pairs={{0,16},{16,32},{32,48},{48,64},{64,80},{80,96},{96,112},{112,0},{1... | collective-permute-start | bytes 688136 | tf_op jit(solution)/shard_map/ppermute | solution.py:432
  17.5 12.0 %collective-permute-start.1 = (bf16[4,112,256]{2,1,0:T(8,128)(2,1)S(1)}, bf16[4,112,256]{2,1,0:T(8,128)(2,1)S(1)}, u32[]{:S(2)}, u32[]{:S(2)}) collective-permute-start(bf16[4,112,256]{2,1,0:T(8,128)(2,1)S(1)} %get-tuple-element.46), channel_id=1, source_target_pairs={{0,112},{16,0},{32,16},{48,32},{64,48},{80,64},{96,80},{112,96},{1... | collective-permute-start | bytes 688136 | tf_op jit(solution)/shard_map/ppermute | solution.py:432
  21.4 48.1 %collective-permute-start.2 = (bf16[4,112,256]{2,1,0:T(8,128)(2,1)}, bf16[4,112,256]{2,1,0:T(8,128)(2,1)S(1)}, u32[]{:S(2)}, u32[]{:S(2)}) collective-permute-start(bf16[4,112,256]{2,1,0:T(8,128)(2,1)} %get-tuple-element.47), channel_id=1, source_target_pairs={{0,32},{16,48},{32,64},{48,80},{64,96},{80,112},{96,0},{112,16},{1... | collective-permute-start | bytes 688136 | tf_op jit(solution)/shard_map/ppermute | solution.py:432
  21.4 48.1 %collective-permute-start.3 = (bf16[4,112,256]{2,1,0:T(8,128)(2,1)}, bf16[4,112,256]{2,1,0:T(8,128)(2,1)S(1)}, u32[]{:S(2)}, u32[]{:S(2)}) collective-permute-start(bf16[4,112,256]{2,1,0:T(8,128)(2,1)} %get-tuple-element.48), channel_id=1, source_target_pairs={{0,96},{16,112},{32,0},{48,16},{64,32},{80,48},{96,64},{112,80},{1... | collective-permute-start | bytes 688136 | tf_op jit(solution)/shard_map/ppermute | solution.py:432
  25.0 44.5 %collective-permute-start.4 = (bf16[4,112,256]{2,1,0:T(8,128)(2,1)}, bf16[4,112,256]{2,1,0:T(8,128)(2,1)S(1)}, u32[]{:S(2)}, u32[]{:S(2)}) collective-permute-start(bf16[4,112,256]{2,1,0:T(8,128)(2,1)} %get-tuple-element.49), channel_id=1, source_target_pairs={{0,48},{16,64},{32,80},{48,96},{64,112},{80,0},{96,16},{112,32},{1... | collective-permute-start | bytes 688136 | tf_op jit(solution)/shard_map/ppermute | solution.py:432
  26.1 43.4 %collective-permute-start.5 = (bf16[4,112,256]{2,1,0:T(8,128)(2,1)}, bf16[4,112,256]{2,1,0:T(8,128)(2,1)S(1)}, u32[]{:S(2)}, u32[]{:S(2)}) collective-permute-start(bf16[4,112,256]{2,1,0:T(8,128)(2,1)} %get-tuple-element.50), channel_id=1, source_target_pairs={{0,80},{16,96},{32,112},{48,0},{64,16},{80,32},{96,48},{112,64},{1... | collective-permute-start | bytes 688136 | tf_op jit(solution)/shard_map/ppermute | solution.py:432
  29.5 40.0 %collective-permute-start.6 = (bf16[4,112,256]{2,1,0:T(8,128)(2,1)}, bf16[4,112,256]{2,1,0:T(8,128)(2,1)}, u32[]{:S(2)}, u32[]{:S(2)}) collective-permute-start(bf16[4,112,256]{2,1,0:T(8,128)(2,1)} %get-tuple-element.51), channel_id=1, source_target_pairs={{0,64},{16,80},{32,96},{48,112},{64,0},{80,16},{96,32},{112,48},{1... | collective-permute-start | bytes 688136 | tf_op jit(solution)/shard_map/ppermute | solution.py:432
  69.5 0.9 copy-start.1
  73.4 2.1 %copy-start = (bf16[16,32,4224]{2,1,0:T(8,128)(2,1)}, bf16[16,32,4224]{2,1,0:T(8,128)(2,1)S(1)}, u32[]{:S(2)}) copy-start(bf16[16,32,4224]{2,1,0:T(8,128)(2,1)S(1)} %first_mix.1) | copy-start | bytes 12976132
  75.4 52.5 %copy-start.2 = (s32[8,28]{1,0:T(8,128)S(1)}, s32[8,28]{1,0:T(8,128)}, u32[]{:S(2)}) copy-start(s32[8,28]{1,0:T(8,128)} %order_ref.5) | copy-start | bytes 2692
  75.5 103.5 %all-to-all-start.2 = ((bf16[16,32,4224]{2,1,0:T(8,128)(2,1)}), bf16[16,32,4224]{2,1,0:T(8,128)(2,1)}, u32[]{:S(2)}, u32[]{:S(2)}) async-start(bf16[16,32,4224]{2,1,0:T(8,128)(2,1)} %copy-done), calls=%async_computation.2 | async-start | bytes 8650752 | tf_op jit(solution)/shard_map/all_to_all | solution.py:421
  82.0 8.9 %collective-permute-start.7 = (bf16[8,112,256]{2,1,0:T(8,128)(2,1)S(1)}, bf16[8,112,256]{2,1,0:T(8,128)(2,1)S(1)}, u32[]{:S(2)}, u32[]{:S(2)}) collective-permute-start(bf16[8,112,256]{2,1,0:T(8,128)(2,1)S(1)} %get-tuple-element.62), channel_id=1, source_target_pairs={{0,8},{8,0},{128,136},{136,128},{1,9},{9,1},{129,137},{137,129},{2... | collective-permute-start | bytes 1376264 | tf_op jit(solution)/shard_map/ppermute | solution.py:439
  87.6 23.0 %collective-permute-start.8 = (bf16[8,112,256]{2,1,0:T(8,128)(2,1)S(1)}, bf16[8,112,256]{2,1,0:T(8,128)(2,1)S(1)}, u32[]{:S(2)}, u32[]{:S(2)}) collective-permute-start(bf16[8,112,256]{2,1,0:T(8,128)(2,1)S(1)} %get-tuple-element.63), channel_id=1, source_target_pairs={{0,128},{8,136},{128,0},{136,8},{1,129},{9,137},{129,1},{137,9},{2... | collective-permute-start | bytes 1376264 | tf_op jit(solution)/shard_map/ppermute | solution.py:439
  90.7 37.2 %collective-permute-start.9 = (bf16[8,112,256]{2,1,0:T(8,128)(2,1)S(1)}, bf16[8,112,256]{2,1,0:T(8,128)(2,1)S(1)}, u32[]{:S(2)}, u32[]{:S(2)}) collective-permute-start(bf16[8,112,256]{2,1,0:T(8,128)(2,1)S(1)} %get-tuple-element.64), channel_id=1, source_target_pairs={{0,136},{8,128},{128,8},{136,0},{1,137},{9,129},{129,9},{137,1},{2... | collective-permute-start | bytes 1376264 | tf_op jit(solution)/shard_map/ppermute | solution.py:439
  180.8 5.0 %collective-permute-start.11 = (bf16[4,32,4224]{2,1,0:T(8,128)(2,1)S(1)}, bf16[4,32,4224]{2,1,0:T(8,128)(2,1)S(1)}, u32[]{:S(2)}, u32[]{:S(2)}) collective-permute-start(bf16[4,32,4224]{2,1,0:T(8,128)(2,1)S(1)} %get-tuple-element.71), channel_id=1, source_target_pairs={{0,8},{8,0},{1,9},{9,1},{2,10},{10,2},{3,11},{11,3},{4,12},{12,4},... | collective-permute-start | bytes 3244040 | tf_op jit(solution)/shard_map/ppermute | solution.py:444
  185.3 2.8 %collective-permute-start.10 = (bf16[4,32,4224]{2,1,0:T(8,128)(2,1)S(1)}, bf16[4,32,4224]{2,1,0:T(8,128)(2,1)S(1)}, u32[]{:S(2)}, u32[]{:S(2)}) collective-permute-start(bf16[4,32,4224]{2,1,0:T(8,128)(2,1)S(1)} %get-tuple-element.69), channel_id=1, source_target_pairs={{0,8},{8,0},{1,9},{9,1},{2,10},{10,2},{3,11},{11,3},{4,12},{12,4},... | collective-permute-start | bytes 3244040 | tf_op jit(solution)/shard_map/ppermute | solution.py:444
